TPU v7x, 32 devices: a whole 2x2x4 slice. The times are simulated.
32 devices in a mesh: tm: 16 (over z, x, core), space: 2 (over y).
Axes of the slice: x: 2, y: 2, z: 4, core: 2. Of those that a mesh axis runs over, the one named last changes fastest.
Arguments:
- observations: bfloat16 [4096, 16, 2, 512], P(None, 'tm', 'space'), may hold values from -6 to 6
- pod_basis: bfloat16 [16, 2, 512, 1024], P(None, 'space'), may hold values from -0.046875 to 0.046875
- decay: float32 [4096, 1024], P('tm', 'space'), may hold values from 0 to 1
- step_mask: int32 [4096], P('tm'), may hold values 0 or 1
- process_var: float32 [1024], P('space'), may hold values from 0.00024414062 to 1
- obs_var: float32 [1024], P('space'), may hold values from 1 to 256
- prior_mean: float32 [1024], P('space'), may hold values from -6 to 6
- prior_var: float32 [1024], P('space'), may hold values from 0.5 to 4
Outputs:
- coefficients: float32 [4096, 1024], P('tm', 'space')
- filtered_mean: float32 [4096, 1024], P('tm', 'space')
- smoothed_mean: float32 [4096, 1024], P('tm', 'space')
- log_variance: float32 [4096, 1024], P('tm', 'space')
All inputs are finite; a program needn't handle non-finite values. No bound on the sum of `step_mask` on one device may be relied on, other than what follows from the above.
Results may differ from a plain program's by a relative error of at most 0.0003.
Values may be sent and summed in bfloat16 or wider, within the bound.
No kernel may reach another device: no remote copies, remote signals or barrier semaphores. Data moves between devices by JAX's collectives and lax.ppermute only.
A program may use at most 256 MiB of HBM per device.

v0:
```python
import functools

import jax
import jax.numpy as jnp
from jax import lax
from jax.experimental import pallas as pl
from jax.experimental.pallas import tpu as pltpu
from jax.sharding import PartitionSpec as P

CHUNK = 16
LANES = 128
PAD = 16
STEPS16 = 32512.0
TINY = 1e-30
F32 = jnp.float32
LIMIT = 16 * 1024 * 1024


def rotate(block, axis, turn, group):
    route = [(i, i // group * group + (i + turn) % group) for i in range(lax.axis_size(axis))]
    return lax.ppermute(block, axis, route)


def inner_size(count):
    group = 1
    while group * group < count:
        group *= 2
    return group if count % group == 0 else count


def gather_near(rows, axis):
    count = lax.axis_size(axis)
    group = inner_size(count)
    return jnp.stack([rows] + [rotate(rows, axis, s, group) for s in range(1, group)])


def gather_across(blocks, axis):
    away = blocks.shape[0]
    return jnp.concatenate(
        [blocks, lax.ppermute(blocks, axis, [(i, i ^ away) for i in range(lax.axis_size(axis))])], 0
    )


def place(me, j, count):
    group = inner_size(count)
    high = lax.bitwise_xor(me // group, j // group)
    low = lax.rem(lax.rem(me, group) - j % group + group, group)
    return high * group + low


def lanes(ref, strip_ref):
    for m in range(strip_ref.shape[0]):
        strip_ref[m] = ref[:, m * LANES : (m + 1) * LANES]


def unlanes(strip_ref, ref):
    for m in range(strip_ref.shape[0]):
        ref[:, m * LANES : (m + 1) * LANES] = strip_ref[m]


def chunk_rows(strip_ref, i, chunks):
    rows = pl.ds(i, chunks, stride=CHUNK)
    return jnp.concatenate([strip_ref[m, rows, :] for m in range(strip_ref.shape[0])], 1)


def put_rows(strip_ref, i, chunks, value):
    rows = pl.ds(i, chunks, stride=CHUNK)
    for m in range(strip_ref.shape[0]):
        strip_ref[m, rows, :] = value[:, m * LANES : (m + 1) * LANES]


def opened(me_ref, shape):
    rows = lax.broadcasted_iota(jnp.int32, shape, 0)
    return jnp.logical_and(rows == 0, me_ref[0] == 0)


def step_terms(i, chunks, first, q, r, decay_ref, seen_ref):
    d = chunk_rows(decay_ref, i, chunks)
    seen = chunk_rows(seen_ref, i, chunks) > 0.5
    base = q
    if i == 0:
        d = jnp.where(first, 1.0, d)
        base = jnp.where(first, 0.0, q)
    return d, seen, base


def element(d, seen, base, r):
    inverse = 1.0 / (base + r)
    retain = jnp.where(seen, r * inverse, 1.0)
    return retain * d, retain * base, jnp.where(seen, d * d * inverse, 0.0), inverse


def join(early, late):
    lead, spread, weight = early
    lead_late, spread_late, weight_late = late
    factor = 1.0 / (1.0 + spread * weight_late)
    return (
        lead_late * factor * lead,
        lead_late * lead_late * factor * spread + spread_late,
        lead * lead * factor * weight_late + weight,
    )


def totals_kernel(me_ref, decay_in, seen_in, q_ref, r_ref, chunk_ref, block_ref, decay_ref, seen_ref):
    steps, modes = decay_in.shape
    lanes(decay_in, decay_ref)
    lanes(seen_in, seen_ref)
    chunks = steps // CHUNK
    shape = (chunks, modes)
    q = jnp.broadcast_to(q_ref[...], shape)
    r = jnp.broadcast_to(r_ref[...], shape)
    first = opened(me_ref, shape)
    total = None
    for i in range(CHUNK):
        step = element(*step_terms(i, chunks, first, q, r, decay_ref, seen_ref), r)[:3]
        total = step if i == 0 else join(total, step)
    for k in range(3):
        chunk_ref[k] = total[k]
    total = tuple(chunk_ref[k, 0:1, :] for k in range(3))
    for c in range(1, chunks):
        total = join(total, tuple(chunk_ref[k, c : c + 1, :] for k in range(3)))
    for k in range(3):
        block_ref[k : k + 1, :] = total[k]


def gains_kernel(
    count, me_ref, decay_in, seen_in, q_ref, r_ref, prior_ref, chunk_ref, blocks_ref,
    a_ref, b_ref, alpha_ref, beta_ref, keep_ref, lift_ref, whole_ref, carry_ref, edge_ref, log_ref,
    enter_ref, var_ref, info_ref, decay_ref, seen_ref,
):
    steps, modes = decay_in.shape
    lanes(decay_in, decay_ref)
    lanes(seen_in, seen_ref)
    chunks = steps // CHUNK
    shape = (chunks, modes)
    me = me_ref[0]
    q = jnp.broadcast_to(q_ref[...], shape)
    r = jnp.broadcast_to(r_ref[...], shape)
    first = opened(me_ref, shape)

    v = prior_ref[...]
    mine = v
    for j in range(count):
        mine = jnp.where(j == me, v, mine)
        at = place(me, j, count)
        lead, spread, weight = (blocks_ref[at, k : k + 1, :] for k in range(3))
        along = lead / (1.0 + weight * v)
        edge_ref[0, j : j + 1, :] = along
        v = spread + lead * along * v
    v = mine
    for c in range(chunks):
        enter_ref[0, c : c + 1, :] = v
        lead, spread, weight = (chunk_ref[k, c : c + 1, :] for k in range(3))
        v = spread + lead * lead * v / (1.0 + weight * v)

    info = jnp.zeros((1, modes), F32)
    mine = info
    for j in reversed(range(count)):
        mine = jnp.where(j == me, info, mine)
        at = place(me, j, count)
        lead, spread, weight = (blocks_ref[at, k : k + 1, :] for k in range(3))
        along = lead / (1.0 + spread * info)
        edge_ref[1, j : j + 1, :] = along
        info = weight + lead * along * info
    info = mine
    for c in reversed(range(chunks)):
        enter_ref[1, c : c + 1, :] = info
        lead, spread, weight = (chunk_ref[k, c : c + 1, :] for k in range(3))
        info = weight + lead * lead * info / (1.0 + spread * info)

    v = enter_ref[0]
    run = None
    for i in range(CHUNK):
        d, seen, base = step_terms(i, chunks, first, q, r, decay_ref, seen_ref)
        ahead = d * d * v + base
        inverse = 1.0 / (ahead + r)
        retain = jnp.where(seen, r * inverse, 1.0)
        v = retain * ahead
        a = retain * d
        run = a if i == 0 else a * run
        a_ref[i] = a
        b_ref[i] = jnp.where(seen, ahead * inverse, 0.0)
        var_ref[i] = v
        whole_ref[0, i] = run
    carry_ref[0] = run

    info = enter_ref[1]
    run = jnp.ones(shape, F32)
    for i in reversed(range(CHUNK)):
        lead, spread, weight, inverse = element(*step_terms(i, chunks, first, q, r, decay_ref, seen_ref), r)
        d, seen, _ = step_terms(i, chunks, first, q, r, decay_ref, seen_ref)
        factor = 1.0 / (1.0 + spread * info)
        alpha = lead * factor
        info_ref[i] = info
        whole_ref[2, i] = run
        alpha_ref[i] = alpha
        beta_ref[i] = jnp.where(seen, d * inverse * factor, 0.0)
        info = weight + lead * alpha * info
        run = alpha * run
    carry_ref[1] = run

    along = jnp.ones((1, modes), F32)
    for c in range(chunks):
        enter_ref[0, c : c + 1, :] = along
        along = along * carry_ref[0, c : c + 1, :]
    along = jnp.ones((1, modes), F32)
    for c in reversed(range(chunks)):
        enter_ref[1, c : c + 1, :] = along
        along = along * carry_ref[1, c : c + 1, :]
    onward = enter_ref[0]
    back = enter_ref[1]
    for i in range(CHUNK):
        v = var_ref[i]
        keep = 1.0 / (1.0 + v * info_ref[i])
        lift = v * keep
        weight = whole_ref[0, i] * onward
        keep_ref[i] = keep
        lift_ref[i] = lift
        whole_ref[0, i] = weight
        whole_ref[1, i] = keep * weight
        whole_ref[2, i] = lift * (whole_ref[2, i] * back)
        put_rows(decay_ref, i, chunks, jnp.log(lift))
    unlanes(decay_ref, log_ref)


def means_kernel(parts, *refs):
    part_refs = refs[:parts]
    a_ref, b_ref, alpha_ref, beta_ref, keep_ref, lift_ref, carry_ref = refs[parts : parts + 7]
    coef_ref, mean_ref, smooth_ref, block_ref, enter_ref, strip_ref = refs[parts + 7 :]
    steps, modes = coef_ref.shape
    chunks = steps // CHUNK
    c = part_refs[0][...]
    for ref in part_refs[1:]:
        c = c + decode(ref)
    coef_ref[...] = c
    lanes(coef_ref, strip_ref)
    f = e = jnp.zeros((chunks, modes), F32)
    for i in range(CHUNK):
        f = a_ref[i] * f + b_ref[i] * chunk_rows(strip_ref, i, chunks)
        k = CHUNK - 1 - i
        e = alpha_ref[k] * e + beta_ref[k] * chunk_rows(strip_ref, k, chunks)
    mean_ref[0] = f
    mean_ref[1] = e
    f = e = jnp.zeros((1, modes), F32)
    for c in range(chunks):
        k = chunks - 1 - c
        enter_ref[0, c : c + 1, :] = f
        enter_ref[1, k : k + 1, :] = e
        f = mean_ref[0, c : c + 1, :] + carry_ref[0, c : c + 1, :] * f
        e = mean_ref[1, k : k + 1, :] + carry_ref[1, k : k + 1, :] * e
    block_ref[0:1, :] = f
    block_ref[1:2, :] = e
    f = enter_ref[0]
    e = enter_ref[1]
    for i in range(CHUNK):
        f = a_ref[i] * f + b_ref[i] * chunk_rows(strip_ref, i, chunks)
        mean_ref[i] = f
    for i in reversed(range(CHUNK)):
        smooth_ref[i] = keep_ref[i] * mean_ref[i] + lift_ref[i] * e
        e = alpha_ref[i] * e + beta_ref[i] * chunk_rows(strip_ref, i, chunks)


def finish_kernel(count, me_ref, prior_ref, whole_ref, edge_ref, blocks_ref, mean_ref, smooth_ref, out_mean_ref, out_smooth_ref, mean_strip_ref, smooth_strip_ref):
    steps, modes = out_mean_ref.shape
    chunks = steps // CHUNK
    me = me_ref[0]
    f = prior_ref[...]
    e = jnp.zeros((1, modes), F32)
    for j in range(count - 1):
        f = jnp.where(j < me, blocks_ref[j, 0:1, :] + edge_ref[0, j : j + 1, :] * f, f)
        k = count - 1 - j
        e = jnp.where(k > me, blocks_ref[k, 1:2, :] + edge_ref[1, k : k + 1, :] * e, e)
    f = jnp.broadcast_to(f, (chunks, modes))
    e = jnp.broadcast_to(e, (chunks, modes))
    for i in range(CHUNK):
        put_rows(mean_strip_ref, i, chunks, mean_ref[i] + whole_ref[0, i] * f)
        put_rows(smooth_strip_ref, i, chunks, smooth_ref[i] + whole_ref[1, i] * f + whole_ref[2, i] * e)
    unlanes(mean_strip_ref, out_mean_ref)
    unlanes(smooth_strip_ref, out_smooth_ref)


def encode(values, ref):
    steps = values.shape[0]
    top = jnp.max(jnp.abs(values), axis=0, keepdims=True)
    power = jnp.floor(jnp.log2(jnp.maximum(top, TINY))) + 1.0
    coded = jnp.floor(values * (jnp.exp2(-power) * STEPS16) + 0.5)
    ref[0:steps, :] = coded.astype(jnp.int32).astype(jnp.int16)
    power = jnp.broadcast_to(power, (PAD, power.shape[1]))
    ref[steps : steps + PAD, :] = power.astype(jnp.int32).astype(jnp.int16)


def decode(ref):
    steps = ref.shape[0] - PAD
    power = ref[steps : steps + PAD, :].astype(jnp.int32).astype(F32)[0:1, :]
    return ref[0:steps, :].astype(jnp.int32).astype(F32) * (jnp.exp2(power) * (1.0 / STEPS16))


def project_kernel(held, at_ref, slab_ref, basis_ref, own_ref, *refs):
    owners = at_ref.shape[0] - 1
    coded_refs = refs[: owners - 1]
    basis_area, sum_area, basis_sems, *refs = refs[owners - 1 :]
    slab_area = slab_ref if held else refs[0]
    count = slab_ref.shape[0]
    modes = own_ref.shape[1]
    copies = []
    for g in range(count):
        pair = [pltpu.make_async_copy(basis_ref.at[at_ref[0] + g], basis_area.at[g], basis_sems.at[g])]
        if not held:
            pair.append(pltpu.make_async_copy(slab_ref.at[g], slab_area.at[g], refs[1].at[g]))
        copies.append(pair)
    for pair in copies:
        for copy in pair:
            copy.start()
    for g in range(count):
        for copy in copies[g]:
            copy.wait()
        for turn in range(owners):
            columns = pl.ds(pl.multiple_of(at_ref[1 + turn] * modes, LANES), modes)
            term = jnp.dot(slab_area[g], basis_area[g, :, columns], preferred_element_type=F32)
            sum_area[turn] = term if g == 0 else sum_area[turn] + term
    own_ref[...] = sum_area[0]
    for turn in range(1, owners):
        encode(sum_area[turn], coded_refs[turn - 1])


def project(slabs, basis, first, owners, modes, held=False):
    count, steps, cells = slabs.shape
    others = len(owners) - 1
    own, *coded = pl.pallas_call(
        functools.partial(project_kernel, held),
        in_specs=[
            pl.BlockSpec(memory_space=pltpu.SMEM),
            pl.BlockSpec(memory_space=pltpu.VMEM if held else pl.ANY),
            pl.BlockSpec(memory_space=pl.ANY),
        ],
        out_specs=[pl.BlockSpec(memory_space=pltpu.VMEM)] * (1 + others),
        out_shape=[jax.ShapeDtypeStruct((steps, modes), F32)]
        + [jax.ShapeDtypeStruct((steps + PAD, modes), jnp.int16)] * others,
        scratch_shapes=[
            pltpu.VMEM((count,) + basis.shape[1:], basis.dtype),
            pltpu.VMEM((1 + others, steps, modes), F32),
            pltpu.SemaphoreType.DMA((count,)),
        ]
        + ([] if held else [pltpu.VMEM(slabs.shape, slabs.dtype), pltpu.SemaphoreType.DMA((count,))]),
        compiler_params=pltpu.CompilerParams(vmem_limit_bytes=(36 if held else 60) * LIMIT // 16),
        cost_estimate=pl.CostEstimate(
            flops=2 * count * steps * cells * modes * (1 + others),
            bytes_accessed=2 * count * cells * (steps + modes * (1 + others)) + 4 * steps * modes,
            transcendentals=0,
        ),
    )(jnp.stack([first] + owners), slabs, basis)
    return own, coded


def fold_kernel(own_ref, *refs):
    total = own_ref[...]
    for ref in refs[:-1]:
        total = total + decode(ref)
    encode(total, refs[-1])


def call(kernel, inputs, outputs, scratch, flops):
    smem = pl.BlockSpec(memory_space=pltpu.SMEM)
    vmem = pl.BlockSpec(memory_space=pltpu.VMEM)
    moved = sum(4 * x.size for x in inputs) + sum(4 * x.size for x in outputs)
    return pl.pallas_call(
        kernel,
        in_specs=[smem if x.dtype == jnp.int32 else vmem for x in inputs],
        out_specs=[vmem] * len(outputs),
        out_shape=outputs,
        scratch_shapes=scratch,
        compiler_params=pltpu.CompilerParams(vmem_limit_bytes=LIMIT),
        cost_estimate=pl.CostEstimate(flops=flops, bytes_accessed=moved, transcendentals=0),
    )(*inputs)


def swap_halves(block, axis):
    half = lax.axis_size(axis) // 2
    return lax.ppermute(block, axis, [(i, (i + half) % (2 * half)) for i in range(2 * half)])


def send_along(term, axis, turn):
    count = lax.axis_size(axis)
    return lax.ppermute(term, axis, [(i, (i + turn) % count) for i in range(count)])


def body(observations, pod_basis, decay, step_mask, process_var, obs_var, prior_mean, prior_var):
    tm_count = lax.axis_size("tm")
    space_count = lax.axis_size("space")
    steps, modes = decay.shape
    chunks = steps // CHUNK
    rank = lax.axis_index("tm").astype(jnp.int32)
    me = rank.reshape(1)
    side = lax.axis_index("space").astype(jnp.int32)
    shape = functools.partial(jax.ShapeDtypeStruct, dtype=F32)
    area = pltpu.VMEM
    group = tm_count // 2
    groups = [[half * group + i for i in range(group)] for half in range(2)]
    half = rank // group

    seen = jnp.broadcast_to(step_mask.astype(F32)[:, None], (steps, modes))
    q, r = process_var[None, :], obs_var[None, :]
    flat = (chunks, modes)
    deep = (CHUNK, chunks, modes)
    strips = area((modes // LANES, steps, LANES), F32)
    slabs = observations.reshape(2, group, steps, observations.shape[3])
    basis = pod_basis.reshape(tm_count, -1, pod_basis.shape[3])
    first = half * group
    owners = [lax.rem(side + turn, space_count) for turn in range(space_count)]
    far = lax.dynamic_index_in_dim(slabs, 1 - half, 0, keepdims=False)
    far, q = lax.optimization_barrier((far, q))
    far = lax.all_to_all(far, "tm", 0, 0, axis_index_groups=groups, tiled=True)
    chunk_totals, block_totals = call(
        totals_kernel, (me, decay, seen, q, r), [shape((3,) + flat), shape((3, modes))], [strips] * 2, 40 * steps * modes
    )
    block_totals, own_half = lax.optimization_barrier((block_totals, half))
    near = lax.dynamic_index_in_dim(slabs, own_half, 0, keepdims=False)
    blocks = gather_near(block_totals, "tm")
    far, near, blocks = lax.optimization_barrier((far, near, blocks))
    near = lax.all_to_all(near, "tm", 0, 0, axis_index_groups=groups, tiled=True)

    own, theirs = project(far, basis, first, owners, modes)
    arriving = [send_along(term, "space", turn + 1) for turn, term in enumerate(theirs)]
    coded = jax.ShapeDtypeStruct((steps + PAD, modes), jnp.int16)
    (crossing,) = call(fold_kernel, (own, *arriving), [coded], [], 8 * steps * modes)
    blocks, near, _ = lax.optimization_barrier((blocks, near, crossing))
    while blocks.shape[0] * 2 < tm_count:
        blocks = gather_across(blocks, "tm")
    blocks, near = lax.optimization_barrier((blocks, near))
    crossing = swap_halves(crossing, "tm")
    blocks = gather_across(blocks, "tm")

    own, theirs = project(near, basis, first, owners, modes, True)
    parts = [send_along(term, "space", turn + 1) for turn, term in enumerate(theirs)] + [crossing]
    own, chunk_totals = lax.optimization_barrier((own, chunk_totals))
    parts.insert(0, own)
    *maps, whole, carry, edge, log_variance = call(
        functools.partial(gains_kernel, tm_count),
        (me, decay, seen, q, r, prior_var[None, :], chunk_totals, blocks),
        [shape(deep)] * 6 + [shape((3,) + deep), shape((2,) + flat), shape((2, tm_count, modes)), shape((steps, modes))],
        [area((2,) + flat, F32), area(deep, F32), area(deep, F32), strips, strips],
        80 * steps * modes,
    )

    coefficients, mean, smooth, ends = call(
        functools.partial(means_kernel, len(parts)),
        (*parts, *maps, carry),
        [shape((steps, modes)), shape(deep), shape(deep), shape((2, modes))],
        [area((2,) + flat, F32), strips],
        12 * steps * modes,
    )
    ends = jnp.broadcast_to(ends[None], (tm_count,) + ends.shape)
    ends = lax.all_to_all(ends, "tm", 0, 0, tiled=True)
    filtered, smoothed = call(
        functools.partial(finish_kernel, tm_count),
        (me, prior_mean[None, :], whole, edge, ends, mean, smooth),
        [shape((steps, modes))] * 2,
        [strips, strips],
        8 * steps * modes,
    )
    return coefficients, filtered, smoothed, log_variance


def solution(mesh):
    return jax.shard_map(
        body,
        mesh=mesh,
        in_specs=(
            P(None, "tm", "space", None),
            P(None, "space", None, None),
            P("tm", "space"),
            P("tm"),
            P("space"),
            P("space"),
            P("space"),
            P("space"),
        ),
        out_specs=(P("tm", "space"), P("tm", "space"), P("tm", "space"), P("tm", "space")),
        check_vma=False,
    )
```

profile of v0, /device:TPU:0, one launch (start us, length us, event | category | flops | bytes accessed | tf_op | source)
XLA Modules:
  0.0 103.3 jit_solution(7820870756799474611)
XLA Ops:
  0.7 3.0 %dynamic-slice_bitcast_fusion.1 = bf16[8,256,512]{2,1,0:T(8,128)(2,1)} fusion(bf16[2,8,256,512]{3,2,1,0:T(8,128)(2,1)} %bitcast.27, s32[]{:T(128)S(6)} %select_n.13), kind=kLoop, calls=%fused_computation.1 | loop fusion | bytes 4194308 | tf_op jit(solution)/shard_map/jit(dynamic_index_in_dim)/squeeze | solution.py:410
  3.7 5.4 %all-to-all-start = ((bf16[8,256,512]{2,1,0:T(8,128)(2,1)}), bf16[8,256,512]{2,1,0:T(8,128)(2,1)S(1)}, u32[]{:S(2)}, u32[]{:S(2)}) async-start(bf16[8,256,512]{2,1,0:T(8,128)(2,1)} %dynamic-slice_bitcast_fusion.1), calls=%async_computation | async-start | bytes 4194304 | tf_op jit(solution)/shard_map/all_to_all | solution.py:412
  10.1 1.8 %collective-permute-start.2 = (f32[3,512]{1,0:T(4,128)S(1)}, f32[3,512]{1,0:T(4,128)S(1)}, u32[]{:S(2)}, u32[]{:S(2)}) collective-permute-start(f32[3,512]{1,0:T(4,128)S(1)} %get-tuple-element.43), channel_id=1, source_target_pairs={{0,6},{2,0},{4,2},{6,4},{8,14},{10,8},{12,10},{14,12},{16,22},{18,... | collective-permute-start | bytes 18440 | tf_op jit(solution)/shard_map/ppermute | solution.py:21
  12.4 3.1 %dynamic-slice_bitcast_fusion = bf16[8,256,512]{2,1,0:T(8,128)(2,1)} fusion(bf16[2,8,256,512]{3,2,1,0:T(8,128)(2,1)} %bitcast.28, s32[]{:T(128)S(6)} %select_n.14), kind=kLoop, calls=%fused_computation | loop fusion | bytes 4194308 | tf_op jit(solution)/shard_map/jit(dynamic_index_in_dim)/squeeze | solution.py:417
  15.5 17.4 %collective-permute-done.2 = f32[3,512]{1,0:T(4,128)S(1)} collective-permute-done((f32[3,512]{1,0:T(4,128)S(1)}, f32[3,512]{1,0:T(4,128)S(1)}, u32[]{:S(2)}, u32[]{:S(2)}) %collective-permute-start.2) | collective-permute-done | bytes 6176 | tf_op jit(solution)/shard_map/ppermute | solution.py:21
  32.9 2.2 %collective-permute-done.1 = f32[3,512]{1,0:T(4,128)S(1)} collective-permute-done((f32[3,512]{1,0:T(4,128)S(1)}, f32[3,512]{1,0:T(4,128)S(1)}, u32[]{:S(2)}, u32[]{:S(2)}) %collective-permute-start.1) | collective-permute-done | bytes 6176 | tf_op jit(solution)/shard_map/ppermute | solution.py:21
  35.7 1.3 %copy-done.7 = bf16[8,256,512]{2,1,0:T(8,128)(2,1)} copy-done((bf16[8,256,512]{2,1,0:T(8,128)(2,1)}, bf16[8,256,512]{2,1,0:T(8,128)(2,1)S(1)}, u32[]{:S(2)}) %copy-start.7) | copy-done | bytes 2097176
  37.0 3.6 %all-to-all-start.1 = ((bf16[8,256,512]{2,1,0:T(8,128)(2,1)}), bf16[8,256,512]{2,1,0:T(8,128)(2,1)S(1)}, u32[]{:S(2)}, u32[]{:S(2)}) async-start(bf16[8,256,512]{2,1,0:T(8,128)(2,1)} %dynamic-slice_bitcast_fusion), calls=%async_computation.1 | async-start | bytes 4194304 | tf_op jit(solution)/shard_map/all_to_all | solution.py:420
  41.3 6.2 %shard_map.112 = (f32[256,512]{1,0:T(8,128)}, s16[272,512]{1,0:T(8,128)(2,1)}) custom-call(s32[3]{0:T(128)} %pad_add_fusion.at_ref, bf16[8,256,512]{2,1,0:T(8,128)(2,1)} %copy-done.7, bf16[16,512,1024]{2,1,0:T(8,128)(2,1)} %bitcast.25), custom_call_target="tpu_custom_call" | custom-call | flops 2147483648 | bytes 11010048 | tf_op jit(solution)/shard_map/pallas_call | solution.py:329
  47.5 1.6 %collective-permute-start.3 = (s16[272,512]{1,0:T(8,128)(2,1)}, s16[272,512]{1,0:T(8,128)(2,1)S(1)}, u32[]{:S(2)}, u32[]{:S(2)}) collective-permute-start(s16[272,512]{1,0:T(8,128)(2,1)} %get-tuple-element.48), channel_id=1, source_target_pairs={{0,1},{1,0},{2,3},{3,2},{4,5},{5,4},{6,7},{7,6},{8,9},{9,8},{10,11... | collective-permute-start | bytes 835592 | tf_op jit(solution)/shard_map/ppermute | solution.py:384
  49.1 7.6 %collective-permute-done.3.refs_0_ = s16[272,512]{1,0:T(8,128)(2,1)S(1)} collective-permute-done((s16[272,512]{1,0:T(8,128)(2,1)}, s16[272,512]{1,0:T(8,128)(2,1)S(1)}, u32[]{:S(2)}, u32[]{:S(2)}) %collective-permute-start.3) | collective-permute-done | bytes 278560 | tf_op jit(solution)/shard_map/ppermute | solution.py:384
  56.7 1.0 %copy-done.1 = f32[256,512]{1,0:T(8,128)S(1)} copy-done((f32[256,512]{1,0:T(8,128)S(1)}, f32[256,512]{1,0:T(8,128)}, u32[]{:S(2)}) %copy-start.1) | copy-done | bytes 524312
  58.0 8.3 %all-to-all-done.1.slab_ref = bf16[8,256,512]{2,1,0:T(8,128)(2,1)S(1)} async-done(((bf16[8,256,512]{2,1,0:T(8,128)(2,1)}), bf16[8,256,512]{2,1,0:T(8,128)(2,1)S(1)}, u32[]{:S(2)}, u32[]{:S(2)}) %all-to-all-start.1) | async-done | bytes 2097184 | tf_op jit(solution)/shard_map/all_to_all | solution.py:420
  66.3 1.5 %collective-permute-start.4 = (f32[4,3,512]{2,1,0:T(4,128)}, f32[4,3,512]{2,1,0:T(4,128)S(1)}, u32[]{:S(2)}, u32[]{:S(2)}) collective-permute-start(f32[4,3,512]{2,1,0:T(4,128)} %pad_maximum_fusion.2), channel_id=1, source_target_pairs={{0,8},{2,10},{4,12},{6,14},{8,0},{10,2},{12,4},{14,6},{16,24},{18,... | collective-permute-start | bytes 73736 | tf_op jit(solution)/shard_map/ppermute | solution.py:40
  67.7 2.6 %collective-permute-start.6 = (s16[272,512]{1,0:T(8,128)(2,1)S(1)}, s16[272,512]{1,0:T(8,128)(2,1)S(1)}, u32[]{:S(2)}, u32[]{:S(2)}) collective-permute-start(s16[272,512]{1,0:T(8,128)(2,1)S(1)} %shard_map.113), channel_id=1, source_target_pairs={{0,16},{2,18},{4,20},{6,22},{8,24},{10,26},{12,28},{14,30},{16,0},... | collective-permute-start | bytes 835592 | tf_op jit(solution)/shard_map/ppermute | solution.py:379
  70.3 1.2 %collective-permute-done.4 = f32[4,3,512]{2,1,0:T(4,128)S(1)} collective-permute-done((f32[4,3,512]{2,1,0:T(4,128)}, f32[4,3,512]{2,1,0:T(4,128)S(1)}, u32[]{:S(2)}, u32[]{:S(2)}) %collective-permute-start.4) | collective-permute-done | bytes 24608 | tf_op jit(solution)/shard_map/ppermute | solution.py:40
  72.3 4.7 %shard_map.114 = (f32[256,512]{1,0:T(8,128)S(1)}, s16[272,512]{1,0:T(8,128)(2,1)S(1)}) custom-call(s32[3]{0:T(128)S(1)} %copy-done.4, bf16[8,256,512]{2,1,0:T(8,128)(2,1)S(1)} %all-to-all-done.1.slab_ref, bf16[16,512,1024]{2,1,0:T(8,128)(2,1)} %bitcast.26), custom_call_target="tpu_custom_call" | custom-call | flops 2147483648 | bytes 11010048 | tf_op jit(solution)/shard_map/pallas_call | solution.py:329
  77.0 1.6 %collective-permute-start.5 = (s16[272,512]{1,0:T(8,128)(2,1)S(1)}, s16[272,512]{1,0:T(8,128)(2,1)S(1)}, u32[]{:S(2)}, u32[]{:S(2)}) collective-permute-start(s16[272,512]{1,0:T(8,128)(2,1)S(1)} %get-tuple-element.55), channel_id=1, source_target_pairs={{0,1},{1,0},{2,3},{3,2},{4,5},{5,4},{6,7},{7,6},{8,9},{9,8},{10,11... | collective-permute-start | bytes 835592 | tf_op jit(solution)/shard_map/ppermute | solution.py:384
  78.6 1.9 %collective-permute-start.7 = (f32[8,3,512]{2,1,0:T(4,128)S(1)}, f32[8,3,512]{2,1,0:T(4,128)S(1)}, u32[]{:S(2)}, u32[]{:S(2)}) collective-permute-start(f32[8,3,512]{2,1,0:T(4,128)S(1)} %pad_maximum_fusion.1), channel_id=1, source_target_pairs={{0,16},{2,18},{4,20},{6,22},{8,24},{10,26},{12,28},{14,30},{16,0},... | collective-permute-start | bytes 147464 | tf_op jit(solution)/shard_map/ppermute | solution.py:40
  80.5 4.0 %collective-permute-done.7 = f32[8,3,512]{2,1,0:T(4,128)S(1)} collective-permute-done((f32[8,3,512]{2,1,0:T(4,128)S(1)}, f32[8,3,512]{2,1,0:T(4,128)S(1)}, u32[]{:S(2)}, u32[]{:S(2)}) %collective-permute-start.7) | collective-permute-done | bytes 49184 | tf_op jit(solution)/shard_map/ppermute | solution.py:40
  84.5 2.8 %shard_map.115 = (f32[16,16,512]{2,1,0:T(8,128)S(1)}, f32[16,16,512]{2,1,0:T(8,128)S(1)}, f32[16,16,512]{2,1,0:T(8,128)S(1)}, f32[16,16,512]{2,1,0:T(8,128)S(1)}...) custom-call(s32[1]{0:T(128)} %bitcast.6.me_ref, ...), custom_call_target="tpu_custom_call" | custom-call | flops 10485760 | bytes 6625284 | tf_op jit(solution)/shard_map/pallas_call | solution.py:366
  87.4 1.9 %shard_map.116 = (f32[256,512]{1,0:T(8,128)}, f32[16,16,512]{2,1,0:T(8,128)S(1)}, f32[16,16,512]{2,1,0:T(8,128)S(1)}, f32[2,512]{1,0:T(2,128)S(1)}) custom-call(f32[256,512]{1,0:T(8,128)S(1)} %get-tuple-element.54.refs_0_, s16[272,512]{1,0:T(8,128)(2,1)S(1)} %collective-permute-done.5.refs_1_, s16[272,512]{1,0:T(8,128)(2,1)S(1)} %collective-permute-done.6.refs_2_, ...), custom_call_target="tpu_custom_call" | custom-call | flops 1572864 | bytes 6426624 | tf_op jit(solution)/shard_map/pallas_call | solution.py:366
  89.3 12.4 %all_to_all.15.blocks_ref = f32[16,2,512]{2,1,0:T(2,128)S(1)} all-to-all(f32[16,2,512]{2,1,0:T(2,128)S(1)} %broadcast_in_dim.29), channel_id=1, replica_groups=mesh['tm'=16,'space'=2] {'tm'}, dimensions={0} | all-to-all | bytes 131072 | tf_op jit(solution)/shard_map/all_to_all | solution.py:453
  101.6 1.6 %shard_map.117 = (f32[256,512]{1,0:T(8,128)}, f32[256,512]{1,0:T(8,128)}) custom-call(s32[1]{0:T(128)} %bitcast.6.me_ref, f32[1,512]{1,0:T(1,128)S(1)} %bitcast.24, f32[3,16,16,512]{3,2,1,0:T(8,128)S(1)} %get-tuple-element.66.whole_ref, f32[2,16,512]{2,1,0:T(8,128)S(1)} %get-tuple-element.67.edge_ref, f32[16,2,512]{2,1,0:T(2,128)S(1)} %all_to_all.15.blocks_ref, ...), custom_call_target="tpu_custom_call" | custom-call | flops 1048576 | bytes 3803140 | tf_op jit(solution)/shard_map/pallas_call | solution.py:366
  (31 shorter events, 3.8 us)
Async XLA Ops:
  3.7 5.4 %copy-start.8 = (s32[256]{0:T(256)S(1)}, s32[256]{0:T(256)}, u32[]{:S(2)}) copy-start(s32[256]{0:T(256)} %param.11) | copy-start | bytes 3076
  3.7 5.5 %copy-start = (f32[256,512]{1,0:T(8,128)S(1)}, f32[256,512]{1,0:T(8,128)}, u32[]{:S(2)}) copy-start(f32[256,512]{1,0:T(8,128)} %decay_in.3) | copy-start | bytes 1572868
  3.7 5.5 %copy-start.2 = (f32[512]{0:T(512)S(1)}, f32[512]{0:T(512)}, u32[]{:S(2)}) copy-start(f32[512]{0:T(512)} %param.12) | copy-start | bytes 6148
  3.7 5.5 %copy-start.3 = (f32[512]{0:T(512)S(1)}, f32[512]{0:T(512)}, u32[]{:S(2)}) copy-start(f32[512]{0:T(512)} %param.13) | copy-start | bytes 6148
  3.7 32.0 %all-to-all-start = ((bf16[8,256,512]{2,1,0:T(8,128)(2,1)}), bf16[8,256,512]{2,1,0:T(8,128)(2,1)S(1)}, u32[]{:S(2)}, u32[]{:S(2)}) async-start(bf16[8,256,512]{2,1,0:T(8,128)(2,1)} %dynamic-slice_bitcast_fusion.1), calls=%async_computation | async-start | bytes 4194304 | tf_op jit(solution)/shard_map/all_to_all | solution.py:412
  10.1 22.8 %collective-permute-start.2 = (f32[3,512]{1,0:T(4,128)S(1)}, f32[3,512]{1,0:T(4,128)S(1)}, u32[]{:S(2)}, u32[]{:S(2)}) collective-permute-start(f32[3,512]{1,0:T(4,128)S(1)} %get-tuple-element.43), channel_id=1, source_target_pairs={{0,6},{2,0},{4,2},{6,4},{8,14},{10,8},{12,10},{14,12},{16,22},{18,... | collective-permute-start | bytes 18440 | tf_op jit(solution)/shard_map/ppermute | solution.py:21
  11.9 23.2 %collective-permute-start.1 = (f32[3,512]{1,0:T(4,128)S(1)}, f32[3,512]{1,0:T(4,128)S(1)}, u32[]{:S(2)}, u32[]{:S(2)}) collective-permute-start(f32[3,512]{1,0:T(4,128)S(1)} %get-tuple-element.43), channel_id=1, source_target_pairs={{0,4},{2,6},{4,0},{6,2},{8,12},{10,14},{12,8},{14,10},{16,20},{18,... | collective-permute-start | bytes 18440 | tf_op jit(solution)/shard_map/ppermute | solution.py:21
  12.3 22.8 %collective-permute-start = (f32[3,512]{1,0:T(4,128)S(1)}, f32[3,512]{1,0:T(4,128)S(1)}, u32[]{:S(2)}, u32[]{:S(2)}) collective-permute-start(f32[3,512]{1,0:T(4,128)S(1)} %get-tuple-element.43), channel_id=1, source_target_pairs={{0,2},{2,4},{4,6},{6,0},{8,10},{10,12},{12,14},{14,8},{16,18},{18,... | collective-permute-start | bytes 18440 | tf_op jit(solution)/shard_map/ppermute | solution.py:21
  35.7 1.3 %copy-start.7 = (bf16[8,256,512]{2,1,0:T(8,128)(2,1)}, bf16[8,256,512]{2,1,0:T(8,128)(2,1)S(1)}, u32[]{:S(2)}) copy-start(bf16[8,256,512]{2,1,0:T(8,128)(2,1)S(1)} %all-to-all-done.slab_ref) | copy-start | bytes 6291460
  37.0 29.2 %all-to-all-start.1 = ((bf16[8,256,512]{2,1,0:T(8,128)(2,1)}), bf16[8,256,512]{2,1,0:T(8,128)(2,1)S(1)}, u32[]{:S(2)}, u32[]{:S(2)}) async-start(bf16[8,256,512]{2,1,0:T(8,128)(2,1)} %dynamic-slice_bitcast_fusion), calls=%async_computation.1 | async-start | bytes 4194304 | tf_op jit(solution)/shard_map/all_to_all | solution.py:420
  41.3 31.0 %copy-start.4 = (s32[3]{0:T(128)S(1)}, s32[3]{0:T(128)}, u32[]{:S(2)}) copy-start(s32[3]{0:T(128)} %pad_add_fusion.at_ref) | copy-start | bytes 40
  47.5 9.2 %collective-permute-start.3 = (s16[272,512]{1,0:T(8,128)(2,1)}, s16[272,512]{1,0:T(8,128)(2,1)S(1)}, u32[]{:S(2)}, u32[]{:S(2)}) collective-permute-start(s16[272,512]{1,0:T(8,128)(2,1)} %get-tuple-element.48), channel_id=1, source_target_pairs={{0,1},{1,0},{2,3},{3,2},{4,5},{5,4},{6,7},{7,6},{8,9},{9,8},{10,11... | collective-permute-start | bytes 835592 | tf_op jit(solution)/shard_map/ppermute | solution.py:384
  56.7 1.0 %copy-start.1 = (f32[256,512]{1,0:T(8,128)S(1)}, f32[256,512]{1,0:T(8,128)}, u32[]{:S(2)}) copy-start(f32[256,512]{1,0:T(8,128)} %get-tuple-element.47.own_ref) | copy-start | bytes 1572868
  66.3 5.3 %collective-permute-start.4 = (f32[4,3,512]{2,1,0:T(4,128)}, f32[4,3,512]{2,1,0:T(4,128)S(1)}, u32[]{:S(2)}, u32[]{:S(2)}) collective-permute-start(f32[4,3,512]{2,1,0:T(4,128)} %pad_maximum_fusion.2), channel_id=1, source_target_pairs={{0,8},{2,10},{4,12},{6,14},{8,0},{10,2},{12,4},{14,6},{16,24},{18,... | collective-permute-start | bytes 73736 | tf_op jit(solution)/shard_map/ppermute | solution.py:40
  67.7 19.6 %collective-permute-start.6 = (s16[272,512]{1,0:T(8,128)(2,1)S(1)}, s16[272,512]{1,0:T(8,128)(2,1)S(1)}, u32[]{:S(2)}, u32[]{:S(2)}) collective-permute-start(s16[272,512]{1,0:T(8,128)(2,1)S(1)} %shard_map.113), channel_id=1, source_target_pairs={{0,16},{2,18},{4,20},{6,22},{8,24},{10,26},{12,28},{14,30},{16,0},... | collective-permute-start | bytes 835592 | tf_op jit(solution)/shard_map/ppermute | solution.py:379
  72.3 12.2 %copy-start.5 = (f32[512]{0:T(512)S(1)}, f32[512]{0:T(512)}, u32[]{:S(2)}) copy-start(f32[512]{0:T(512)} %param.15) | copy-start | bytes 6148
  77.0 10.3 %collective-permute-start.5 = (s16[272,512]{1,0:T(8,128)(2,1)S(1)}, s16[272,512]{1,0:T(8,128)(2,1)S(1)}, u32[]{:S(2)}, u32[]{:S(2)}) collective-permute-start(s16[272,512]{1,0:T(8,128)(2,1)S(1)} %get-tuple-element.55), channel_id=1, source_target_pairs={{0,1},{1,0},{2,3},{3,2},{4,5},{5,4},{6,7},{7,6},{8,9},{9,8},{10,11... | collective-permute-start | bytes 835592 | tf_op jit(solution)/shard_map/ppermute | solution.py:384
  78.6 5.9 %collective-permute-start.7 = (f32[8,3,512]{2,1,0:T(4,128)S(1)}, f32[8,3,512]{2,1,0:T(4,128)S(1)}, u32[]{:S(2)}, u32[]{:S(2)}) collective-permute-start(f32[8,3,512]{2,1,0:T(4,128)S(1)} %pad_maximum_fusion.1), channel_id=1, source_target_pairs={{0,16},{2,18},{4,20},{6,22},{8,24},{10,26},{12,28},{14,30},{16,0},... | collective-permute-start | bytes 147464 | tf_op jit(solution)/shard_map/ppermute | solution.py:40
  87.4 14.3 %copy-start.6 = (f32[512]{0:T(512)S(1)}, f32[512]{0:T(512)}, u32[]{:S(2)}) copy-start(f32[512]{0:T(512)} %param.14) | copy-start | bytes 6148
where the time goes:
time: 104 us; the launch traced here: 103 us
  waiting for transfers between devices  40.7 us (39%)
  starting transfers between devices  20.4 us (20%)
  Pallas kernels  18.3 us (18%)
  blocking collectives  12.4 us (12%)
  local copies, waits for them, and re-layouts  8.57 us (8%)
  other arithmetic  2.08 us (2%)
    ppermute x3, waiting for transfers between devices, rotate(): return lax.ppermute(block, axis, route)  19.6 us
    all_to_all x1, blocking collectives, body(): ends = lax.all_to_all(ends, 'tm', 0, 0, tiled=True)  12.4 us
    pallas_call x2, Pallas kernels, project(): pl.pallas_call(functools.partial(project_kernel, held), in_specs=[pl.Bloc...  10.9 us
    all_to_all x1, waiting for transfers between devices, body(): lax.all_to_all(near, 'tm', 0, 0, axis_index_groups=groups, tiled=True)  8.27 us
    ppermute x2, waiting for transfers between devices, send_along(): lax.ppermute(term, axis, [(i, (i + turn) % count) for i in range(count)])  7.62 us
    pallas_call x5, Pallas kernels, call(): pl.pallas_call(kernel, in_specs=[smem if x.dtype == jnp.int32 else vmem f...  7.41 us
    all_to_all x1, starting transfers between devices, body(): far = lax.all_to_all(far, 'tm', 0, 0, axis_index_groups=groups, tiled=True)  5.37 us
    ppermute x2, waiting for transfers between devices, gather_across(): lax.ppermute(blocks, axis, [(i, i ^ away) for i in range(lax.axis_size(ax...  5.21 us
  transfers between devices with their start and end apart: 10, of which 6 were waited for; matrix products, arithmetic and copies ran while one was open for 5% of the time, Pallas kernels for 14%

commit v1 on v0

--- a/solution.py
+++ b/solution.py
@@ -34,11 +34,13 @@
     return jnp.stack([rows] + [rotate(rows, axis, s, group) for s in range(1, group)])
 
 
-def gather_across(blocks, axis):
-    away = blocks.shape[0]
-    return jnp.concatenate(
-        [blocks, lax.ppermute(blocks, axis, [(i, i ^ away) for i in range(lax.axis_size(axis))])], 0
-    )
+def gather_far(near, axis):
+    count = lax.axis_size(axis)
+    group = near.shape[0]
+    rest = [
+        lax.ppermute(near, axis, [(i, i ^ (turn * group)) for i in range(count)]) for turn in range(1, count // group)
+    ]
+    return jnp.concatenate([near] + rest, 0)
 
 
 def place(me, j, count):
@@ -423,16 +425,13 @@
     arriving = [send_along(term, "space", turn + 1) for turn, term in enumerate(theirs)]
     coded = jax.ShapeDtypeStruct((steps + PAD, modes), jnp.int16)
     (crossing,) = call(fold_kernel, (own, *arriving), [coded], [], 8 * steps * modes)
-    blocks, near, _ = lax.optimization_barrier((blocks, near, crossing))
-    while blocks.shape[0] * 2 < tm_count:
-        blocks = gather_across(blocks, "tm")
-    blocks, near = lax.optimization_barrier((blocks, near))
+    near, _ = lax.optimization_barrier((near, crossing))
     crossing = swap_halves(crossing, "tm")
-    blocks = gather_across(blocks, "tm")
+    blocks = gather_far(blocks, "tm")
 
     own, theirs = project(near, basis, first, owners, modes, True)
     parts = [send_along(term, "space", turn + 1) for turn, term in enumerate(theirs)] + [crossing]
-    own, chunk_totals = lax.optimization_barrier((own, chunk_totals))
+    own, chunk_totals, blocks = lax.optimization_barrier((own, chunk_totals, blocks))
     parts.insert(0, own)
     *maps, whole, carry, edge, log_variance = call(
         functools.partial(gains_kernel, tm_count),

time: 104 us -> 103 us (level)
  starting transfers between devices: 20.4 us -> 21.5 us
    ppermute x2 -> x3, waiting for transfers between devices: 5.21 us -> 1.89 us  [gather_far(): lax.ppermute(near, axis, [(i, i ^ turn * group) for i in range(count)])]
    all_to_all x1, waiting for transfers between devices: 8.27 us -> 10.9 us  [body(): lax.all_to_all(near, 'tm', 0, 0, axis_index_groups=groups, tiled=True)]
    ppermute x2 -> x3, starting transfers between devices: 3.34 us -> 4.39 us  [gather_far(): lax.ppermute(near, axis, [(i, i ^ turn * group) for i in range(count)])]
    unnamed x18 -> x20, local copies, waits for them, and re-layouts: 2.37 us -> 2.38 us
  transfers between devices with their start and end apart: 10 -> 11, of which waited for: 6 -> 6; matrix products, arithmetic and copies ran while one was open for 5% -> 4% of each run, Pallas kernels for 14% -> 15%
where the time goes in v1:
time: 103 us
  waiting for transfers between devices  40.1 us (39%)
  starting transfers between devices  21.5 us (21%)
  Pallas kernels  19 us (18%)
  blocking collectives  11.4 us (11%)
  local copies, waits for them, and re-layouts  8.6 us (8%)
  other arithmetic  1.31 us (1%)
    ppermute x3, waiting for transfers between devices, rotate(): return lax.ppermute(block, axis, route)  19.6 us
    all_to_all x1, blocking collectives, body(): ends = lax.all_to_all(ends, 'tm', 0, 0, tiled=True)  11.4 us
    all_to_all x1, waiting for transfers between devices, body(): lax.all_to_all(near, 'tm', 0, 0, axis_index_groups=groups, tiled=True)  10.9 us
    pallas_call x2, Pallas kernels, project(): pl.pallas_call(functools.partial(project_kernel, held), in_specs=[pl.Bloc...  10.9 us
    pallas_call x5, Pallas kernels, call(): pl.pallas_call(kernel, in_specs=[smem if x.dtype == jnp.int32 else vmem f...  8.13 us
    ppermute x2, waiting for transfers between devices, send_along(): lax.ppermute(term, axis, [(i, (i + turn) % count) for i in range(count)])  7.62 us
    all_to_all x1, starting transfers between devices, body(): far = lax.all_to_all(far, 'tm', 0, 0, axis_index_groups=groups, tiled=True)  5.37 us
    ppermute x3, starting transfers between devices, gather_far(): lax.ppermute(near, axis, [(i, i ^ turn * group) for i in range(count)])  4.39 us
  transfers between devices with their start and end apart: 11, of which 6 were waited for; matrix products, arithmetic and copies ran while one was open for 4% of the time, Pallas kernels for 15%

profile of v1, /device:TPU:0, one launch (start us, length us, event | category | flops | bytes accessed | tf_op | source)
XLA Modules:
  0.0 102.6 jit_solution(11649057783639069932)
XLA Ops:
  0.7 3.0 %dynamic-slice_bitcast_fusion.1 = bf16[8,256,512]{2,1,0:T(8,128)(2,1)} fusion(bf16[2,8,256,512]{3,2,1,0:T(8,128)(2,1)} %bitcast.27, s32[]{:T(128)S(6)} %select_n.13), kind=kLoop, calls=%fused_computation.1 | loop fusion | bytes 4194308 | tf_op jit(solution)/shard_map/jit(dynamic_index_in_dim)/squeeze | solution.py:412
  3.7 5.4 %all-to-all-start = ((bf16[8,256,512]{2,1,0:T(8,128)(2,1)}), bf16[8,256,512]{2,1,0:T(8,128)(2,1)S(1)}, u32[]{:S(2)}, u32[]{:S(2)}) async-start(bf16[8,256,512]{2,1,0:T(8,128)(2,1)} %dynamic-slice_bitcast_fusion.1), calls=%async_computation | async-start | bytes 4194304 | tf_op jit(solution)/shard_map/all_to_all | solution.py:414
  10.1 1.8 %collective-permute-start.2 = (f32[3,512]{1,0:T(4,128)S(1)}, f32[3,512]{1,0:T(4,128)S(1)}, u32[]{:S(2)}, u32[]{:S(2)}) collective-permute-start(f32[3,512]{1,0:T(4,128)S(1)} %get-tuple-element.41), channel_id=1, source_target_pairs={{0,6},{2,0},{4,2},{6,4},{8,14},{10,8},{12,10},{14,12},{16,22},{18,... | collective-permute-start | bytes 18440 | tf_op jit(solution)/shard_map/ppermute | solution.py:21
  12.5 3.1 %dynamic-slice_bitcast_fusion = bf16[8,256,512]{2,1,0:T(8,128)(2,1)} fusion(bf16[2,8,256,512]{3,2,1,0:T(8,128)(2,1)} %bitcast.28, s32[]{:T(128)S(6)} %select_n.14), kind=kLoop, calls=%fused_computation | loop fusion | bytes 4194308 | tf_op jit(solution)/shard_map/jit(dynamic_index_in_dim)/squeeze | solution.py:419
  15.5 17.4 %collective-permute-done.2 = f32[3,512]{1,0:T(4,128)S(1)} collective-permute-done((f32[3,512]{1,0:T(4,128)S(1)}, f32[3,512]{1,0:T(4,128)S(1)}, u32[]{:S(2)}, u32[]{:S(2)}) %collective-permute-start.2) | collective-permute-done | bytes 6176 | tf_op jit(solution)/shard_map/ppermute | solution.py:21
  32.9 2.2 %collective-permute-done.1 = f32[3,512]{1,0:T(4,128)S(1)} collective-permute-done((f32[3,512]{1,0:T(4,128)S(1)}, f32[3,512]{1,0:T(4,128)S(1)}, u32[]{:S(2)}, u32[]{:S(2)}) %collective-permute-start.1) | collective-permute-done | bytes 6176 | tf_op jit(solution)/shard_map/ppermute | solution.py:21
  35.8 1.3 %copy-done.7 = bf16[8,256,512]{2,1,0:T(8,128)(2,1)} copy-done((bf16[8,256,512]{2,1,0:T(8,128)(2,1)}, bf16[8,256,512]{2,1,0:T(8,128)(2,1)S(1)}, u32[]{:S(2)}) %copy-start.7) | copy-done | bytes 2097176
  37.1 3.6 %all-to-all-start.1 = ((bf16[8,256,512]{2,1,0:T(8,128)(2,1)}), bf16[8,256,512]{2,1,0:T(8,128)(2,1)S(1)}, u32[]{:S(2)}, u32[]{:S(2)}) async-start(bf16[8,256,512]{2,1,0:T(8,128)(2,1)} %dynamic-slice_bitcast_fusion), calls=%async_computation.1 | async-start | bytes 4194304 | tf_op jit(solution)/shard_map/all_to_all | solution.py:422
  41.3 6.2 %shard_map.112 = (f32[256,512]{1,0:T(8,128)}, s16[272,512]{1,0:T(8,128)(2,1)}) custom-call(s32[3]{0:T(128)} %pad_add_fusion.at_ref, bf16[8,256,512]{2,1,0:T(8,128)(2,1)} %copy-done.7, bf16[16,512,1024]{2,1,0:T(8,128)(2,1)} %bitcast.25), custom_call_target="tpu_custom_call" | custom-call | flops 2147483648 | bytes 11010048 | tf_op jit(solution)/shard_map/pallas_call | solution.py:331
  47.5 1.6 %collective-permute-start.3 = (s16[272,512]{1,0:T(8,128)(2,1)}, s16[272,512]{1,0:T(8,128)(2,1)S(1)}, u32[]{:S(2)}, u32[]{:S(2)}) collective-permute-start(s16[272,512]{1,0:T(8,128)(2,1)} %get-tuple-element.45), channel_id=1, source_target_pairs={{0,1},{1,0},{2,3},{3,2},{4,5},{5,4},{6,7},{7,6},{8,9},{9,8},{10,11... | collective-permute-start | bytes 835592 | tf_op jit(solution)/shard_map/ppermute | solution.py:386
  49.1 7.6 %collective-permute-done.3.refs_0_ = s16[272,512]{1,0:T(8,128)(2,1)S(1)} collective-permute-done((s16[272,512]{1,0:T(8,128)(2,1)}, s16[272,512]{1,0:T(8,128)(2,1)S(1)}, u32[]{:S(2)}, u32[]{:S(2)}) %collective-permute-start.3) | collective-permute-done | bytes 278560 | tf_op jit(solution)/shard_map/ppermute | solution.py:386
  56.8 1.0 %copy-done.1 = f32[256,512]{1,0:T(8,128)S(1)} copy-done((f32[256,512]{1,0:T(8,128)S(1)}, f32[256,512]{1,0:T(8,128)}, u32[]{:S(2)}) %copy-start.1) | copy-done | bytes 524312
  57.8 0.9 shard_map.113
  58.7 2.6 %collective-permute-start.8 = (s16[272,512]{1,0:T(8,128)(2,1)}, s16[272,512]{1,0:T(8,128)(2,1)S(1)}, u32[]{:S(2)}, u32[]{:S(2)}) collective-permute-start(s16[272,512]{1,0:T(8,128)(2,1)} %shard_map.113), channel_id=1, source_target_pairs={{0,16},{2,18},{4,20},{6,22},{8,24},{10,26},{12,28},{14,30},{16,0},... | collective-permute-start | bytes 835592 | tf_op jit(solution)/shard_map/ppermute | solution.py:381
  61.3 10.9 %all-to-all-done.1.slab_ref = bf16[8,256,512]{2,1,0:T(8,128)(2,1)S(1)} async-done(((bf16[8,256,512]{2,1,0:T(8,128)(2,1)}), bf16[8,256,512]{2,1,0:T(8,128)(2,1)S(1)}, u32[]{:S(2)}, u32[]{:S(2)}) %all-to-all-start.1) | async-done | bytes 2097184 | tf_op jit(solution)/shard_map/all_to_all | solution.py:422
  72.3 4.7 %shard_map.114 = (f32[256,512]{1,0:T(8,128)S(1)}, s16[272,512]{1,0:T(8,128)(2,1)S(1)}) custom-call(s32[3]{0:T(128)S(1)} %copy-done.4, bf16[8,256,512]{2,1,0:T(8,128)(2,1)S(1)} %all-to-all-done.1.slab_ref, bf16[16,512,1024]{2,1,0:T(8,128)(2,1)} %bitcast.26), custom_call_target="tpu_custom_call" | custom-call | flops 2147483648 | bytes 11010048 | tf_op jit(solution)/shard_map/pallas_call | solution.py:331
  77.0 1.6 %collective-permute-start.7 = (s16[272,512]{1,0:T(8,128)(2,1)S(1)}, s16[272,512]{1,0:T(8,128)(2,1)S(1)}, u32[]{:S(2)}, u32[]{:S(2)}) collective-permute-start(s16[272,512]{1,0:T(8,128)(2,1)S(1)} %get-tuple-element.51), channel_id=1, source_target_pairs={{0,1},{1,0},{2,3},{3,2},{4,5},{5,4},{6,7},{7,6},{8,9},{9,8},{10,11... | collective-permute-start | bytes 835592 | tf_op jit(solution)/shard_map/ppermute | solution.py:386
  78.6 1.1 %collective-permute-start.5 = (f32[4,3,512]{2,1,0:T(4,128)S(1)}, f32[4,3,512]{2,1,0:T(4,128)S(1)}, u32[]{:S(2)}, u32[]{:S(2)}) collective-permute-start(f32[4,3,512]{2,1,0:T(4,128)S(1)} %copy-done.8), channel_id=1, source_target_pairs={{0,16},{2,18},{4,20},{6,22},{8,24},{10,26},{12,28},{14,30},{16,0},... | collective-permute-start | bytes 73736 | tf_op jit(solution)/shard_map/ppermute | solution.py:41
  79.7 3.3 %collective-permute-start.4 = (f32[4,3,512]{2,1,0:T(4,128)S(1)}, f32[4,3,512]{2,1,0:T(4,128)S(1)}, u32[]{:S(2)}, u32[]{:S(2)}) collective-permute-start(f32[4,3,512]{2,1,0:T(4,128)S(1)} %copy-done.8), channel_id=1, source_target_pairs={{0,8},{2,10},{4,12},{6,14},{8,0},{10,2},{12,4},{14,6},{16,24},{18,... | collective-permute-start | bytes 73736 | tf_op jit(solution)/shard_map/ppermute | solution.py:41
  82.9 1.3 %collective-permute-done.6 = f32[4,3,512]{2,1,0:T(4,128)S(1)} collective-permute-done((f32[4,3,512]{2,1,0:T(4,128)S(1)}, f32[4,3,512]{2,1,0:T(4,128)S(1)}, u32[]{:S(2)}, u32[]{:S(2)}) %collective-permute-start.6) | collective-permute-done | bytes 24608 | tf_op jit(solution)/shard_map/ppermute | solution.py:41
  84.9 2.8 %shard_map.115 = (f32[16,16,512]{2,1,0:T(8,128)S(1)}, f32[16,16,512]{2,1,0:T(8,128)S(1)}, f32[16,16,512]{2,1,0:T(8,128)S(1)}, f32[16,16,512]{2,1,0:T(8,128)S(1)}...) custom-call(s32[1]{0:T(128)} %bitcast.6.me_ref, ...), custom_call_target="tpu_custom_call" | custom-call | flops 10485760 | bytes 6625284 | tf_op jit(solution)/shard_map/pallas_call | solution.py:368
  87.7 1.9 %shard_map.116 = (f32[256,512]{1,0:T(8,128)}, f32[16,16,512]{2,1,0:T(8,128)S(1)}, f32[16,16,512]{2,1,0:T(8,128)S(1)}, f32[2,512]{1,0:T(2,128)S(1)}) custom-call(f32[256,512]{1,0:T(8,128)S(1)} %get-tuple-element.50.refs_0_, s16[272,512]{1,0:T(8,128)(2,1)S(1)} %collective-permute-done.7.refs_1_, s16[272,512]{1,0:T(8,128)(2,1)S(1)} %collective-permute-done.8.refs_2_, ...), custom_call_target="tpu_custom_call" | custom-call | flops 1572864 | bytes 6426624 | tf_op jit(solution)/shard_map/pallas_call | solution.py:368
  89.6 11.4 %all_to_all.15.blocks_ref = f32[16,2,512]{2,1,0:T(2,128)S(1)} all-to-all(f32[16,2,512]{2,1,0:T(2,128)S(1)} %broadcast_in_dim.29), channel_id=1, replica_groups=mesh['tm'=16,'space'=2] {'tm'}, dimensions={0} | all-to-all | bytes 131072 | tf_op jit(solution)/shard_map/all_to_all | solution.py:452
  100.9 1.6 %shard_map.117 = (f32[256,512]{1,0:T(8,128)}, f32[256,512]{1,0:T(8,128)}) custom-call(s32[1]{0:T(128)} %bitcast.6.me_ref, f32[1,512]{1,0:T(1,128)S(1)} %bitcast.24, f32[3,16,16,512]{3,2,1,0:T(8,128)S(1)} %get-tuple-element.62.whole_ref, f32[2,16,512]{2,1,0:T(8,128)S(1)} %get-tuple-element.63.edge_ref, f32[16,2,512]{2,1,0:T(2,128)S(1)} %all_to_all.15.blocks_ref, ...), custom_call_target="tpu_custom_call" | custom-call | flops 1048576 | bytes 3803140 | tf_op jit(solution)/shard_map/pallas_call | solution.py:368
  (34 shorter events, 3.4 us)
Async XLA Ops:
  3.7 5.4 %copy-start.9 = (s32[256]{0:T(256)S(1)}, s32[256]{0:T(256)}, u32[]{:S(2)}) copy-start(s32[256]{0:T(256)} %param.11) | copy-start | bytes 3076
  3.7 5.5 %copy-start = (f32[256,512]{1,0:T(8,128)S(1)}, f32[256,512]{1,0:T(8,128)}, u32[]{:S(2)}) copy-start(f32[256,512]{1,0:T(8,128)} %decay_in.3) | copy-start | bytes 1572868
  3.7 5.5 %copy-start.2 = (f32[512]{0:T(512)S(1)}, f32[512]{0:T(512)}, u32[]{:S(2)}) copy-start(f32[512]{0:T(512)} %param.12) | copy-start | bytes 6148
  3.7 5.5 %copy-start.3 = (f32[512]{0:T(512)S(1)}, f32[512]{0:T(512)}, u32[]{:S(2)}) copy-start(f32[512]{0:T(512)} %param.13) | copy-start | bytes 6148
  3.7 32.0 %all-to-all-start = ((bf16[8,256,512]{2,1,0:T(8,128)(2,1)}), bf16[8,256,512]{2,1,0:T(8,128)(2,1)S(1)}, u32[]{:S(2)}, u32[]{:S(2)}) async-start(bf16[8,256,512]{2,1,0:T(8,128)(2,1)} %dynamic-slice_bitcast_fusion.1), calls=%async_computation | async-start | bytes 4194304 | tf_op jit(solution)/shard_map/all_to_all | solution.py:414
  10.1 22.8 %collective-permute-start.2 = (f32[3,512]{1,0:T(4,128)S(1)}, f32[3,512]{1,0:T(4,128)S(1)}, u32[]{:S(2)}, u32[]{:S(2)}) collective-permute-start(f32[3,512]{1,0:T(4,128)S(1)} %get-tuple-element.41), channel_id=1, source_target_pairs={{0,6},{2,0},{4,2},{6,4},{8,14},{10,8},{12,10},{14,12},{16,22},{18,... | collective-permute-start | bytes 18440 | tf_op jit(solution)/shard_map/ppermute | solution.py:21
  11.9 23.2 %collective-permute-start.1 = (f32[3,512]{1,0:T(4,128)S(1)}, f32[3,512]{1,0:T(4,128)S(1)}, u32[]{:S(2)}, u32[]{:S(2)}) collective-permute-start(f32[3,512]{1,0:T(4,128)S(1)} %get-tuple-element.41), channel_id=1, source_target_pairs={{0,4},{2,6},{4,0},{6,2},{8,12},{10,14},{12,8},{14,10},{16,20},{18,... | collective-permute-start | bytes 18440 | tf_op jit(solution)/shard_map/ppermute | solution.py:21
  12.3 22.8 %collective-permute-start = (f32[3,512]{1,0:T(4,128)S(1)}, f32[3,512]{1,0:T(4,128)S(1)}, u32[]{:S(2)}, u32[]{:S(2)}) collective-permute-start(f32[3,512]{1,0:T(4,128)S(1)} %get-tuple-element.41), channel_id=1, source_target_pairs={{0,2},{2,4},{4,6},{6,0},{8,10},{10,12},{12,14},{14,8},{16,18},{18,... | collective-permute-start | bytes 18440 | tf_op jit(solution)/shard_map/ppermute | solution.py:21
  35.8 1.3 %copy-start.7 = (bf16[8,256,512]{2,1,0:T(8,128)(2,1)}, bf16[8,256,512]{2,1,0:T(8,128)(2,1)S(1)}, u32[]{:S(2)}) copy-start(bf16[8,256,512]{2,1,0:T(8,128)(2,1)S(1)} %all-to-all-done.slab_ref) | copy-start | bytes 6291460
  37.1 35.2 %all-to-all-start.1 = ((bf16[8,256,512]{2,1,0:T(8,128)(2,1)}), bf16[8,256,512]{2,1,0:T(8,128)(2,1)S(1)}, u32[]{:S(2)}, u32[]{:S(2)}) async-start(bf16[8,256,512]{2,1,0:T(8,128)(2,1)} %dynamic-slice_bitcast_fusion), calls=%async_computation.1 | async-start | bytes 4194304 | tf_op jit(solution)/shard_map/all_to_all | solution.py:422
  41.3 30.9 %copy-start.4 = (s32[3]{0:T(128)S(1)}, s32[3]{0:T(128)}, u32[]{:S(2)}) copy-start(s32[3]{0:T(128)} %pad_add_fusion.at_ref) | copy-start | bytes 40
  47.5 9.2 %collective-permute-start.3 = (s16[272,512]{1,0:T(8,128)(2,1)}, s16[272,512]{1,0:T(8,128)(2,1)S(1)}, u32[]{:S(2)}, u32[]{:S(2)}) collective-permute-start(s16[272,512]{1,0:T(8,128)(2,1)} %get-tuple-element.45), channel_id=1, source_target_pairs={{0,1},{1,0},{2,3},{3,2},{4,5},{5,4},{6,7},{7,6},{8,9},{9,8},{10,11... | collective-permute-start | bytes 835592 | tf_op jit(solution)/shard_map/ppermute | solution.py:386
  56.8 1.0 %copy-start.1 = (f32[256,512]{1,0:T(8,128)S(1)}, f32[256,512]{1,0:T(8,128)}, u32[]{:S(2)}) copy-start(f32[256,512]{1,0:T(8,128)} %get-tuple-element.44.own_ref) | copy-start | bytes 1572868
  58.7 26.1 %copy-start.5 = (f32[512]{0:T(512)S(1)}, f32[512]{0:T(512)}, u32[]{:S(2)}) copy-start(f32[512]{0:T(512)} %param.15) | copy-start | bytes 6148
  58.7 29.0 %collective-permute-start.8 = (s16[272,512]{1,0:T(8,128)(2,1)}, s16[272,512]{1,0:T(8,128)(2,1)S(1)}, u32[]{:S(2)}, u32[]{:S(2)}) collective-permute-start(s16[272,512]{1,0:T(8,128)(2,1)} %shard_map.113), channel_id=1, source_target_pairs={{0,16},{2,18},{4,20},{6,22},{8,24},{10,26},{12,28},{14,30},{16,0},... | collective-permute-start | bytes 835592 | tf_op jit(solution)/shard_map/ppermute | solution.py:381
  72.3 6.3 %copy-start.8 = (f32[4,3,512]{2,1,0:T(4,128)S(1)}, f32[4,3,512]{2,1,0:T(4,128)}, u32[]{:S(2)}) copy-start(f32[4,3,512]{2,1,0:T(4,128)} %pad_maximum_fusion.1) | copy-start | bytes 73732
  77.0 10.7 %collective-permute-start.7 = (s16[272,512]{1,0:T(8,128)(2,1)S(1)}, s16[272,512]{1,0:T(8,128)(2,1)S(1)}, u32[]{:S(2)}, u32[]{:S(2)}) collective-permute-start(s16[272,512]{1,0:T(8,128)(2,1)S(1)} %get-tuple-element.51), channel_id=1, source_target_pairs={{0,1},{1,0},{2,3},{3,2},{4,5},{5,4},{6,7},{7,6},{8,9},{9,8},{10,11... | collective-permute-start | bytes 835592 | tf_op jit(solution)/shard_map/ppermute | solution.py:386
  78.5 5.7 %collective-permute-start.6 = (f32[4,3,512]{2,1,0:T(4,128)S(1)}, f32[4,3,512]{2,1,0:T(4,128)S(1)}, u32[]{:S(2)}, u32[]{:S(2)}) collective-permute-start(f32[4,3,512]{2,1,0:T(4,128)S(1)} %copy-done.8), channel_id=1, source_target_pairs={{0,24},{2,26},{4,28},{6,30},{8,16},{10,18},{12,20},{14,22},{16,8},... | collective-permute-start | bytes 73736 | tf_op jit(solution)/shard_map/ppermute | solution.py:41
  78.6 5.7 %collective-permute-start.5 = (f32[4,3,512]{2,1,0:T(4,128)S(1)}, f32[4,3,512]{2,1,0:T(4,128)S(1)}, u32[]{:S(2)}, u32[]{:S(2)}) collective-permute-start(f32[4,3,512]{2,1,0:T(4,128)S(1)} %copy-done.8), channel_id=1, source_target_pairs={{0,16},{2,18},{4,20},{6,22},{8,24},{10,26},{12,28},{14,30},{16,0},... | collective-permute-start | bytes 73736 | tf_op jit(solution)/shard_map/ppermute | solution.py:41
  79.7 5.2 %collective-permute-start.4 = (f32[4,3,512]{2,1,0:T(4,128)S(1)}, f32[4,3,512]{2,1,0:T(4,128)S(1)}, u32[]{:S(2)}, u32[]{:S(2)}) collective-permute-start(f32[4,3,512]{2,1,0:T(4,128)S(1)} %copy-done.8), channel_id=1, source_target_pairs={{0,8},{2,10},{4,12},{6,14},{8,0},{10,2},{12,4},{14,6},{16,24},{18,... | collective-permute-start | bytes 73736 | tf_op jit(solution)/shard_map/ppermute | solution.py:41
  87.7 13.2 %copy-start.6 = (f32[512]{0:T(512)S(1)}, f32[512]{0:T(512)}, u32[]{:S(2)}) copy-start(f32[512]{0:T(512)} %param.14) | copy-start | bytes 6148

commit v2 on v1

--- a/solution.py
+++ b/solution.py
@@ -37,10 +37,9 @@
 def gather_far(near, axis):
     count = lax.axis_size(axis)
     group = near.shape[0]
-    rest = [
+    return [
         lax.ppermute(near, axis, [(i, i ^ (turn * group)) for i in range(count)]) for turn in range(1, count // group)
     ]
-    return jnp.concatenate([near] + rest, 0)
 
 
 def place(me, j, count):
@@ -422,16 +421,18 @@
     near = lax.all_to_all(near, "tm", 0, 0, axis_index_groups=groups, tiled=True)
 
     own, theirs = project(far, basis, first, owners, modes)
+    own, blocks = lax.optimization_barrier((own, blocks))
+    rest = gather_far(blocks, "tm")
     arriving = [send_along(term, "space", turn + 1) for turn, term in enumerate(theirs)]
     coded = jax.ShapeDtypeStruct((steps + PAD, modes), jnp.int16)
     (crossing,) = call(fold_kernel, (own, *arriving), [coded], [], 8 * steps * modes)
-    near, _ = lax.optimization_barrier((near, crossing))
+    rest, near, crossing = lax.optimization_barrier((rest, near, crossing))
     crossing = swap_halves(crossing, "tm")
-    blocks = gather_far(blocks, "tm")
 
     own, theirs = project(near, basis, first, owners, modes, True)
     parts = [send_along(term, "space", turn + 1) for turn, term in enumerate(theirs)] + [crossing]
-    own, chunk_totals, blocks = lax.optimization_barrier((own, chunk_totals, blocks))
+    own, chunk_totals, rest = lax.optimization_barrier((own, chunk_totals, rest))
+    blocks = jnp.concatenate([blocks] + rest, 0)
     parts.insert(0, own)
     *maps, whole, carry, edge, log_variance = call(
         functools.partial(gains_kernel, tm_count),

time: 103 us -> 105 us (1.019)
  waiting for transfers between devices: 40.1 us -> 44.2 us
  starting transfers between devices: 21.5 us -> 19.3 us
  blocking collectives: 11.4 us -> 9.98 us
  local copies, waits for them, and re-layouts: 8.6 us -> 9.85 us
    all_to_all x1, waiting for transfers between devices: 10.9 us -> 0.01 us  [body(): lax.all_to_all(near, 'tm', 0, 0, axis_index_groups=groups, tiled=True)]
    ppermute x3, waiting for transfers between devices: 1.89 us -> 11.5 us  [gather_far(): lax.ppermute(near, axis, [(i, i ^ turn * group) for i in range(count)])]
    ppermute x1, waiting for transfers between devices: 0.01 us -> 8.11 us  [swap_halves(): lax.ppermute(block, axis, [(i, (i + half) % (2 * half)) for i in range(2...]
    ppermute x2, waiting for transfers between devices: 7.62 us -> 5.03 us  [send_along(): lax.ppermute(term, axis, [(i, (i + turn) % count) for i in range(count)])]
    ppermute x1, starting transfers between devices: 2.59 us -> 0.36 us  [swap_halves(): lax.ppermute(block, axis, [(i, (i + half) % (2 * half)) for i in range(2...]
    all_to_all x1, blocking collectives: 11.4 us -> 9.98 us  [body(): ends = lax.all_to_all(ends, 'tm', 0, 0, tiled=True)]
    unnamed x20 -> x26, local copies, waits for them, and re-layouts: 2.38 us -> 3.62 us
  transfers between devices with their start and end apart: 11 -> 11, of which waited for: 6 -> 6; matrix products, arithmetic and copies ran while one was open for 4% -> 5% of each run, Pallas kernels for 15% -> 10%
where the time goes in v2:
time: 105 us
  waiting for transfers between devices  44.2 us (42%)
  starting transfers between devices  19.3 us (18%)
  Pallas kernels  18.3 us (17%)
  blocking collectives  9.98 us (10%)
  local copies, waits for them, and re-layouts  9.85 us (9%)
  other arithmetic  2.09 us (2%)
    ppermute x3, waiting for transfers between devices, rotate(): return lax.ppermute(block, axis, route)  19.6 us
    ppermute x3, waiting for transfers between devices, gather_far(): lax.ppermute(near, axis, [(i, i ^ turn * group) for i in range(count)])  11.5 us
    pallas_call x2, Pallas kernels, project(): pl.pallas_call(functools.partial(project_kernel, held), in_specs=[pl.Bloc...  10.9 us
    all_to_all x1, blocking collectives, body(): ends = lax.all_to_all(ends, 'tm', 0, 0, tiled=True)  9.98 us
    ppermute x1, waiting for transfers between devices, swap_halves(): lax.ppermute(block, axis, [(i, (i + half) % (2 * half)) for i in range(2...  8.11 us
    pallas_call x5, Pallas kernels, call(): pl.pallas_call(kernel, in_specs=[smem if x.dtype == jnp.int32 else vmem f...  7.42 us
    all_to_all x1, starting transfers between devices, body(): far = lax.all_to_all(far, 'tm', 0, 0, axis_index_groups=groups, tiled=True)  5.37 us
    ppermute x2, waiting for transfers between devices, send_along(): lax.ppermute(term, axis, [(i, (i + turn) % count) for i in range(count)])  5.03 us
  transfers between devices with their start and end apart: 11, of which 6 were waited for; matrix products, arithmetic and copies ran while one was open for 5% of the time, Pallas kernels for 10%

profile of v2, /device:TPU:0, one launch (start us, length us, event | category | flops | bytes accessed | tf_op | source)
XLA Modules:
  0.0 104.6 jit_solution(10997501277736625073)
XLA Ops:
  0.7 3.0 %dynamic-slice_bitcast_fusion.1 = bf16[8,256,512]{2,1,0:T(8,128)(2,1)} fusion(bf16[2,8,256,512]{3,2,1,0:T(8,128)(2,1)} %bitcast.27, s32[]{:T(128)S(6)} %select_n.13), kind=kLoop, calls=%fused_computation.1 | loop fusion | bytes 4194308 | tf_op jit(solution)/shard_map/jit(dynamic_index_in_dim)/squeeze | solution.py:411
  3.7 5.4 %all-to-all-start = ((bf16[8,256,512]{2,1,0:T(8,128)(2,1)}), bf16[8,256,512]{2,1,0:T(8,128)(2,1)S(1)}, u32[]{:S(2)}, u32[]{:S(2)}) async-start(bf16[8,256,512]{2,1,0:T(8,128)(2,1)} %dynamic-slice_bitcast_fusion.1), calls=%async_computation | async-start | bytes 4194304 | tf_op jit(solution)/shard_map/all_to_all | solution.py:413
  9.2 0.9 shard_map.111
  10.1 1.8 %collective-permute-start.2 = (f32[3,512]{1,0:T(4,128)S(1)}, f32[3,512]{1,0:T(4,128)S(1)}, u32[]{:S(2)}, u32[]{:S(2)}) collective-permute-start(f32[3,512]{1,0:T(4,128)S(1)} %get-tuple-element.49), channel_id=1, source_target_pairs={{0,6},{2,0},{4,2},{6,4},{8,14},{10,8},{12,10},{14,12},{16,22},{18,... | collective-permute-start | bytes 18440 | tf_op jit(solution)/shard_map/ppermute | solution.py:21
  12.5 3.1 %dynamic-slice_bitcast_fusion = bf16[8,256,512]{2,1,0:T(8,128)(2,1)} fusion(bf16[2,8,256,512]{3,2,1,0:T(8,128)(2,1)} %bitcast.28, s32[]{:T(128)S(6)} %select_n.14), kind=kLoop, calls=%fused_computation | loop fusion | bytes 4194308 | tf_op jit(solution)/shard_map/jit(dynamic_index_in_dim)/squeeze | solution.py:418
  15.5 17.4 %collective-permute-done.2 = f32[3,512]{1,0:T(4,128)S(1)} collective-permute-done((f32[3,512]{1,0:T(4,128)S(1)}, f32[3,512]{1,0:T(4,128)S(1)}, u32[]{:S(2)}, u32[]{:S(2)}) %collective-permute-start.2) | collective-permute-done | bytes 6176 | tf_op jit(solution)/shard_map/ppermute | solution.py:21
  32.9 2.2 %collective-permute-done.1 = f32[3,512]{1,0:T(4,128)S(1)} collective-permute-done((f32[3,512]{1,0:T(4,128)S(1)}, f32[3,512]{1,0:T(4,128)S(1)}, u32[]{:S(2)}, u32[]{:S(2)}) %collective-permute-start.1) | collective-permute-done | bytes 6176 | tf_op jit(solution)/shard_map/ppermute | solution.py:21
  35.8 1.3 %copy-done.7 = bf16[8,256,512]{2,1,0:T(8,128)(2,1)} copy-done((bf16[8,256,512]{2,1,0:T(8,128)(2,1)}, bf16[8,256,512]{2,1,0:T(8,128)(2,1)S(1)}, u32[]{:S(2)}) %copy-start.7) | copy-done | bytes 2097176
  37.1 3.6 %all-to-all-start.1 = ((bf16[8,256,512]{2,1,0:T(8,128)(2,1)}), bf16[8,256,512]{2,1,0:T(8,128)(2,1)S(1)}, u32[]{:S(2)}, u32[]{:S(2)}) async-start(bf16[8,256,512]{2,1,0:T(8,128)(2,1)} %dynamic-slice_bitcast_fusion), calls=%async_computation.1 | async-start | bytes 4194304 | tf_op jit(solution)/shard_map/all_to_all | solution.py:421
  41.3 6.2 %shard_map.112 = (f32[256,512]{1,0:T(8,128)}, s16[272,512]{1,0:T(8,128)(2,1)}) custom-call(s32[3]{0:T(128)} %pad_add_fusion.at_ref, bf16[8,256,512]{2,1,0:T(8,128)(2,1)} %copy-done.7, bf16[16,512,1024]{2,1,0:T(8,128)(2,1)} %bitcast.25), custom_call_target="tpu_custom_call" | custom-call | flops 2147483648 | bytes 11010048 | tf_op jit(solution)/shard_map/pallas_call | solution.py:330
  47.5 1.6 %collective-permute-start.6 = (s16[272,512]{1,0:T(8,128)(2,1)}, s16[272,512]{1,0:T(8,128)(2,1)S(1)}, u32[]{:S(2)}, u32[]{:S(2)}) collective-permute-start(s16[272,512]{1,0:T(8,128)(2,1)} %get-tuple-element.56), channel_id=1, source_target_pairs={{0,1},{1,0},{2,3},{3,2},{4,5},{5,4},{6,7},{7,6},{8,9},{9,8},{10,11... | collective-permute-start | bytes 835592 | tf_op jit(solution)/shard_map/ppermute | solution.py:385
  49.1 3.9 %collective-permute-start.5 = (f32[4,3,512]{2,1,0:T(4,128)}, f32[4,3,512]{2,1,0:T(4,128)S(1)}, u32[]{:S(2)}, u32[]{:S(2)}) collective-permute-start(f32[4,3,512]{2,1,0:T(4,128)} %pad_maximum_fusion.1), channel_id=1, source_target_pairs={{0,24},{2,26},{4,28},{6,30},{8,16},{10,18},{12,20},{14,22},{16,8},... | collective-permute-start | bytes 73736 | tf_op jit(solution)/shard_map/ppermute | solution.py:41
  53.6 3.1 %collective-permute-done.6.refs_0_ = s16[272,512]{1,0:T(8,128)(2,1)S(1)} collective-permute-done((s16[272,512]{1,0:T(8,128)(2,1)}, s16[272,512]{1,0:T(8,128)(2,1)S(1)}, u32[]{:S(2)}, u32[]{:S(2)}) %collective-permute-start.6) | collective-permute-done | bytes 278560 | tf_op jit(solution)/shard_map/ppermute | solution.py:385
  56.8 1.0 copy-done.1
  58.0 11.5 %collective-permute-done.5 = f32[4,3,512]{2,1,0:T(4,128)S(1)} collective-permute-done((f32[4,3,512]{2,1,0:T(4,128)}, f32[4,3,512]{2,1,0:T(4,128)S(1)}, u32[]{:S(2)}, u32[]{:S(2)}) %collective-permute-start.5) | collective-permute-done | bytes 24608 | tf_op jit(solution)/shard_map/ppermute | solution.py:41
  70.8 4.7 %shard_map.114 = (f32[256,512]{1,0:T(8,128)S(1)}, s16[272,512]{1,0:T(8,128)(2,1)S(1)}) custom-call(s32[3]{0:T(128)S(1)} %copy-done.4, bf16[8,256,512]{2,1,0:T(8,128)(2,1)S(1)} %all-to-all-done.1.slab_ref, bf16[16,512,1024]{2,1,0:T(8,128)(2,1)} %bitcast.26), custom_call_target="tpu_custom_call" | custom-call | flops 2147483648 | bytes 11010048 | tf_op jit(solution)/shard_map/pallas_call | solution.py:330
  75.5 1.6 %collective-permute-start.7 = (s16[272,512]{1,0:T(8,128)(2,1)S(1)}, s16[272,512]{1,0:T(8,128)(2,1)S(1)}, u32[]{:S(2)}, u32[]{:S(2)}) collective-permute-start(s16[272,512]{1,0:T(8,128)(2,1)S(1)} %get-tuple-element.64), channel_id=1, source_target_pairs={{0,1},{1,0},{2,3},{3,2},{4,5},{5,4},{6,7},{7,6},{8,9},{9,8},{10,11... | collective-permute-start | bytes 835592 | tf_op jit(solution)/shard_map/ppermute | solution.py:385
  77.4 0.8 pad_maximum_fusion.blocks_ref
  78.2 2.8 %shard_map.115 = (f32[16,16,512]{2,1,0:T(8,128)S(1)}, f32[16,16,512]{2,1,0:T(8,128)S(1)}, f32[16,16,512]{2,1,0:T(8,128)S(1)}, f32[16,16,512]{2,1,0:T(8,128)S(1)}...) custom-call(s32[1]{0:T(128)} %bitcast.6.me_ref, ...), custom_call_target="tpu_custom_call" | custom-call | flops 10485760 | bytes 6625284 | tf_op jit(solution)/shard_map/pallas_call | solution.py:367
  81.1 1.9 %collective-permute-done.7.refs_1_ = s16[272,512]{1,0:T(8,128)(2,1)S(1)} collective-permute-done((s16[272,512]{1,0:T(8,128)(2,1)S(1)}, s16[272,512]{1,0:T(8,128)(2,1)S(1)}, u32[]{:S(2)}, u32[]{:S(2)}) %collective-permute-start.7) | collective-permute-done | bytes 278560 | tf_op jit(solution)/shard_map/ppermute | solution.py:385
  83.0 8.1 %collective-permute-done.8.refs_2_ = s16[272,512]{1,0:T(8,128)(2,1)S(1)} collective-permute-done((s16[272,512]{1,0:T(8,128)(2,1)S(1)}, s16[272,512]{1,0:T(8,128)(2,1)S(1)}, u32[]{:S(2)}, u32[]{:S(2)}) %collective-permute-start.8) | collective-permute-done | bytes 278560 | tf_op jit(solution)/shard_map/ppermute | solution.py:380
  91.1 1.9 %shard_map.116 = (f32[256,512]{1,0:T(8,128)}, f32[16,16,512]{2,1,0:T(8,128)S(1)}, f32[16,16,512]{2,1,0:T(8,128)S(1)}, f32[2,512]{1,0:T(2,128)S(1)}) custom-call(f32[256,512]{1,0:T(8,128)S(1)} %get-tuple-element.63.refs_0_, s16[272,512]{1,0:T(8,128)(2,1)S(1)} %collective-permute-done.7.refs_1_, s16[272,512]{1,0:T(8,128)(2,1)S(1)} %collective-permute-done.8.refs_2_, ...), custom_call_target="tpu_custom_call" | custom-call | flops 1572864 | bytes 6426624 | tf_op jit(solution)/shard_map/pallas_call | solution.py:367
  93.0 10.0 %all_to_all.15.blocks_ref = f32[16,2,512]{2,1,0:T(2,128)S(1)} all-to-all(f32[16,2,512]{2,1,0:T(2,128)S(1)} %broadcast_in_dim.29), channel_id=1, replica_groups=mesh['tm'=16,'space'=2] {'tm'}, dimensions={0} | all-to-all | bytes 131072 | tf_op jit(solution)/shard_map/all_to_all | solution.py:453
  102.9 1.6 %shard_map.117 = (f32[256,512]{1,0:T(8,128)}, f32[256,512]{1,0:T(8,128)}) custom-call(s32[1]{0:T(128)} %bitcast.6.me_ref, f32[1,512]{1,0:T(1,128)S(1)} %bitcast.24, f32[3,16,16,512]{3,2,1,0:T(8,128)S(1)} %get-tuple-element.78.whole_ref, f32[2,16,512]{2,1,0:T(8,128)S(1)} %get-tuple-element.79.edge_ref, f32[16,2,512]{2,1,0:T(2,128)S(1)} %all_to_all.15.blocks_ref, ...), custom_call_target="tpu_custom_call" | custom-call | flops 1048576 | bytes 3803140 | tf_op jit(solution)/shard_map/pallas_call | solution.py:367
  (40 shorter events, 4.3 us)
Async XLA Ops:
  3.7 5.4 %copy-start.12 = (s32[256]{0:T(256)S(1)}, s32[256]{0:T(256)}, u32[]{:S(2)}) copy-start(s32[256]{0:T(256)} %param.11) | copy-start | bytes 3076
  3.7 5.5 %copy-start = (f32[256,512]{1,0:T(8,128)S(1)}, f32[256,512]{1,0:T(8,128)}, u32[]{:S(2)}) copy-start(f32[256,512]{1,0:T(8,128)} %decay_in.3) | copy-start | bytes 1572868
  3.7 5.5 %copy-start.2 = (f32[512]{0:T(512)S(1)}, f32[512]{0:T(512)}, u32[]{:S(2)}) copy-start(f32[512]{0:T(512)} %param.12) | copy-start | bytes 6148
  3.7 5.5 %copy-start.3 = (f32[512]{0:T(512)S(1)}, f32[512]{0:T(512)}, u32[]{:S(2)}) copy-start(f32[512]{0:T(512)} %param.13) | copy-start | bytes 6148
  3.7 32.0 %all-to-all-start = ((bf16[8,256,512]{2,1,0:T(8,128)(2,1)}), bf16[8,256,512]{2,1,0:T(8,128)(2,1)S(1)}, u32[]{:S(2)}, u32[]{:S(2)}) async-start(bf16[8,256,512]{2,1,0:T(8,128)(2,1)} %dynamic-slice_bitcast_fusion.1), calls=%async_computation | async-start | bytes 4194304 | tf_op jit(solution)/shard_map/all_to_all | solution.py:413
  10.1 22.8 %collective-permute-start.2 = (f32[3,512]{1,0:T(4,128)S(1)}, f32[3,512]{1,0:T(4,128)S(1)}, u32[]{:S(2)}, u32[]{:S(2)}) collective-permute-start(f32[3,512]{1,0:T(4,128)S(1)} %get-tuple-element.49), channel_id=1, source_target_pairs={{0,6},{2,0},{4,2},{6,4},{8,14},{10,8},{12,10},{14,12},{16,22},{18,... | collective-permute-start | bytes 18440 | tf_op jit(solution)/shard_map/ppermute | solution.py:21
  11.9 23.2 %collective-permute-start.1 = (f32[3,512]{1,0:T(4,128)S(1)}, f32[3,512]{1,0:T(4,128)S(1)}, u32[]{:S(2)}, u32[]{:S(2)}) collective-permute-start(f32[3,512]{1,0:T(4,128)S(1)} %get-tuple-element.49), channel_id=1, source_target_pairs={{0,4},{2,6},{4,0},{6,2},{8,12},{10,14},{12,8},{14,10},{16,20},{18,... | collective-permute-start | bytes 18440 | tf_op jit(solution)/shard_map/ppermute | solution.py:21
  12.3 22.8 %collective-permute-start = (f32[3,512]{1,0:T(4,128)S(1)}, f32[3,512]{1,0:T(4,128)S(1)}, u32[]{:S(2)}, u32[]{:S(2)}) collective-permute-start(f32[3,512]{1,0:T(4,128)S(1)} %get-tuple-element.49), channel_id=1, source_target_pairs={{0,2},{2,4},{4,6},{6,0},{8,10},{10,12},{12,14},{14,8},{16,18},{18,... | collective-permute-start | bytes 18440 | tf_op jit(solution)/shard_map/ppermute | solution.py:21
  35.8 1.3 %copy-start.7 = (bf16[8,256,512]{2,1,0:T(8,128)(2,1)}, bf16[8,256,512]{2,1,0:T(8,128)(2,1)S(1)}, u32[]{:S(2)}) copy-start(bf16[8,256,512]{2,1,0:T(8,128)(2,1)S(1)} %all-to-all-done.slab_ref) | copy-start | bytes 6291460
  37.1 33.7 %all-to-all-start.1 = ((bf16[8,256,512]{2,1,0:T(8,128)(2,1)}), bf16[8,256,512]{2,1,0:T(8,128)(2,1)S(1)}, u32[]{:S(2)}, u32[]{:S(2)}) async-start(bf16[8,256,512]{2,1,0:T(8,128)(2,1)} %dynamic-slice_bitcast_fusion), calls=%async_computation.1 | async-start | bytes 4194304 | tf_op jit(solution)/shard_map/all_to_all | solution.py:421
  41.3 29.4 %copy-start.4 = (s32[3]{0:T(128)S(1)}, s32[3]{0:T(128)}, u32[]{:S(2)}) copy-start(s32[3]{0:T(128)} %pad_add_fusion.at_ref) | copy-start | bytes 40
  47.5 9.2 %collective-permute-start.6 = (s16[272,512]{1,0:T(8,128)(2,1)}, s16[272,512]{1,0:T(8,128)(2,1)S(1)}, u32[]{:S(2)}, u32[]{:S(2)}) collective-permute-start(s16[272,512]{1,0:T(8,128)(2,1)} %get-tuple-element.56), channel_id=1, source_target_pairs={{0,1},{1,0},{2,3},{3,2},{4,5},{5,4},{6,7},{7,6},{8,9},{9,8},{10,11... | collective-permute-start | bytes 835592 | tf_op jit(solution)/shard_map/ppermute | solution.py:385
  49.1 20.3 %collective-permute-start.5 = (f32[4,3,512]{2,1,0:T(4,128)}, f32[4,3,512]{2,1,0:T(4,128)S(1)}, u32[]{:S(2)}, u32[]{:S(2)}) collective-permute-start(f32[4,3,512]{2,1,0:T(4,128)} %pad_maximum_fusion.1), channel_id=1, source_target_pairs={{0,24},{2,26},{4,28},{6,30},{8,16},{10,18},{12,20},{14,22},{16,8},... | collective-permute-start | bytes 73736 | tf_op jit(solution)/shard_map/ppermute | solution.py:41
  53.1 16.4 %collective-permute-start.4 = (f32[4,3,512]{2,1,0:T(4,128)}, f32[4,3,512]{2,1,0:T(4,128)S(1)}, u32[]{:S(2)}, u32[]{:S(2)}) collective-permute-start(f32[4,3,512]{2,1,0:T(4,128)} %pad_maximum_fusion.1), channel_id=1, source_target_pairs={{0,16},{2,18},{4,20},{6,22},{8,24},{10,26},{12,28},{14,30},{16,0},... | collective-permute-start | bytes 73736 | tf_op jit(solution)/shard_map/ppermute | solution.py:41
  53.1 17.7 %collective-permute-start.3 = (f32[4,3,512]{2,1,0:T(4,128)}, f32[4,3,512]{2,1,0:T(4,128)}, u32[]{:S(2)}, u32[]{:S(2)}) collective-permute-start(f32[4,3,512]{2,1,0:T(4,128)} %pad_maximum_fusion.1), channel_id=1, source_target_pairs={{0,8},{2,10},{4,12},{6,14},{8,0},{10,2},{12,4},{14,6},{16,24},{18,... | collective-permute-start | bytes 73736 | tf_op jit(solution)/shard_map/ppermute | solution.py:41
  56.8 1.0 copy-start.1
  58.0 20.2 %copy-start.5 = (f32[512]{0:T(512)S(1)}, f32[512]{0:T(512)}, u32[]{:S(2)}) copy-start(f32[512]{0:T(512)} %param.15) | copy-start | bytes 6148
  69.5 0.6 copy-start.8
  70.1 0.6 copy-start.10
  70.7 6.7 %copy-start.9 = (f32[4,3,512]{2,1,0:T(4,128)S(1)}, f32[4,3,512]{2,1,0:T(4,128)}, u32[]{:S(2)}) copy-start(f32[4,3,512]{2,1,0:T(4,128)} %copy-done.8) | copy-start | bytes 73732
  70.7 6.7 %copy-start.11 = (f32[4,3,512]{2,1,0:T(4,128)S(1)}, f32[4,3,512]{2,1,0:T(4,128)}, u32[]{:S(2)}) copy-start(f32[4,3,512]{2,1,0:T(4,128)} %copy-done.10) | copy-start | bytes 73732
  75.5 7.5 %collective-permute-start.7 = (s16[272,512]{1,0:T(8,128)(2,1)S(1)}, s16[272,512]{1,0:T(8,128)(2,1)S(1)}, u32[]{:S(2)}, u32[]{:S(2)}) collective-permute-start(s16[272,512]{1,0:T(8,128)(2,1)S(1)} %get-tuple-element.64), channel_id=1, source_target_pairs={{0,1},{1,0},{2,3},{3,2},{4,5},{5,4},{6,7},{7,6},{8,9},{9,8},{10,11... | collective-permute-start | bytes 835592 | tf_op jit(solution)/shard_map/ppermute | solution.py:385
  77.0 14.0 %collective-permute-start.8 = (s16[272,512]{1,0:T(8,128)(2,1)S(1)}, s16[272,512]{1,0:T(8,128)(2,1)S(1)}, u32[]{:S(2)}, u32[]{:S(2)}) collective-permute-start(s16[272,512]{1,0:T(8,128)(2,1)S(1)} %shard_map.113), channel_id=1, source_target_pairs={{0,16},{2,18},{4,20},{6,22},{8,24},{10,26},{12,28},{14,30},{16,0},... | collective-permute-start | bytes 835592 | tf_op jit(solution)/shard_map/ppermute | solution.py:380
  91.1 11.9 %copy-start.6 = (f32[512]{0:T(512)S(1)}, f32[512]{0:T(512)}, u32[]{:S(2)}) copy-start(f32[512]{0:T(512)} %param.14) | copy-start | bytes 6148

commit v3 on v2

--- a/solution.py
+++ b/solution.py
@@ -12,6 +12,7 @@
 PAD = 16
 STEPS16 = 32512.0
 TINY = 1e-30
+EARLY = 1 << 34
 F32 = jnp.float32
 LIMIT = 16 * 1024 * 1024
 
@@ -353,6 +354,10 @@
     return own, coded
 
 
+def add_kernel(own_ref, coded_ref, out_ref):
+    out_ref[...] = own_ref[...] + decode(coded_ref)
+
+
 def fold_kernel(own_ref, *refs):
     total = own_ref[...]
     for ref in refs[:-1]:
@@ -421,18 +426,18 @@
     near = lax.all_to_all(near, "tm", 0, 0, axis_index_groups=groups, tiled=True)
 
     own, theirs = project(far, basis, first, owners, modes)
-    own, blocks = lax.optimization_barrier((own, blocks))
-    rest = gather_far(blocks, "tm")
     arriving = [send_along(term, "space", turn + 1) for turn, term in enumerate(theirs)]
     coded = jax.ShapeDtypeStruct((steps + PAD, modes), jnp.int16)
     (crossing,) = call(fold_kernel, (own, *arriving), [coded], [], 8 * steps * modes)
-    rest, near, crossing = lax.optimization_barrier((rest, near, crossing))
+    near, crossing = lax.optimization_barrier((near, crossing))
     crossing = swap_halves(crossing, "tm")
+    rest = gather_far(blocks, "tm")
 
     own, theirs = project(near, basis, first, owners, modes, True)
-    parts = [send_along(term, "space", turn + 1) for turn, term in enumerate(theirs)] + [crossing]
+    parts = [send_along(term, "space", turn + 1) for turn, term in enumerate(theirs)]
     own, chunk_totals, rest = lax.optimization_barrier((own, chunk_totals, rest))
     blocks = jnp.concatenate([blocks] + rest, 0)
+    (own,) = call(add_kernel, (own, crossing), [shape((steps, modes))], [], EARLY)
     parts.insert(0, own)
     *maps, whole, carry, edge, log_variance = call(
         functools.partial(gains_kernel, tm_count),

time: 105 us -> 97.8 us (0.931)
  waiting for transfers between devices: 44.2 us -> 34.8 us
  blocking collectives: 9.98 us -> 11.8 us
  starting transfers between devices: 19.3 us -> 21 us
  local copies, waits for them, and re-layouts: 9.85 us -> 8.56 us
    ppermute x3, waiting for transfers between devices: 11.5 us -> 0.01 us  [gather_far(): lax.ppermute(near, axis, [(i, i ^ turn * group) for i in range(count)])]
    all_to_all x1, waiting for transfers between devices: 0.01 us -> 9.36 us  [body(): lax.all_to_all(near, 'tm', 0, 0, axis_index_groups=groups, tiled=True)]
    ppermute x1, waiting for transfers between devices: 8.11 us -> 2.72 us  [swap_halves(): lax.ppermute(block, axis, [(i, (i + half) % (2 * half)) for i in range(2...]
    ppermute x2, waiting for transfers between devices: 5.03 us -> 3.13 us  [send_along(): lax.ppermute(term, axis, [(i, (i + turn) % count) for i in range(count)])]
    all_to_all x1, blocking collectives: 9.98 us -> 11.8 us  [body(): ends = lax.all_to_all(ends, 'tm', 0, 0, tiled=True)]
    ppermute x1, starting transfers between devices: 0.36 us -> 2.01 us  [swap_halves(): lax.ppermute(block, axis, [(i, (i + half) % (2 * half)) for i in range(2...]
    unnamed x26 -> x18, local copies, waits for them, and re-layouts: 3.62 us -> 2.37 us
    pallas_call x5 -> x6, Pallas kernels: 7.42 us -> 7.32 us  [call(): pl.pallas_call(kernel, in_specs=[smem if x.dtype == jnp.int32 else vmem f...]
  transfers between devices with their start and end apart: 11 -> 11, of which waited for: 6 -> 5; matrix products, arithmetic and copies ran while one was open for 5% -> 5% of each run, Pallas kernels for 10% -> 15%
where the time goes in v3:
time: 97.8 us; the launch traced here: 97.3 us
  waiting for transfers between devices  34.8 us (36%)
  starting transfers between devices  21 us (21%)
  Pallas kernels  18.2 us (19%)
  blocking collectives  11.8 us (12%)
  local copies, waits for them, and re-layouts  8.56 us (9%)
  other arithmetic  2.07 us (2%)
    ppermute x3, waiting for transfers between devices, rotate(): return lax.ppermute(block, axis, route)  19.6 us
    all_to_all x1, blocking collectives, body(): ends = lax.all_to_all(ends, 'tm', 0, 0, tiled=True)  11.8 us
    pallas_call x2, Pallas kernels, project(): pl.pallas_call(functools.partial(project_kernel, held), in_specs=[pl.Bloc...  10.9 us
    all_to_all x1, waiting for transfers between devices, body(): lax.all_to_all(near, 'tm', 0, 0, axis_index_groups=groups, tiled=True)  9.36 us
    pallas_call x6, Pallas kernels, call(): pl.pallas_call(kernel, in_specs=[smem if x.dtype == jnp.int32 else vmem f...  7.32 us
    all_to_all x1, starting transfers between devices, body(): far = lax.all_to_all(far, 'tm', 0, 0, axis_index_groups=groups, tiled=True)  5.37 us
    ppermute x3, starting transfers between devices, gather_far(): lax.ppermute(near, axis, [(i, i ^ turn * group) for i in range(count)])  4.49 us
    all_to_all x1, starting transfers between devices, body(): lax.all_to_all(near, 'tm', 0, 0, axis_index_groups=groups, tiled=True)  3.6 us
  transfers between devices with their start and end apart: 11, of which 5 were waited for; matrix products, arithmetic and copies ran while one was open for 5% of the time, Pallas kernels for 15%

profile of v3, /device:TPU:0, one launch (start us, length us, event | category | flops | bytes accessed | tf_op | source)
XLA Modules:
  0.0 97.3 jit_solution(4090772107325404827)
XLA Ops:
  0.7 3.0 %dynamic-slice_bitcast_fusion.1 = bf16[8,256,512]{2,1,0:T(8,128)(2,1)} fusion(bf16[2,8,256,512]{3,2,1,0:T(8,128)(2,1)} %bitcast.27, s32[]{:T(128)S(6)} %select_n.13), kind=kLoop, calls=%fused_computation.1 | loop fusion | bytes 4194308 | tf_op jit(solution)/shard_map/jit(dynamic_index_in_dim)/squeeze | solution.py:416
  3.7 5.4 %all-to-all-start = ((bf16[8,256,512]{2,1,0:T(8,128)(2,1)}), bf16[8,256,512]{2,1,0:T(8,128)(2,1)S(1)}, u32[]{:S(2)}, u32[]{:S(2)}) async-start(bf16[8,256,512]{2,1,0:T(8,128)(2,1)} %dynamic-slice_bitcast_fusion.1), calls=%async_computation | async-start | bytes 4194304 | tf_op jit(solution)/shard_map/all_to_all | solution.py:418
  9.2 0.9 shard_map.111
  10.1 1.8 %collective-permute-start.2 = (f32[3,512]{1,0:T(4,128)S(1)}, f32[3,512]{1,0:T(4,128)S(1)}, u32[]{:S(2)}, u32[]{:S(2)}) collective-permute-start(f32[3,512]{1,0:T(4,128)S(1)} %get-tuple-element.44), channel_id=1, source_target_pairs={{0,6},{2,0},{4,2},{6,4},{8,14},{10,8},{12,10},{14,12},{16,22},{18,... | collective-permute-start | bytes 18440 | tf_op jit(solution)/shard_map/ppermute | solution.py:22
  12.4 3.1 %dynamic-slice_bitcast_fusion = bf16[8,256,512]{2,1,0:T(8,128)(2,1)} fusion(bf16[2,8,256,512]{3,2,1,0:T(8,128)(2,1)} %bitcast.28, s32[]{:T(128)S(6)} %select_n.14), kind=kLoop, calls=%fused_computation | loop fusion | bytes 4194308 | tf_op jit(solution)/shard_map/jit(dynamic_index_in_dim)/squeeze | solution.py:423
  15.5 17.4 %collective-permute-done.2 = f32[3,512]{1,0:T(4,128)S(1)} collective-permute-done((f32[3,512]{1,0:T(4,128)S(1)}, f32[3,512]{1,0:T(4,128)S(1)}, u32[]{:S(2)}, u32[]{:S(2)}) %collective-permute-start.2) | collective-permute-done | bytes 6176 | tf_op jit(solution)/shard_map/ppermute | solution.py:22
  32.9 2.2 %collective-permute-done.1 = f32[3,512]{1,0:T(4,128)S(1)} collective-permute-done((f32[3,512]{1,0:T(4,128)S(1)}, f32[3,512]{1,0:T(4,128)S(1)}, u32[]{:S(2)}, u32[]{:S(2)}) %collective-permute-start.1) | collective-permute-done | bytes 6176 | tf_op jit(solution)/shard_map/ppermute | solution.py:22
  35.7 1.3 %copy-done.7 = bf16[8,256,512]{2,1,0:T(8,128)(2,1)} copy-done((bf16[8,256,512]{2,1,0:T(8,128)(2,1)}, bf16[8,256,512]{2,1,0:T(8,128)(2,1)S(1)}, u32[]{:S(2)}) %copy-start.7) | copy-done | bytes 2097176
  37.0 3.6 %all-to-all-start.1 = ((bf16[8,256,512]{2,1,0:T(8,128)(2,1)}), bf16[8,256,512]{2,1,0:T(8,128)(2,1)S(1)}, u32[]{:S(2)}, u32[]{:S(2)}) async-start(bf16[8,256,512]{2,1,0:T(8,128)(2,1)} %dynamic-slice_bitcast_fusion), calls=%async_computation.1 | async-start | bytes 4194304 | tf_op jit(solution)/shard_map/all_to_all | solution.py:426
  41.3 6.2 %shard_map.112 = (f32[256,512]{1,0:T(8,128)}, s16[272,512]{1,0:T(8,128)(2,1)}) custom-call(s32[3]{0:T(128)} %pad_add_fusion.at_ref, bf16[8,256,512]{2,1,0:T(8,128)(2,1)} %copy-done.7, bf16[16,512,1024]{2,1,0:T(8,128)(2,1)} %bitcast.25), custom_call_target="tpu_custom_call" | custom-call | flops 2147483648 | bytes 11010048 | tf_op jit(solution)/shard_map/pallas_call | solution.py:331
  47.5 1.6 %collective-permute-start.3 = (s16[272,512]{1,0:T(8,128)(2,1)}, s16[272,512]{1,0:T(8,128)(2,1)S(1)}, u32[]{:S(2)}, u32[]{:S(2)}) collective-permute-start(s16[272,512]{1,0:T(8,128)(2,1)} %get-tuple-element.48), channel_id=1, source_target_pairs={{0,1},{1,0},{2,3},{3,2},{4,5},{5,4},{6,7},{7,6},{8,9},{9,8},{10,11... | collective-permute-start | bytes 835592 | tf_op jit(solution)/shard_map/ppermute | solution.py:390
  49.1 3.9 %collective-permute-start.6 = (f32[4,3,512]{2,1,0:T(4,128)}, f32[4,3,512]{2,1,0:T(4,128)}, u32[]{:S(2)}, u32[]{:S(2)}) collective-permute-start(f32[4,3,512]{2,1,0:T(4,128)} %pad_maximum_fusion.1), channel_id=1, source_target_pairs={{0,24},{2,26},{4,28},{6,30},{8,16},{10,18},{12,20},{14,22},{16,8},... | collective-permute-start | bytes 73736 | tf_op jit(solution)/shard_map/ppermute | solution.py:42
  53.6 3.1 %collective-permute-done.3.refs_0_ = s16[272,512]{1,0:T(8,128)(2,1)S(1)} collective-permute-done((s16[272,512]{1,0:T(8,128)(2,1)}, s16[272,512]{1,0:T(8,128)(2,1)S(1)}, u32[]{:S(2)}, u32[]{:S(2)}) %collective-permute-start.3) | collective-permute-done | bytes 278560 | tf_op jit(solution)/shard_map/ppermute | solution.py:390
  56.7 1.0 %copy-done.1 = f32[256,512]{1,0:T(8,128)S(1)} copy-done((f32[256,512]{1,0:T(8,128)S(1)}, f32[256,512]{1,0:T(8,128)}, u32[]{:S(2)}) %copy-start.1) | copy-done | bytes 524312
  58.0 9.4 %all-to-all-done.1.slab_ref = bf16[8,256,512]{2,1,0:T(8,128)(2,1)S(1)} async-done(((bf16[8,256,512]{2,1,0:T(8,128)(2,1)}), bf16[8,256,512]{2,1,0:T(8,128)(2,1)S(1)}, u32[]{:S(2)}, u32[]{:S(2)}) %all-to-all-start.1) | async-done | bytes 2097184 | tf_op jit(solution)/shard_map/all_to_all | solution.py:426
  67.3 2.0 %collective-permute-start.7 = (s16[272,512]{1,0:T(8,128)(2,1)S(1)}, s16[272,512]{1,0:T(8,128)(2,1)S(1)}, u32[]{:S(2)}, u32[]{:S(2)}) collective-permute-start(s16[272,512]{1,0:T(8,128)(2,1)S(1)} %shard_map.113), channel_id=1, source_target_pairs={{0,16},{2,18},{4,20},{6,22},{8,24},{10,26},{12,28},{14,30},{16,0},... | collective-permute-start | bytes 835592 | tf_op jit(solution)/shard_map/ppermute | solution.py:385
  69.3 4.7 %shard_map.114 = (f32[256,512]{1,0:T(8,128)S(1)}, s16[272,512]{1,0:T(8,128)(2,1)S(1)}) custom-call(s32[3]{0:T(128)S(1)} %copy-done.4, bf16[8,256,512]{2,1,0:T(8,128)(2,1)S(1)} %all-to-all-done.1.slab_ref, bf16[16,512,1024]{2,1,0:T(8,128)(2,1)} %bitcast.26), custom_call_target="tpu_custom_call" | custom-call | flops 2147483648 | bytes 11010048 | tf_op jit(solution)/shard_map/pallas_call | solution.py:331
  74.1 1.6 %collective-permute-start.8 = (s16[272,512]{1,0:T(8,128)(2,1)S(1)}, s16[272,512]{1,0:T(8,128)(2,1)S(1)}, u32[]{:S(2)}, u32[]{:S(2)}) collective-permute-start(s16[272,512]{1,0:T(8,128)(2,1)S(1)} %get-tuple-element.55), channel_id=1, source_target_pairs={{0,1},{1,0},{2,3},{3,2},{4,5},{5,4},{6,7},{7,6},{8,9},{9,8},{10,11... | collective-permute-start | bytes 835592 | tf_op jit(solution)/shard_map/ppermute | solution.py:390
  75.6 0.8 pad_maximum_fusion.blocks_ref
  76.5 2.8 %shard_map.116 = (f32[16,16,512]{2,1,0:T(8,128)S(1)}, f32[16,16,512]{2,1,0:T(8,128)S(1)}, f32[16,16,512]{2,1,0:T(8,128)S(1)}, f32[16,16,512]{2,1,0:T(8,128)S(1)}...) custom-call(s32[1]{0:T(128)} %bitcast.6.me_ref, ...), custom_call_target="tpu_custom_call" | custom-call | flops 10485760 | bytes 6625284 | tf_op jit(solution)/shard_map/pallas_call | solution.py:372
  79.3 2.7 %collective-permute-done.7.coded_ref = s16[272,512]{1,0:T(8,128)(2,1)S(1)} collective-permute-done((s16[272,512]{1,0:T(8,128)(2,1)S(1)}, s16[272,512]{1,0:T(8,128)(2,1)S(1)}, u32[]{:S(2)}, u32[]{:S(2)}) %collective-permute-start.7) | collective-permute-done | bytes 278560 | tf_op jit(solution)/shard_map/ppermute | solution.py:385
  82.1 1.7 %shard_map.117 = (f32[256,512]{1,0:T(8,128)}, f32[16,16,512]{2,1,0:T(8,128)S(1)}, f32[16,16,512]{2,1,0:T(8,128)S(1)}, f32[2,512]{1,0:T(2,128)S(1)}) custom-call(f32[256,512]{1,0:T(8,128)S(1)} %shard_map.115.refs_0_, s16[272,512]{1,0:T(8,128)(2,1)S(1)} %collective-permute-done.8.refs_1_, f32[16,16,512]{2,1,0:T(8,128)S(1)} %get-tuple-element.60.refs_2_, ...), custom_call_target="tpu_custom_call" | custom-call | flops 1572864 | bytes 5869568 | tf_op jit(solution)/shard_map/pallas_call | solution.py:372
  83.9 11.8 %all_to_all.15.blocks_ref = f32[16,2,512]{2,1,0:T(2,128)S(1)} all-to-all(f32[16,2,512]{2,1,0:T(2,128)S(1)} %broadcast_in_dim.29), channel_id=1, replica_groups=mesh['tm'=16,'space'=2] {'tm'}, dimensions={0} | all-to-all | bytes 131072 | tf_op jit(solution)/shard_map/all_to_all | solution.py:458
  95.6 1.6 %shard_map.118 = (f32[256,512]{1,0:T(8,128)}, f32[256,512]{1,0:T(8,128)}) custom-call(s32[1]{0:T(128)} %bitcast.6.me_ref, f32[1,512]{1,0:T(1,128)S(1)} %bitcast.24, f32[3,16,16,512]{3,2,1,0:T(8,128)S(1)} %get-tuple-element.68.whole_ref, f32[2,16,512]{2,1,0:T(8,128)S(1)} %get-tuple-element.69.edge_ref, f32[16,2,512]{2,1,0:T(2,128)S(1)} %all_to_all.15.blocks_ref, ...), custom_call_target="tpu_custom_call" | custom-call | flops 1048576 | bytes 3803140 | tf_op jit(solution)/shard_map/pallas_call | solution.py:372
  (33 shorter events, 2.8 us)
Async XLA Ops:
  3.7 5.4 %copy-start.8 = (s32[256]{0:T(256)S(1)}, s32[256]{0:T(256)}, u32[]{:S(2)}) copy-start(s32[256]{0:T(256)} %param.11) | copy-start | bytes 3076
  3.7 5.5 %copy-start = (f32[256,512]{1,0:T(8,128)S(1)}, f32[256,512]{1,0:T(8,128)}, u32[]{:S(2)}) copy-start(f32[256,512]{1,0:T(8,128)} %decay_in.3) | copy-start | bytes 1572868
  3.7 5.5 %copy-start.2 = (f32[512]{0:T(512)S(1)}, f32[512]{0:T(512)}, u32[]{:S(2)}) copy-start(f32[512]{0:T(512)} %param.12) | copy-start | bytes 6148
  3.7 5.5 %copy-start.3 = (f32[512]{0:T(512)S(1)}, f32[512]{0:T(512)}, u32[]{:S(2)}) copy-start(f32[512]{0:T(512)} %param.13) | copy-start | bytes 6148
  3.7 32.0 %all-to-all-start = ((bf16[8,256,512]{2,1,0:T(8,128)(2,1)}), bf16[8,256,512]{2,1,0:T(8,128)(2,1)S(1)}, u32[]{:S(2)}, u32[]{:S(2)}) async-start(bf16[8,256,512]{2,1,0:T(8,128)(2,1)} %dynamic-slice_bitcast_fusion.1), calls=%async_computation | async-start | bytes 4194304 | tf_op jit(solution)/shard_map/all_to_all | solution.py:418
  10.1 22.8 %collective-permute-start.2 = (f32[3,512]{1,0:T(4,128)S(1)}, f32[3,512]{1,0:T(4,128)S(1)}, u32[]{:S(2)}, u32[]{:S(2)}) collective-permute-start(f32[3,512]{1,0:T(4,128)S(1)} %get-tuple-element.44), channel_id=1, source_target_pairs={{0,6},{2,0},{4,2},{6,4},{8,14},{10,8},{12,10},{14,12},{16,22},{18,... | collective-permute-start | bytes 18440 | tf_op jit(solution)/shard_map/ppermute | solution.py:22
  11.9 23.2 %collective-permute-start.1 = (f32[3,512]{1,0:T(4,128)S(1)}, f32[3,512]{1,0:T(4,128)S(1)}, u32[]{:S(2)}, u32[]{:S(2)}) collective-permute-start(f32[3,512]{1,0:T(4,128)S(1)} %get-tuple-element.44), channel_id=1, source_target_pairs={{0,4},{2,6},{4,0},{6,2},{8,12},{10,14},{12,8},{14,10},{16,20},{18,... | collective-permute-start | bytes 18440 | tf_op jit(solution)/shard_map/ppermute | solution.py:22
  12.3 22.8 %collective-permute-start = (f32[3,512]{1,0:T(4,128)S(1)}, f32[3,512]{1,0:T(4,128)S(1)}, u32[]{:S(2)}, u32[]{:S(2)}) collective-permute-start(f32[3,512]{1,0:T(4,128)S(1)} %get-tuple-element.44), channel_id=1, source_target_pairs={{0,2},{2,4},{4,6},{6,0},{8,10},{10,12},{12,14},{14,8},{16,18},{18,... | collective-permute-start | bytes 18440 | tf_op jit(solution)/shard_map/ppermute | solution.py:22
  35.7 1.3 %copy-start.7 = (bf16[8,256,512]{2,1,0:T(8,128)(2,1)}, bf16[8,256,512]{2,1,0:T(8,128)(2,1)S(1)}, u32[]{:S(2)}) copy-start(bf16[8,256,512]{2,1,0:T(8,128)(2,1)S(1)} %all-to-all-done.slab_ref) | copy-start | bytes 6291460
  37.0 30.3 %all-to-all-start.1 = ((bf16[8,256,512]{2,1,0:T(8,128)(2,1)}), bf16[8,256,512]{2,1,0:T(8,128)(2,1)S(1)}, u32[]{:S(2)}, u32[]{:S(2)}) async-start(bf16[8,256,512]{2,1,0:T(8,128)(2,1)} %dynamic-slice_bitcast_fusion), calls=%async_computation.1 | async-start | bytes 4194304 | tf_op jit(solution)/shard_map/all_to_all | solution.py:426
  41.3 28.1 %copy-start.4 = (s32[3]{0:T(128)S(1)}, s32[3]{0:T(128)}, u32[]{:S(2)}) copy-start(s32[3]{0:T(128)} %pad_add_fusion.at_ref) | copy-start | bytes 40
  47.5 9.2 %collective-permute-start.3 = (s16[272,512]{1,0:T(8,128)(2,1)}, s16[272,512]{1,0:T(8,128)(2,1)S(1)}, u32[]{:S(2)}, u32[]{:S(2)}) collective-permute-start(s16[272,512]{1,0:T(8,128)(2,1)} %get-tuple-element.48), channel_id=1, source_target_pairs={{0,1},{1,0},{2,3},{3,2},{4,5},{5,4},{6,7},{7,6},{8,9},{9,8},{10,11... | collective-permute-start | bytes 835592 | tf_op jit(solution)/shard_map/ppermute | solution.py:390
  49.1 25.0 %collective-permute-start.6 = (f32[4,3,512]{2,1,0:T(4,128)}, f32[4,3,512]{2,1,0:T(4,128)}, u32[]{:S(2)}, u32[]{:S(2)}) collective-permute-start(f32[4,3,512]{2,1,0:T(4,128)} %pad_maximum_fusion.1), channel_id=1, source_target_pairs={{0,24},{2,26},{4,28},{6,30},{8,16},{10,18},{12,20},{14,22},{16,8},... | collective-permute-start | bytes 73736 | tf_op jit(solution)/shard_map/ppermute | solution.py:42
  53.0 21.0 %collective-permute-start.5 = (f32[4,3,512]{2,1,0:T(4,128)}, f32[4,3,512]{2,1,0:T(4,128)}, u32[]{:S(2)}, u32[]{:S(2)}) collective-permute-start(f32[4,3,512]{2,1,0:T(4,128)} %pad_maximum_fusion.1), channel_id=1, source_target_pairs={{0,16},{2,18},{4,20},{6,22},{8,24},{10,26},{12,28},{14,30},{16,0},... | collective-permute-start | bytes 73736 | tf_op jit(solution)/shard_map/ppermute | solution.py:42
  53.0 21.1 %collective-permute-start.4 = (f32[4,3,512]{2,1,0:T(4,128)}, f32[4,3,512]{2,1,0:T(4,128)}, u32[]{:S(2)}, u32[]{:S(2)}) collective-permute-start(f32[4,3,512]{2,1,0:T(4,128)} %pad_maximum_fusion.1), channel_id=1, source_target_pairs={{0,8},{2,10},{4,12},{6,14},{8,0},{10,2},{12,4},{14,6},{16,24},{18,... | collective-permute-start | bytes 73736 | tf_op jit(solution)/shard_map/ppermute | solution.py:42
  56.7 1.0 %copy-start.1 = (f32[256,512]{1,0:T(8,128)S(1)}, f32[256,512]{1,0:T(8,128)}, u32[]{:S(2)}) copy-start(f32[256,512]{1,0:T(8,128)} %get-tuple-element.47.own_ref) | copy-start | bytes 1572868
  57.9 18.5 %copy-start.5 = (f32[512]{0:T(512)S(1)}, f32[512]{0:T(512)}, u32[]{:S(2)}) copy-start(f32[512]{0:T(512)} %param.15) | copy-start | bytes 6148
  67.3 14.7 %collective-permute-start.7 = (s16[272,512]{1,0:T(8,128)(2,1)S(1)}, s16[272,512]{1,0:T(8,128)(2,1)S(1)}, u32[]{:S(2)}, u32[]{:S(2)}) collective-permute-start(s16[272,512]{1,0:T(8,128)(2,1)S(1)} %shard_map.113), channel_id=1, source_target_pairs={{0,16},{2,18},{4,20},{6,22},{8,24},{10,26},{12,28},{14,30},{16,0},... | collective-permute-start | bytes 835592 | tf_op jit(solution)/shard_map/ppermute | solution.py:385
  74.1 8.1 %collective-permute-start.8 = (s16[272,512]{1,0:T(8,128)(2,1)S(1)}, s16[272,512]{1,0:T(8,128)(2,1)S(1)}, u32[]{:S(2)}, u32[]{:S(2)}) collective-permute-start(s16[272,512]{1,0:T(8,128)(2,1)S(1)} %get-tuple-element.55), channel_id=1, source_target_pairs={{0,1},{1,0},{2,3},{3,2},{4,5},{5,4},{6,7},{7,6},{8,9},{9,8},{10,11... | collective-permute-start | bytes 835592 | tf_op jit(solution)/shard_map/ppermute | solution.py:390
  82.1 13.5 %copy-start.6 = (f32[512]{0:T(512)S(1)}, f32[512]{0:T(512)}, u32[]{:S(2)}) copy-start(f32[512]{0:T(512)} %param.14) | copy-start | bytes 6148

commit v4 on v3

--- a/solution.py
+++ b/solution.py
@@ -17,9 +17,8 @@
 LIMIT = 16 * 1024 * 1024
 
 
-def rotate(block, axis, turn, group):
-    route = [(i, i // group * group + (i + turn) % group) for i in range(lax.axis_size(axis))]
-    return lax.ppermute(block, axis, route)
+def swap(block, axis, turn):
+    return lax.ppermute(block, axis, [(i, i ^ turn) for i in range(lax.axis_size(axis))])
 
 
 def inner_size(count):
@@ -30,24 +29,12 @@
 
 
 def gather_near(rows, axis):
-    count = lax.axis_size(axis)
-    group = inner_size(count)
-    return jnp.stack([rows] + [rotate(rows, axis, s, group) for s in range(1, group)])
+    return [rows] + [swap(rows, axis, turn) for turn in range(1, inner_size(lax.axis_size(axis)))]
 
 
 def gather_far(near, axis):
     count = lax.axis_size(axis)
-    group = near.shape[0]
-    return [
-        lax.ppermute(near, axis, [(i, i ^ (turn * group)) for i in range(count)]) for turn in range(1, count // group)
-    ]
-
-
-def place(me, j, count):
-    group = inner_size(count)
-    high = lax.bitwise_xor(me // group, j // group)
-    low = lax.rem(lax.rem(me, group) - j % group + group, group)
-    return high * group + low
+    return [swap(near, axis, turn) for turn in range(near.shape[0], count, near.shape[0])]
 
 
 def lanes(ref, strip_ref):
@@ -144,7 +131,7 @@
     mine = v
     for j in range(count):
         mine = jnp.where(j == me, v, mine)
-        at = place(me, j, count)
+        at = lax.bitwise_xor(me, j)
         lead, spread, weight = (blocks_ref[at, k : k + 1, :] for k in range(3))
         along = lead / (1.0 + weight * v)
         edge_ref[0, j : j + 1, :] = along
@@ -159,7 +146,7 @@
     mine = info
     for j in reversed(range(count)):
         mine = jnp.where(j == me, info, mine)
-        at = place(me, j, count)
+        at = lax.bitwise_xor(me, j)
         lead, spread, weight = (blocks_ref[at, k : k + 1, :] for k in range(3))
         along = lead / (1.0 + spread * info)
         edge_ref[1, j : j + 1, :] = along
@@ -421,7 +408,7 @@
     )
     block_totals, own_half = lax.optimization_barrier((block_totals, half))
     near = lax.dynamic_index_in_dim(slabs, own_half, 0, keepdims=False)
-    blocks = gather_near(block_totals, "tm")
+    blocks = jnp.stack(gather_near(block_totals, "tm"))
     far, near, blocks = lax.optimization_barrier((far, near, blocks))
     near = lax.all_to_all(near, "tm", 0, 0, axis_index_groups=groups, tiled=True)
 

time: 97.8 us -> 97.8 us (level)
  no operation moved by 1% of the time
where the time goes in v4:
time: 97.8 us; the launch traced here: 97.3 us
  waiting for transfers between devices  35 us (36%)
  starting transfers between devices  20.9 us (21%)
  Pallas kernels  18.2 us (19%)
  blocking collectives  11.8 us (12%)
  local copies, waits for them, and re-layouts  8.56 us (9%)
  other arithmetic  2.07 us (2%)
    ppermute x6, waiting for transfers between devices, swap(): lax.ppermute(block, axis, [(i, i ^ turn) for i in range(lax.axis_size(axi...  19.8 us
    all_to_all x1, blocking collectives, body(): ends = lax.all_to_all(ends, 'tm', 0, 0, tiled=True)  11.8 us
    pallas_call x2, Pallas kernels, project(): pl.pallas_call(functools.partial(project_kernel, held), in_specs=[pl.Bloc...  10.9 us
    all_to_all x1, waiting for transfers between devices, body(): lax.all_to_all(near, 'tm', 0, 0, axis_index_groups=groups, tiled=True)  9.36 us
    pallas_call x6, Pallas kernels, call(): pl.pallas_call(kernel, in_specs=[smem if x.dtype == jnp.int32 else vmem f...  7.31 us
    ppermute x6, starting transfers between devices, swap(): lax.ppermute(block, axis, [(i, i ^ turn) for i in range(lax.axis_size(axi...  6.69 us
    all_to_all x1, starting transfers between devices, body(): far = lax.all_to_all(far, 'tm', 0, 0, axis_index_groups=groups, tiled=True)  5.37 us
    all_to_all x1, starting transfers between devices, body(): lax.all_to_all(near, 'tm', 0, 0, axis_index_groups=groups, tiled=True)  3.6 us
  transfers between devices with their start and end apart: 11, of which 5 were waited for; matrix products, arithmetic and copies ran while one was open for 5% of the time, Pallas kernels for 15%

profile of v4, /device:TPU:0, one launch (start us, length us, event | category | flops | bytes accessed | tf_op | source)
XLA Modules:
  0.0 97.3 jit_solution(2856680221148160245)
XLA Ops:
  0.7 3.0 %dynamic-slice_bitcast_fusion.1 = bf16[8,256,512]{2,1,0:T(8,128)(2,1)} fusion(bf16[2,8,256,512]{3,2,1,0:T(8,128)(2,1)} %bitcast.27, s32[]{:T(128)S(6)} %select_n.13), kind=kLoop, calls=%fused_computation.1 | loop fusion | bytes 4194308 | tf_op jit(solution)/shard_map/jit(dynamic_index_in_dim)/squeeze | solution.py:403
  3.7 5.4 %all-to-all-start = ((bf16[8,256,512]{2,1,0:T(8,128)(2,1)}), bf16[8,256,512]{2,1,0:T(8,128)(2,1)S(1)}, u32[]{:S(2)}, u32[]{:S(2)}) async-start(bf16[8,256,512]{2,1,0:T(8,128)(2,1)} %dynamic-slice_bitcast_fusion.1), calls=%async_computation | async-start | bytes 4194304 | tf_op jit(solution)/shard_map/all_to_all | solution.py:405
  9.2 0.9 shard_map.111
  10.1 1.8 %collective-permute-start.2 = (f32[3,512]{1,0:T(4,128)S(1)}, f32[3,512]{1,0:T(4,128)S(1)}, u32[]{:S(2)}, u32[]{:S(2)}) collective-permute-start(f32[3,512]{1,0:T(4,128)S(1)} %get-tuple-element.44), channel_id=1, source_target_pairs={{0,6},{2,4},{4,2},{6,0},{8,14},{10,12},{12,10},{14,8},{16,22},{18,... | collective-permute-start | bytes 18440 | tf_op jit(solution)/shard_map/ppermute | solution.py:21
  12.3 3.1 %dynamic-slice_bitcast_fusion = bf16[8,256,512]{2,1,0:T(8,128)(2,1)} fusion(bf16[2,8,256,512]{3,2,1,0:T(8,128)(2,1)} %bitcast.28, s32[]{:T(128)S(6)} %select_n.14), kind=kLoop, calls=%fused_computation | loop fusion | bytes 4194308 | tf_op jit(solution)/shard_map/jit(dynamic_index_in_dim)/squeeze | solution.py:410
  15.4 19.1 %collective-permute-done.2 = f32[3,512]{1,0:T(4,128)S(1)} collective-permute-done((f32[3,512]{1,0:T(4,128)S(1)}, f32[3,512]{1,0:T(4,128)S(1)}, u32[]{:S(2)}, u32[]{:S(2)}) %collective-permute-start.2) | collective-permute-done | bytes 6176 | tf_op jit(solution)/shard_map/ppermute | solution.py:21
  34.5 0.7 collective-permute-done.1
  35.7 1.3 %copy-done.7 = bf16[8,256,512]{2,1,0:T(8,128)(2,1)} copy-done((bf16[8,256,512]{2,1,0:T(8,128)(2,1)}, bf16[8,256,512]{2,1,0:T(8,128)(2,1)S(1)}, u32[]{:S(2)}) %copy-start.7) | copy-done | bytes 2097176
  37.0 3.6 %all-to-all-start.1 = ((bf16[8,256,512]{2,1,0:T(8,128)(2,1)}), bf16[8,256,512]{2,1,0:T(8,128)(2,1)S(1)}, u32[]{:S(2)}, u32[]{:S(2)}) async-start(bf16[8,256,512]{2,1,0:T(8,128)(2,1)} %dynamic-slice_bitcast_fusion), calls=%async_computation.1 | async-start | bytes 4194304 | tf_op jit(solution)/shard_map/all_to_all | solution.py:413
  41.3 6.2 %shard_map.112 = (f32[256,512]{1,0:T(8,128)}, s16[272,512]{1,0:T(8,128)(2,1)}) custom-call(s32[3]{0:T(128)} %pad_add_fusion.at_ref, bf16[8,256,512]{2,1,0:T(8,128)(2,1)} %copy-done.7, bf16[16,512,1024]{2,1,0:T(8,128)(2,1)} %bitcast.25), custom_call_target="tpu_custom_call" | custom-call | flops 2147483648 | bytes 11010048 | tf_op jit(solution)/shard_map/pallas_call | solution.py:318
  47.5 1.6 %collective-permute-start.3 = (s16[272,512]{1,0:T(8,128)(2,1)}, s16[272,512]{1,0:T(8,128)(2,1)S(1)}, u32[]{:S(2)}, u32[]{:S(2)}) collective-permute-start(s16[272,512]{1,0:T(8,128)(2,1)} %get-tuple-element.48), channel_id=1, source_target_pairs={{0,1},{1,0},{2,3},{3,2},{4,5},{5,4},{6,7},{7,6},{8,9},{9,8},{10,11... | collective-permute-start | bytes 835592 | tf_op jit(solution)/shard_map/ppermute | solution.py:377
  49.1 3.9 %collective-permute-start.6 = (f32[4,3,512]{2,1,0:T(4,128)}, f32[4,3,512]{2,1,0:T(4,128)}, u32[]{:S(2)}, u32[]{:S(2)}) collective-permute-start(f32[4,3,512]{2,1,0:T(4,128)} %pad_maximum_fusion.1), channel_id=1, source_target_pairs={{0,24},{2,26},{4,28},{6,30},{8,16},{10,18},{12,20},{14,22},{16,8},... | collective-permute-start | bytes 73736 | tf_op jit(solution)/shard_map/ppermute | solution.py:21
  53.6 3.1 %collective-permute-done.3.refs_0_ = s16[272,512]{1,0:T(8,128)(2,1)S(1)} collective-permute-done((s16[272,512]{1,0:T(8,128)(2,1)}, s16[272,512]{1,0:T(8,128)(2,1)S(1)}, u32[]{:S(2)}, u32[]{:S(2)}) %collective-permute-start.3) | collective-permute-done | bytes 278560 | tf_op jit(solution)/shard_map/ppermute | solution.py:377
  56.7 1.0 %copy-done.1 = f32[256,512]{1,0:T(8,128)S(1)} copy-done((f32[256,512]{1,0:T(8,128)S(1)}, f32[256,512]{1,0:T(8,128)}, u32[]{:S(2)}) %copy-start.1) | copy-done | bytes 524312
  58.0 9.4 %all-to-all-done.1.slab_ref = bf16[8,256,512]{2,1,0:T(8,128)(2,1)S(1)} async-done(((bf16[8,256,512]{2,1,0:T(8,128)(2,1)}), bf16[8,256,512]{2,1,0:T(8,128)(2,1)S(1)}, u32[]{:S(2)}, u32[]{:S(2)}) %all-to-all-start.1) | async-done | bytes 2097184 | tf_op jit(solution)/shard_map/all_to_all | solution.py:413
  67.3 2.0 %collective-permute-start.7 = (s16[272,512]{1,0:T(8,128)(2,1)S(1)}, s16[272,512]{1,0:T(8,128)(2,1)S(1)}, u32[]{:S(2)}, u32[]{:S(2)}) collective-permute-start(s16[272,512]{1,0:T(8,128)(2,1)S(1)} %shard_map.113), channel_id=1, source_target_pairs={{0,16},{2,18},{4,20},{6,22},{8,24},{10,26},{12,28},{14,30},{16,0},... | collective-permute-start | bytes 835592 | tf_op jit(solution)/shard_map/ppermute | solution.py:372
  69.3 4.7 %shard_map.114 = (f32[256,512]{1,0:T(8,128)S(1)}, s16[272,512]{1,0:T(8,128)(2,1)S(1)}) custom-call(s32[3]{0:T(128)S(1)} %copy-done.4, bf16[8,256,512]{2,1,0:T(8,128)(2,1)S(1)} %all-to-all-done.1.slab_ref, bf16[16,512,1024]{2,1,0:T(8,128)(2,1)} %bitcast.26), custom_call_target="tpu_custom_call" | custom-call | flops 2147483648 | bytes 11010048 | tf_op jit(solution)/shard_map/pallas_call | solution.py:318
  74.1 1.6 %collective-permute-start.8 = (s16[272,512]{1,0:T(8,128)(2,1)S(1)}, s16[272,512]{1,0:T(8,128)(2,1)S(1)}, u32[]{:S(2)}, u32[]{:S(2)}) collective-permute-start(s16[272,512]{1,0:T(8,128)(2,1)S(1)} %get-tuple-element.55), channel_id=1, source_target_pairs={{0,1},{1,0},{2,3},{3,2},{4,5},{5,4},{6,7},{7,6},{8,9},{9,8},{10,11... | collective-permute-start | bytes 835592 | tf_op jit(solution)/shard_map/ppermute | solution.py:377
  75.6 0.8 pad_maximum_fusion.blocks_ref
  76.5 2.8 %shard_map.116 = (f32[16,16,512]{2,1,0:T(8,128)S(1)}, f32[16,16,512]{2,1,0:T(8,128)S(1)}, f32[16,16,512]{2,1,0:T(8,128)S(1)}, f32[16,16,512]{2,1,0:T(8,128)S(1)}...) custom-call(s32[1]{0:T(128)} %bitcast.6.me_ref, ...), custom_call_target="tpu_custom_call" | custom-call | flops 10485760 | bytes 6625284 | tf_op jit(solution)/shard_map/pallas_call | solution.py:359
  79.3 2.7 %collective-permute-done.7.coded_ref = s16[272,512]{1,0:T(8,128)(2,1)S(1)} collective-permute-done((s16[272,512]{1,0:T(8,128)(2,1)S(1)}, s16[272,512]{1,0:T(8,128)(2,1)S(1)}, u32[]{:S(2)}, u32[]{:S(2)}) %collective-permute-start.7) | collective-permute-done | bytes 278560 | tf_op jit(solution)/shard_map/ppermute | solution.py:372
  82.1 1.7 %shard_map.117 = (f32[256,512]{1,0:T(8,128)}, f32[16,16,512]{2,1,0:T(8,128)S(1)}, f32[16,16,512]{2,1,0:T(8,128)S(1)}, f32[2,512]{1,0:T(2,128)S(1)}) custom-call(f32[256,512]{1,0:T(8,128)S(1)} %shard_map.115.refs_0_, s16[272,512]{1,0:T(8,128)(2,1)S(1)} %collective-permute-done.8.refs_1_, f32[16,16,512]{2,1,0:T(8,128)S(1)} %get-tuple-element.60.refs_2_, ...), custom_call_target="tpu_custom_call" | custom-call | flops 1572864 | bytes 5869568 | tf_op jit(solution)/shard_map/pallas_call | solution.py:359
  83.9 11.8 %all_to_all.15.blocks_ref = f32[16,2,512]{2,1,0:T(2,128)S(1)} all-to-all(f32[16,2,512]{2,1,0:T(2,128)S(1)} %broadcast_in_dim.29), channel_id=1, replica_groups=mesh['tm'=16,'space'=2] {'tm'}, dimensions={0} | all-to-all | bytes 131072 | tf_op jit(solution)/shard_map/all_to_all | solution.py:445
  95.6 1.6 %shard_map.118 = (f32[256,512]{1,0:T(8,128)}, f32[256,512]{1,0:T(8,128)}) custom-call(s32[1]{0:T(128)} %bitcast.6.me_ref, f32[1,512]{1,0:T(1,128)S(1)} %bitcast.24, f32[3,16,16,512]{3,2,1,0:T(8,128)S(1)} %get-tuple-element.68.whole_ref, f32[2,16,512]{2,1,0:T(8,128)S(1)} %get-tuple-element.69.edge_ref, f32[16,2,512]{2,1,0:T(2,128)S(1)} %all_to_all.15.blocks_ref, ...), custom_call_target="tpu_custom_call" | custom-call | flops 1048576 | bytes 3803140 | tf_op jit(solution)/shard_map/pallas_call | solution.py:359
  (33 shorter events, 2.6 us)
Async XLA Ops:
  3.7 5.4 %copy-start.8 = (s32[256]{0:T(256)S(1)}, s32[256]{0:T(256)}, u32[]{:S(2)}) copy-start(s32[256]{0:T(256)} %param.11) | copy-start | bytes 3076
  3.7 5.5 %copy-start = (f32[256,512]{1,0:T(8,128)S(1)}, f32[256,512]{1,0:T(8,128)}, u32[]{:S(2)}) copy-start(f32[256,512]{1,0:T(8,128)} %decay_in.3) | copy-start | bytes 1572868
  3.7 5.5 %copy-start.2 = (f32[512]{0:T(512)S(1)}, f32[512]{0:T(512)}, u32[]{:S(2)}) copy-start(f32[512]{0:T(512)} %param.12) | copy-start | bytes 6148
  3.7 5.5 %copy-start.3 = (f32[512]{0:T(512)S(1)}, f32[512]{0:T(512)}, u32[]{:S(2)}) copy-start(f32[512]{0:T(512)} %param.13) | copy-start | bytes 6148
  3.7 32.0 %all-to-all-start = ((bf16[8,256,512]{2,1,0:T(8,128)(2,1)}), bf16[8,256,512]{2,1,0:T(8,128)(2,1)S(1)}, u32[]{:S(2)}, u32[]{:S(2)}) async-start(bf16[8,256,512]{2,1,0:T(8,128)(2,1)} %dynamic-slice_bitcast_fusion.1), calls=%async_computation | async-start | bytes 4194304 | tf_op jit(solution)/shard_map/all_to_all | solution.py:405
  10.1 24.3 %collective-permute-start.2 = (f32[3,512]{1,0:T(4,128)S(1)}, f32[3,512]{1,0:T(4,128)S(1)}, u32[]{:S(2)}, u32[]{:S(2)}) collective-permute-start(f32[3,512]{1,0:T(4,128)S(1)} %get-tuple-element.44), channel_id=1, source_target_pairs={{0,6},{2,4},{4,2},{6,0},{8,14},{10,12},{12,10},{14,8},{16,22},{18,... | collective-permute-start | bytes 18440 | tf_op jit(solution)/shard_map/ppermute | solution.py:21
  11.9 23.2 %collective-permute-start.1 = (f32[3,512]{1,0:T(4,128)S(1)}, f32[3,512]{1,0:T(4,128)S(1)}, u32[]{:S(2)}, u32[]{:S(2)}) collective-permute-start(f32[3,512]{1,0:T(4,128)S(1)} %get-tuple-element.44), channel_id=1, source_target_pairs={{0,4},{2,6},{4,0},{6,2},{8,12},{10,14},{12,8},{14,10},{16,20},{18,... | collective-permute-start | bytes 18440 | tf_op jit(solution)/shard_map/ppermute | solution.py:21
  12.3 22.8 %collective-permute-start = (f32[3,512]{1,0:T(4,128)S(1)}, f32[3,512]{1,0:T(4,128)S(1)}, u32[]{:S(2)}, u32[]{:S(2)}) collective-permute-start(f32[3,512]{1,0:T(4,128)S(1)} %get-tuple-element.44), channel_id=1, source_target_pairs={{0,2},{2,0},{4,6},{6,4},{8,10},{10,8},{12,14},{14,12},{16,18},{18,... | collective-permute-start | bytes 18440 | tf_op jit(solution)/shard_map/ppermute | solution.py:21
  35.7 1.3 %copy-start.7 = (bf16[8,256,512]{2,1,0:T(8,128)(2,1)}, bf16[8,256,512]{2,1,0:T(8,128)(2,1)S(1)}, u32[]{:S(2)}) copy-start(bf16[8,256,512]{2,1,0:T(8,128)(2,1)S(1)} %all-to-all-done.slab_ref) | copy-start | bytes 6291460
  37.0 30.3 %all-to-all-start.1 = ((bf16[8,256,512]{2,1,0:T(8,128)(2,1)}), bf16[8,256,512]{2,1,0:T(8,128)(2,1)S(1)}, u32[]{:S(2)}, u32[]{:S(2)}) async-start(bf16[8,256,512]{2,1,0:T(8,128)(2,1)} %dynamic-slice_bitcast_fusion), calls=%async_computation.1 | async-start | bytes 4194304 | tf_op jit(solution)/shard_map/all_to_all | solution.py:413
  41.3 28.1 %copy-start.4 = (s32[3]{0:T(128)S(1)}, s32[3]{0:T(128)}, u32[]{:S(2)}) copy-start(s32[3]{0:T(128)} %pad_add_fusion.at_ref) | copy-start | bytes 40
  47.5 9.2 %collective-permute-start.3 = (s16[272,512]{1,0:T(8,128)(2,1)}, s16[272,512]{1,0:T(8,128)(2,1)S(1)}, u32[]{:S(2)}, u32[]{:S(2)}) collective-permute-start(s16[272,512]{1,0:T(8,128)(2,1)} %get-tuple-element.48), channel_id=1, source_target_pairs={{0,1},{1,0},{2,3},{3,2},{4,5},{5,4},{6,7},{7,6},{8,9},{9,8},{10,11... | collective-permute-start | bytes 835592 | tf_op jit(solution)/shard_map/ppermute | solution.py:377
  49.1 25.0 %collective-permute-start.6 = (f32[4,3,512]{2,1,0:T(4,128)}, f32[4,3,512]{2,1,0:T(4,128)}, u32[]{:S(2)}, u32[]{:S(2)}) collective-permute-start(f32[4,3,512]{2,1,0:T(4,128)} %pad_maximum_fusion.1), channel_id=1, source_target_pairs={{0,24},{2,26},{4,28},{6,30},{8,16},{10,18},{12,20},{14,22},{16,8},... | collective-permute-start | bytes 73736 | tf_op jit(solution)/shard_map/ppermute | solution.py:21
  53.0 21.0 %collective-permute-start.5 = (f32[4,3,512]{2,1,0:T(4,128)}, f32[4,3,512]{2,1,0:T(4,128)}, u32[]{:S(2)}, u32[]{:S(2)}) collective-permute-start(f32[4,3,512]{2,1,0:T(4,128)} %pad_maximum_fusion.1), channel_id=1, source_target_pairs={{0,16},{2,18},{4,20},{6,22},{8,24},{10,26},{12,28},{14,30},{16,0},... | collective-permute-start | bytes 73736 | tf_op jit(solution)/shard_map/ppermute | solution.py:21
  53.0 21.1 %collective-permute-start.4 = (f32[4,3,512]{2,1,0:T(4,128)}, f32[4,3,512]{2,1,0:T(4,128)}, u32[]{:S(2)}, u32[]{:S(2)}) collective-permute-start(f32[4,3,512]{2,1,0:T(4,128)} %pad_maximum_fusion.1), channel_id=1, source_target_pairs={{0,8},{2,10},{4,12},{6,14},{8,0},{10,2},{12,4},{14,6},{16,24},{18,... | collective-permute-start | bytes 73736 | tf_op jit(solution)/shard_map/ppermute | solution.py:21
  56.7 1.0 %copy-start.1 = (f32[256,512]{1,0:T(8,128)S(1)}, f32[256,512]{1,0:T(8,128)}, u32[]{:S(2)}) copy-start(f32[256,512]{1,0:T(8,128)} %get-tuple-element.47.own_ref) | copy-start | bytes 1572868
  57.9 18.5 %copy-start.5 = (f32[512]{0:T(512)S(1)}, f32[512]{0:T(512)}, u32[]{:S(2)}) copy-start(f32[512]{0:T(512)} %param.15) | copy-start | bytes 6148
  67.3 14.7 %collective-permute-start.7 = (s16[272,512]{1,0:T(8,128)(2,1)S(1)}, s16[272,512]{1,0:T(8,128)(2,1)S(1)}, u32[]{:S(2)}, u32[]{:S(2)}) collective-permute-start(s16[272,512]{1,0:T(8,128)(2,1)S(1)} %shard_map.113), channel_id=1, source_target_pairs={{0,16},{2,18},{4,20},{6,22},{8,24},{10,26},{12,28},{14,30},{16,0},... | collective-permute-start | bytes 835592 | tf_op jit(solution)/shard_map/ppermute | solution.py:372
  74.1 8.1 %collective-permute-start.8 = (s16[272,512]{1,0:T(8,128)(2,1)S(1)}, s16[272,512]{1,0:T(8,128)(2,1)S(1)}, u32[]{:S(2)}, u32[]{:S(2)}) collective-permute-start(s16[272,512]{1,0:T(8,128)(2,1)S(1)} %get-tuple-element.55), channel_id=1, source_target_pairs={{0,1},{1,0},{2,3},{3,2},{4,5},{5,4},{6,7},{7,6},{8,9},{9,8},{10,11... | collective-permute-start | bytes 835592 | tf_op jit(solution)/shard_map/ppermute | solution.py:377
  82.1 13.5 %copy-start.6 = (f32[512]{0:T(512)S(1)}, f32[512]{0:T(512)}, u32[]{:S(2)}) copy-start(f32[512]{0:T(512)} %param.14) | copy-start | bytes 6148

commit v5 on v4

--- a/solution.py
+++ b/solution.py
@@ -293,7 +293,8 @@
     modes = own_ref.shape[1]
     copies = []
     for g in range(count):
-        pair = [pltpu.make_async_copy(basis_ref.at[at_ref[0] + g], basis_area.at[g], basis_sems.at[g])]
+        source = (g + count // 2) % count
+        pair = [pltpu.make_async_copy(basis_ref.at[at_ref[0] + source], basis_area.at[g], basis_sems.at[g])]
         if not held:
             pair.append(pltpu.make_async_copy(slab_ref.at[g], slab_area.at[g], refs[1].at[g]))
         copies.append(pair)
@@ -341,8 +342,50 @@
     return own, coded
 
 
-def add_kernel(own_ref, coded_ref, out_ref):
-    out_ref[...] = own_ref[...] + decode(coded_ref)
+def project_one_kernel(at_ref, slab_ref, basis_ref, out_ref, basis_area, sum_area, sems):
+    count = slab_ref.shape[0]
+    modes = out_ref.shape[1]
+    columns = pl.ds(pl.multiple_of(at_ref[1] * modes, LANES), modes)
+    copies = [
+        pltpu.make_async_copy(basis_ref.at[at_ref[0] + g, :, columns], basis_area.at[g], sems.at[g])
+        for g in range(count)
+    ]
+    for copy in copies:
+        copy.start()
+    for g in range(count):
+        copies[g].wait()
+        term = jnp.dot(slab_ref[g], basis_area[g], preferred_element_type=F32)
+        sum_area[...] = term if g == 0 else sum_area[...] + term
+    if out_ref.dtype == jnp.int16:
+        encode(sum_area[...], out_ref)
+    else:
+        out_ref[...] = sum_area[...]
+
+
+def project_one(slabs, basis, first, owner, modes, out):
+    count, steps, cells = slabs.shape
+    vmem = pl.BlockSpec(memory_space=pltpu.VMEM)
+    return pl.pallas_call(
+        project_one_kernel,
+        in_specs=[pl.BlockSpec(memory_space=pltpu.SMEM), vmem, pl.BlockSpec(memory_space=pl.ANY)],
+        out_specs=vmem,
+        out_shape=out,
+        scratch_shapes=[
+            pltpu.VMEM((count, cells, modes), basis.dtype),
+            pltpu.VMEM((steps, modes), F32),
+            pltpu.SemaphoreType.DMA((count,)),
+        ],
+        compiler_params=pltpu.CompilerParams(vmem_limit_bytes=36 * LIMIT // 16),
+        cost_estimate=pl.CostEstimate(
+            flops=2 * count * steps * cells * modes,
+            bytes_accessed=2 * count * cells * (steps + modes) + 4 * steps * modes,
+            transcendentals=0,
+        ),
+    )(jnp.stack([first, owner]), slabs, basis)
+
+
+def add_kernel(own_ref, early_ref, late_ref, out_ref):
+    out_ref[...] = own_ref[...] + decode(early_ref) + decode(late_ref)
 
 
 def fold_kernel(own_ref, *refs):
@@ -367,9 +410,11 @@
     )(*inputs)
 
 
-def swap_halves(block, axis):
-    half = lax.axis_size(axis) // 2
-    return lax.ppermute(block, axis, [(i, (i + half) % (2 * half)) for i in range(2 * half)])
+def mirror(block, axis, inner):
+    count = lax.axis_size(axis)
+    quarter = count // 4
+    places = [i for i in range(count) if (quarter <= i < 3 * quarter) == inner]
+    return lax.ppermute(block, axis, [(i, i ^ (3 * quarter)) for i in places])
 
 
 def send_along(term, axis, turn):
@@ -402,7 +447,8 @@
     owners = [lax.rem(side + turn, space_count) for turn in range(space_count)]
     far = lax.dynamic_index_in_dim(slabs, 1 - half, 0, keepdims=False)
     far, q = lax.optimization_barrier((far, q))
-    far = lax.all_to_all(far, "tm", 0, 0, axis_index_groups=groups, tiled=True)
+    turned = [places[group // 2 :] + places[: group // 2] for places in groups]
+    far = lax.all_to_all(far, "tm", 0, 0, axis_index_groups=turned, tiled=True)
     chunk_totals, block_totals = call(
         totals_kernel, (me, decay, seen, q, r), [shape((3,) + flat), shape((3, modes))], [strips] * 2, 40 * steps * modes
     )
@@ -416,15 +462,18 @@
     arriving = [send_along(term, "space", turn + 1) for turn, term in enumerate(theirs)]
     coded = jax.ShapeDtypeStruct((steps + PAD, modes), jnp.int16)
     (crossing,) = call(fold_kernel, (own, *arriving), [coded], [], 8 * steps * modes)
-    near, crossing = lax.optimization_barrier((near, crossing))
-    crossing = swap_halves(crossing, "tm")
+    early = mirror(crossing, "tm", True)
+    near, crossing, early = lax.optimization_barrier((near, crossing, early))
+    crossing = mirror(crossing, "tm", False)
     rest = gather_far(blocks, "tm")
 
-    own, theirs = project(near, basis, first, owners, modes, True)
+    theirs = [project_one(near, basis, first, owner, modes, coded) for owner in owners[1:]]
     parts = [send_along(term, "space", turn + 1) for turn, term in enumerate(theirs)]
+    own_near, _ = lax.optimization_barrier((near, theirs))
+    own = project_one(own_near, basis, first, side, modes, shape((steps, modes)))
     own, chunk_totals, rest = lax.optimization_barrier((own, chunk_totals, rest))
     blocks = jnp.concatenate([blocks] + rest, 0)
-    (own,) = call(add_kernel, (own, crossing), [shape((steps, modes))], [], EARLY)
+    (own,) = call(add_kernel, (own, early, crossing), [shape((steps, modes))], [], EARLY)
     parts.insert(0, own)
     *maps, whole, carry, edge, log_variance = call(
         functools.partial(gains_kernel, tm_count),

time: 97.8 us -> 99.7 us (1.019)
  waiting for transfers between devices: 35 us -> 28.4 us
  starting transfers between devices: 20.9 us -> 27.1 us
  Pallas kernels: 18.2 us -> 20.1 us
    all_to_all x1, waiting for transfers between devices: 9.36 us -> 1.33 us  [body(): lax.all_to_all(near, 'tm', 0, 0, axis_index_groups=groups, tiled=True)]
    pallas_call x0 -> x2, Pallas kernels: none -> 6.66 us  [project_one(): pl.pallas_call(project_one_kernel, in_specs=[pl.BlockSpec(memory_space=pl...]
    pallas_call x2 -> x1, Pallas kernels: 10.9 us -> 6.05 us  [project(): pl.pallas_call(functools.partial(project_kernel, held), in_specs=[pl.Bloc...]
    ppermute x2, waiting for transfers between devices: 3.13 us -> 7.62 us  [send_along(): lax.ppermute(term, axis, [(i, (i + turn) % count) for i in range(count)])]
    ppermute x1 -> x2, starting transfers between devices: 2.01 us -> 5.85 us  [mirror(): return lax.ppermute(block, axis, [(i, i ^ 3 * quarter) for i in places])]
    ppermute x1 -> x2, waiting for transfers between devices: 2.73 us -> 0.01 us  [mirror(): return lax.ppermute(block, axis, [(i, i ^ 3 * quarter) for i in places])]
    all_to_all x1, starting transfers between devices: 5.37 us -> 6.69 us  [body(): far = lax.all_to_all(far, 'tm', 0, 0, axis_index_groups=turned, tiled=True)]
    ppermute x6, starting transfers between devices: 6.69 us -> 7.77 us  [swap(): lax.ppermute(block, axis, [(i, i ^ turn) for i in range(lax.axis_size(axi...]
  transfers between devices with their start and end apart: 11 -> 12, of which waited for: 5 -> 4; matrix products, arithmetic and copies ran while one was open for 5% -> 5% of each run, Pallas kernels for 15% -> 17%
where the time goes in v5:
time: 99.7 us; the launch traced here: 99.1 us
  waiting for transfers between devices  28.4 us (28%)
  starting transfers between devices  27.1 us (27%)
  Pallas kernels  20.1 us (20%)
  blocking collectives  11.1 us (11%)
  local copies, waits for them, and re-layouts  9.31 us (9%)
  other arithmetic  2.18 us (2%)
    ppermute x6, waiting for transfers between devices, swap(): lax.ppermute(block, axis, [(i, i ^ turn) for i in range(lax.axis_size(axi...  19.5 us
    all_to_all x1, blocking collectives, body(): ends = lax.all_to_all(ends, 'tm', 0, 0, tiled=True)  11.1 us
    ppermute x6, starting transfers between devices, swap(): lax.ppermute(block, axis, [(i, i ^ turn) for i in range(lax.axis_size(axi...  7.77 us
    ppermute x2, waiting for transfers between devices, send_along(): lax.ppermute(term, axis, [(i, (i + turn) % count) for i in range(count)])  7.62 us
    pallas_call x6, Pallas kernels, call(): pl.pallas_call(kernel, in_specs=[smem if x.dtype == jnp.int32 else vmem f...  7.41 us
    all_to_all x1, starting transfers between devices, body(): far = lax.all_to_all(far, 'tm', 0, 0, axis_index_groups=turned, tiled=True)  6.69 us
    pallas_call x2, Pallas kernels, project_one(): pl.pallas_call(project_one_kernel, in_specs=[pl.BlockSpec(memory_space=pl...  6.66 us
    pallas_call x1, Pallas kernels, project(): pl.pallas_call(functools.partial(project_kernel, held), in_specs=[pl.Bloc...  6.05 us
  transfers between devices with their start and end apart: 12, of which 4 were waited for; matrix products, arithmetic and copies ran while one was open for 5% of the time, Pallas kernels for 17%

profile of v5, /device:TPU:0, one launch (start us, length us, event | category | flops | bytes accessed | tf_op | source)
XLA Modules:
  0.0 99.1 jit_solution(306288010599482976)
XLA Ops:
  0.7 3.0 %dynamic-slice_bitcast_fusion.1 = bf16[8,256,512]{2,1,0:T(8,128)(2,1)} fusion(bf16[2,8,256,512]{3,2,1,0:T(8,128)(2,1)} %bitcast.29, s32[]{:T(128)S(6)} %select_n.13), kind=kLoop, calls=%fused_computation.1 | loop fusion | bytes 4194308 | tf_op jit(solution)/shard_map/jit(dynamic_index_in_dim)/squeeze | solution.py:448
  3.7 6.7 %all-to-all-start = ((bf16[8,256,512]{2,1,0:T(8,128)(2,1)}), bf16[8,256,512]{2,1,0:T(8,128)(2,1)S(1)}, u32[]{:S(2)}, u32[]{:S(2)}) async-start(bf16[8,256,512]{2,1,0:T(8,128)(2,1)} %dynamic-slice_bitcast_fusion.1), calls=%async_computation | async-start | bytes 4194304 | tf_op jit(solution)/shard_map/all_to_all | solution.py:451
  10.5 0.9 shard_map.111
  11.4 1.3 %collective-permute-start.2 = (f32[3,512]{1,0:T(4,128)S(1)}, f32[3,512]{1,0:T(4,128)S(1)}, u32[]{:S(2)}, u32[]{:S(2)}) collective-permute-start(f32[3,512]{1,0:T(4,128)S(1)} %get-tuple-element.44), channel_id=1, source_target_pairs={{0,6},{2,4},{4,2},{6,0},{8,14},{10,12},{12,10},{14,8},{16,22},{18,... | collective-permute-start | bytes 18440 | tf_op jit(solution)/shard_map/ppermute | solution.py:21
  13.4 3.1 %dynamic-slice_bitcast_fusion = bf16[8,256,512]{2,1,0:T(8,128)(2,1)} fusion(bf16[2,8,256,512]{3,2,1,0:T(8,128)(2,1)} %bitcast.30, s32[]{:T(128)S(6)} %select_n.14), kind=kLoop, calls=%fused_computation | loop fusion | bytes 4194308 | tf_op jit(solution)/shard_map/jit(dynamic_index_in_dim)/squeeze | solution.py:456
  16.4 18.8 %collective-permute-done.2 = f32[3,512]{1,0:T(4,128)S(1)} collective-permute-done((f32[3,512]{1,0:T(4,128)S(1)}, f32[3,512]{1,0:T(4,128)S(1)}, u32[]{:S(2)}, u32[]{:S(2)}) %collective-permute-start.2) | collective-permute-done | bytes 6176 | tf_op jit(solution)/shard_map/ppermute | solution.py:21
  36.5 1.3 %copy-done.8 = bf16[8,256,512]{2,1,0:T(8,128)(2,1)} copy-done((bf16[8,256,512]{2,1,0:T(8,128)(2,1)}, bf16[8,256,512]{2,1,0:T(8,128)(2,1)S(1)}, u32[]{:S(2)}) %copy-start.8) | copy-done | bytes 2097176
  37.8 3.6 %all-to-all-start.1 = ((bf16[8,256,512]{2,1,0:T(8,128)(2,1)}), bf16[8,256,512]{2,1,0:T(8,128)(2,1)S(1)}, u32[]{:S(2)}, u32[]{:S(2)}) async-start(bf16[8,256,512]{2,1,0:T(8,128)(2,1)} %dynamic-slice_bitcast_fusion), calls=%async_computation.1 | async-start | bytes 4194304 | tf_op jit(solution)/shard_map/all_to_all | solution.py:459
  42.0 6.0 %shard_map.112 = (f32[256,512]{1,0:T(8,128)}, s16[272,512]{1,0:T(8,128)(2,1)}) custom-call(s32[3]{0:T(128)} %pad_add_fusion.1.at_ref, bf16[8,256,512]{2,1,0:T(8,128)(2,1)} %copy-done.8, bf16[16,512,1024]{2,1,0:T(8,128)(2,1)} %bitcast.26), custom_call_target="tpu_custom_call" | custom-call | flops 2147483648 | bytes 11010048 | tf_op jit(solution)/shard_map/pallas_call | solution.py:319
  48.1 1.6 %collective-permute-start.3 = (s16[272,512]{1,0:T(8,128)(2,1)}, s16[272,512]{1,0:T(8,128)(2,1)S(1)}, u32[]{:S(2)}, u32[]{:S(2)}) collective-permute-start(s16[272,512]{1,0:T(8,128)(2,1)} %get-tuple-element.48), channel_id=1, source_target_pairs={{0,1},{1,0},{2,3},{3,2},{4,5},{5,4},{6,7},{7,6},{8,9},{9,8},{10,11... | collective-permute-start | bytes 835592 | tf_op jit(solution)/shard_map/ppermute | solution.py:422
  49.7 7.6 %collective-permute-done.3.refs_0_ = s16[272,512]{1,0:T(8,128)(2,1)S(1)} collective-permute-done((s16[272,512]{1,0:T(8,128)(2,1)}, s16[272,512]{1,0:T(8,128)(2,1)S(1)}, u32[]{:S(2)}, u32[]{:S(2)}) %collective-permute-start.3) | collective-permute-done | bytes 278560 | tf_op jit(solution)/shard_map/ppermute | solution.py:422
  57.3 1.0 %copy-done.1 = f32[256,512]{1,0:T(8,128)S(1)} copy-done((f32[256,512]{1,0:T(8,128)S(1)}, f32[256,512]{1,0:T(8,128)}, u32[]{:S(2)}) %copy-start.1) | copy-done | bytes 524312
  59.4 3.7 %collective-permute-start.7 = (f32[4,3,512]{2,1,0:T(4,128)}, f32[4,3,512]{2,1,0:T(4,128)}, u32[]{:S(2)}, u32[]{:S(2)}) collective-permute-start(f32[4,3,512]{2,1,0:T(4,128)} %pad_maximum_fusion.1), channel_id=1, source_target_pairs={{0,24},{2,26},{4,28},{6,30},{8,16},{10,18},{12,20},{14,22},{16,8},... | collective-permute-start | bytes 73736 | tf_op jit(solution)/shard_map/ppermute | solution.py:21
  63.1 2.1 %collective-permute-start.6 = (f32[4,3,512]{2,1,0:T(4,128)}, f32[4,3,512]{2,1,0:T(4,128)}, u32[]{:S(2)}, u32[]{:S(2)}) collective-permute-start(f32[4,3,512]{2,1,0:T(4,128)} %pad_maximum_fusion.1), channel_id=1, source_target_pairs={{0,16},{2,18},{4,20},{6,22},{8,24},{10,26},{12,28},{14,30},{16,0},... | collective-permute-start | bytes 73736 | tf_op jit(solution)/shard_map/ppermute | solution.py:21
  66.0 1.3 %all-to-all-done.1.slab_ref = bf16[8,256,512]{2,1,0:T(8,128)(2,1)S(1)} async-done(((bf16[8,256,512]{2,1,0:T(8,128)(2,1)}), bf16[8,256,512]{2,1,0:T(8,128)(2,1)S(1)}, u32[]{:S(2)}, u32[]{:S(2)}) %all-to-all-start.1) | async-done | bytes 2097184 | tf_op jit(solution)/shard_map/all_to_all | solution.py:459
  67.3 5.2 %collective-permute-start.8 = (s16[272,512]{1,0:T(8,128)(2,1)S(1)}, s16[272,512]{1,0:T(8,128)(2,1)S(1)}, u32[]{:S(2)}, u32[]{:S(2)}) collective-permute-start(s16[272,512]{1,0:T(8,128)(2,1)S(1)} %shard_map.113), channel_id=1, source_target_pairs={{0,24},{2,26},{4,28},{6,30},{24,0},{26,2},{28,4},{30,6},{1,25},{3,... | collective-permute-start | bytes 835592 | tf_op jit(solution)/shard_map/ppermute | solution.py:417
  72.5 3.4 %shard_map.114 = s16[272,512]{1,0:T(8,128)(2,1)S(1)} custom-call(s32[2]{0:T(128)S(1)} %pad_add_fusion.2.at_ref, bf16[8,256,512]{2,1,0:T(8,128)(2,1)S(1)} %all-to-all-done.1.slab_ref, bf16[16,512,1024]{2,1,0:T(8,128)(2,1)} %bitcast.27), custom_call_target="tpu_custom_call" | custom-call | flops 1073741824 | bytes 6815744 | tf_op jit(solution)/shard_map/pallas_call | solution.py:368
  75.9 1.6 %collective-permute-start.9 = (s16[272,512]{1,0:T(8,128)(2,1)S(1)}, s16[272,512]{1,0:T(8,128)(2,1)S(1)}, u32[]{:S(2)}, u32[]{:S(2)}) collective-permute-start(s16[272,512]{1,0:T(8,128)(2,1)S(1)} %shard_map.114), channel_id=1, source_target_pairs={{0,1},{1,0},{2,3},{3,2},{4,5},{5,4},{6,7},{7,6},{8,9},{9,8},{10,11... | collective-permute-start | bytes 835592 | tf_op jit(solution)/shard_map/ppermute | solution.py:422
  77.5 3.3 %shard_map.115.own_ref = f32[256,512]{1,0:T(8,128)S(1)} custom-call(s32[2]{0:T(128)S(1)} %pad_add_fusion.at_ref, bf16[8,256,512]{2,1,0:T(8,128)(2,1)S(1)} %all-to-all-done.1.slab_ref, bf16[16,512,1024]{2,1,0:T(8,128)(2,1)} %bitcast.28), custom_call_target="tpu_custom_call" | custom-call | flops 1073741824 | bytes 6815744 | tf_op jit(solution)/shard_map/pallas_call | solution.py:368
  80.8 0.8 pad_maximum_fusion.blocks_ref
  81.6 2.8 %shard_map.117 = (f32[16,16,512]{2,1,0:T(8,128)S(1)}, f32[16,16,512]{2,1,0:T(8,128)S(1)}, f32[16,16,512]{2,1,0:T(8,128)S(1)}, f32[16,16,512]{2,1,0:T(8,128)S(1)}...) custom-call(s32[1]{0:T(128)} %bitcast.5.me_ref, ...), custom_call_target="tpu_custom_call" | custom-call | flops 10485760 | bytes 6625284 | tf_op jit(solution)/shard_map/pallas_call | solution.py:402
  84.6 1.7 %shard_map.118 = (f32[256,512]{1,0:T(8,128)}, f32[16,16,512]{2,1,0:T(8,128)S(1)}, f32[16,16,512]{2,1,0:T(8,128)S(1)}, f32[2,512]{1,0:T(2,128)S(1)}) custom-call(f32[256,512]{1,0:T(8,128)S(1)} %shard_map.116.refs_0_, s16[272,512]{1,0:T(8,128)(2,1)S(1)} %collective-permute-done.9.refs_1_, f32[16,16,512]{2,1,0:T(8,128)S(1)} %get-tuple-element.60.refs_2_, ...), custom_call_target="tpu_custom_call" | custom-call | flops 1572864 | bytes 5869568 | tf_op jit(solution)/shard_map/pallas_call | solution.py:402
  86.4 11.1 %all_to_all.15.blocks_ref = f32[16,2,512]{2,1,0:T(2,128)S(1)} all-to-all(f32[16,2,512]{2,1,0:T(2,128)S(1)} %broadcast_in_dim.29), channel_id=1, replica_groups=mesh['tm'=16,'space'=2] {'tm'}, dimensions={0} | all-to-all | bytes 131072 | tf_op jit(solution)/shard_map/all_to_all | solution.py:494
  97.5 1.6 %shard_map.119 = (f32[256,512]{1,0:T(8,128)}, f32[256,512]{1,0:T(8,128)}) custom-call(s32[1]{0:T(128)} %bitcast.5.me_ref, f32[1,512]{1,0:T(1,128)S(1)} %bitcast.25, f32[3,16,16,512]{3,2,1,0:T(8,128)S(1)} %get-tuple-element.68.whole_ref, f32[2,16,512]{2,1,0:T(8,128)S(1)} %get-tuple-element.69.edge_ref, f32[16,2,512]{2,1,0:T(2,128)S(1)} %all_to_all.15.blocks_ref, ...), custom_call_target="tpu_custom_call" | custom-call | flops 1048576 | bytes 3803140 | tf_op jit(solution)/shard_map/pallas_call | solution.py:402
  (40 shorter events, 4.5 us)
Async XLA Ops:
  3.7 6.7 %copy-start.9 = (s32[256]{0:T(256)S(1)}, s32[256]{0:T(256)}, u32[]{:S(2)}) copy-start(s32[256]{0:T(256)} %param.11) | copy-start | bytes 3076
  3.7 6.8 %copy-start = (f32[256,512]{1,0:T(8,128)S(1)}, f32[256,512]{1,0:T(8,128)}, u32[]{:S(2)}) copy-start(f32[256,512]{1,0:T(8,128)} %decay_in.3) | copy-start | bytes 1572868
  3.7 6.8 %copy-start.2 = (f32[512]{0:T(512)S(1)}, f32[512]{0:T(512)}, u32[]{:S(2)}) copy-start(f32[512]{0:T(512)} %param.12) | copy-start | bytes 6148
  3.7 6.8 %copy-start.3 = (f32[512]{0:T(512)S(1)}, f32[512]{0:T(512)}, u32[]{:S(2)}) copy-start(f32[512]{0:T(512)} %param.13) | copy-start | bytes 6148
  3.7 32.8 %all-to-all-start = ((bf16[8,256,512]{2,1,0:T(8,128)(2,1)}), bf16[8,256,512]{2,1,0:T(8,128)(2,1)S(1)}, u32[]{:S(2)}, u32[]{:S(2)}) async-start(bf16[8,256,512]{2,1,0:T(8,128)(2,1)} %dynamic-slice_bitcast_fusion.1), calls=%async_computation | async-start | bytes 4194304 | tf_op jit(solution)/shard_map/all_to_all | solution.py:451
  11.4 23.8 %collective-permute-start.2 = (f32[3,512]{1,0:T(4,128)S(1)}, f32[3,512]{1,0:T(4,128)S(1)}, u32[]{:S(2)}, u32[]{:S(2)}) collective-permute-start(f32[3,512]{1,0:T(4,128)S(1)} %get-tuple-element.44), channel_id=1, source_target_pairs={{0,6},{2,4},{4,2},{6,0},{8,14},{10,12},{12,10},{14,8},{16,22},{18,... | collective-permute-start | bytes 18440 | tf_op jit(solution)/shard_map/ppermute | solution.py:21
  12.7 23.2 %collective-permute-start.1 = (f32[3,512]{1,0:T(4,128)S(1)}, f32[3,512]{1,0:T(4,128)S(1)}, u32[]{:S(2)}, u32[]{:S(2)}) collective-permute-start(f32[3,512]{1,0:T(4,128)S(1)} %get-tuple-element.44), channel_id=1, source_target_pairs={{0,4},{2,6},{4,0},{6,2},{8,12},{10,14},{12,8},{14,10},{16,20},{18,... | collective-permute-start | bytes 18440 | tf_op jit(solution)/shard_map/ppermute | solution.py:21
  13.3 22.6 %collective-permute-start = (f32[3,512]{1,0:T(4,128)S(1)}, f32[3,512]{1,0:T(4,128)S(1)}, u32[]{:S(2)}, u32[]{:S(2)}) collective-permute-start(f32[3,512]{1,0:T(4,128)S(1)} %get-tuple-element.44), channel_id=1, source_target_pairs={{0,2},{2,0},{4,6},{6,4},{8,10},{10,8},{12,14},{14,12},{16,18},{18,... | collective-permute-start | bytes 18440 | tf_op jit(solution)/shard_map/ppermute | solution.py:21
  36.5 1.3 %copy-start.8 = (bf16[8,256,512]{2,1,0:T(8,128)(2,1)}, bf16[8,256,512]{2,1,0:T(8,128)(2,1)S(1)}, u32[]{:S(2)}) copy-start(bf16[8,256,512]{2,1,0:T(8,128)(2,1)S(1)} %all-to-all-done.slab_ref) | copy-start | bytes 6291460
  37.8 29.4 %all-to-all-start.1 = ((bf16[8,256,512]{2,1,0:T(8,128)(2,1)}), bf16[8,256,512]{2,1,0:T(8,128)(2,1)S(1)}, u32[]{:S(2)}, u32[]{:S(2)}) async-start(bf16[8,256,512]{2,1,0:T(8,128)(2,1)} %dynamic-slice_bitcast_fusion), calls=%async_computation.1 | async-start | bytes 4194304 | tf_op jit(solution)/shard_map/all_to_all | solution.py:459
  48.1 9.2 %collective-permute-start.3 = (s16[272,512]{1,0:T(8,128)(2,1)}, s16[272,512]{1,0:T(8,128)(2,1)S(1)}, u32[]{:S(2)}, u32[]{:S(2)}) collective-permute-start(s16[272,512]{1,0:T(8,128)(2,1)} %get-tuple-element.48), channel_id=1, source_target_pairs={{0,1},{1,0},{2,3},{3,2},{4,5},{5,4},{6,7},{7,6},{8,9},{9,8},{10,11... | collective-permute-start | bytes 835592 | tf_op jit(solution)/shard_map/ppermute | solution.py:422
  57.3 1.0 %copy-start.1 = (f32[256,512]{1,0:T(8,128)S(1)}, f32[256,512]{1,0:T(8,128)}, u32[]{:S(2)}) copy-start(f32[256,512]{1,0:T(8,128)} %get-tuple-element.47.own_ref) | copy-start | bytes 1572868
  58.6 6.7 %collective-permute-start.4 = (s16[272,512]{1,0:T(8,128)(2,1)S(1)}, s16[272,512]{1,0:T(8,128)(2,1)S(1)}, u32[]{:S(2)}, u32[]{:S(2)}) collective-permute-start(s16[272,512]{1,0:T(8,128)(2,1)S(1)} %shard_map.113), channel_id=1, source_target_pairs={{8,16},{10,18},{12,20},{14,22},{16,8},{18,10},{20,12},{22,14},{9,1... | collective-permute-start | bytes 835592 | tf_op jit(solution)/shard_map/ppermute | solution.py:417
  59.4 21.4 %collective-permute-start.7 = (f32[4,3,512]{2,1,0:T(4,128)}, f32[4,3,512]{2,1,0:T(4,128)}, u32[]{:S(2)}, u32[]{:S(2)}) collective-permute-start(f32[4,3,512]{2,1,0:T(4,128)} %pad_maximum_fusion.1), channel_id=1, source_target_pairs={{0,24},{2,26},{4,28},{6,30},{8,16},{10,18},{12,20},{14,22},{16,8},... | collective-permute-start | bytes 73736 | tf_op jit(solution)/shard_map/ppermute | solution.py:21
  63.1 17.7 %collective-permute-start.6 = (f32[4,3,512]{2,1,0:T(4,128)}, f32[4,3,512]{2,1,0:T(4,128)}, u32[]{:S(2)}, u32[]{:S(2)}) collective-permute-start(f32[4,3,512]{2,1,0:T(4,128)} %pad_maximum_fusion.1), channel_id=1, source_target_pairs={{0,16},{2,18},{4,20},{6,22},{8,24},{10,26},{12,28},{14,30},{16,0},... | collective-permute-start | bytes 73736 | tf_op jit(solution)/shard_map/ppermute | solution.py:21
  65.2 15.5 %collective-permute-start.5 = (f32[4,3,512]{2,1,0:T(4,128)}, f32[4,3,512]{2,1,0:T(4,128)}, u32[]{:S(2)}, u32[]{:S(2)}) collective-permute-start(f32[4,3,512]{2,1,0:T(4,128)} %pad_maximum_fusion.1), channel_id=1, source_target_pairs={{0,8},{2,10},{4,12},{6,14},{8,0},{10,2},{12,4},{14,6},{16,24},{18,... | collective-permute-start | bytes 73736 | tf_op jit(solution)/shard_map/ppermute | solution.py:21
  65.3 0.7 copy-start.6
  67.3 17.2 %collective-permute-start.8 = (s16[272,512]{1,0:T(8,128)(2,1)S(1)}, s16[272,512]{1,0:T(8,128)(2,1)S(1)}, u32[]{:S(2)}, u32[]{:S(2)}) collective-permute-start(s16[272,512]{1,0:T(8,128)(2,1)S(1)} %shard_map.113), channel_id=1, source_target_pairs={{0,24},{2,26},{4,28},{6,30},{24,0},{26,2},{28,4},{30,6},{1,25},{3,... | collective-permute-start | bytes 835592 | tf_op jit(solution)/shard_map/ppermute | solution.py:417
  75.9 5.8 %copy-start.4 = (f32[512]{0:T(512)S(1)}, f32[512]{0:T(512)}, u32[]{:S(2)}) copy-start(f32[512]{0:T(512)} %param.15) | copy-start | bytes 6148
  75.9 8.6 %copy-start.7 = (s16[272,512]{1,0:T(8,128)(2,1)S(1)}, s16[272,512]{1,0:T(8,128)(2,1)}, u32[]{:S(2)}) copy-start(s16[272,512]{1,0:T(8,128)(2,1)} %copy-done.6) | copy-start | bytes 835588
  75.9 8.7 %collective-permute-start.9 = (s16[272,512]{1,0:T(8,128)(2,1)S(1)}, s16[272,512]{1,0:T(8,128)(2,1)S(1)}, u32[]{:S(2)}, u32[]{:S(2)}) collective-permute-start(s16[272,512]{1,0:T(8,128)(2,1)S(1)} %shard_map.114), channel_id=1, source_target_pairs={{0,1},{1,0},{2,3},{3,2},{4,5},{5,4},{6,7},{7,6},{8,9},{9,8},{10,11... | collective-permute-start | bytes 835592 | tf_op jit(solution)/shard_map/ppermute | solution.py:422
  84.6 12.9 %copy-start.5 = (f32[512]{0:T(512)S(1)}, f32[512]{0:T(512)}, u32[]{:S(2)}) copy-start(f32[512]{0:T(512)} %param.14) | copy-start | bytes 6148

commit v6 on v4

--- a/solution.py
+++ b/solution.py
@@ -293,7 +293,8 @@
     modes = own_ref.shape[1]
     copies = []
     for g in range(count):
-        pair = [pltpu.make_async_copy(basis_ref.at[at_ref[0] + g], basis_area.at[g], basis_sems.at[g])]
+        source = g if held else (g + count // 2) % count
+        pair = [pltpu.make_async_copy(basis_ref.at[at_ref[0] + source], basis_area.at[g], basis_sems.at[g])]
         if not held:
             pair.append(pltpu.make_async_copy(slab_ref.at[g], slab_area.at[g], refs[1].at[g]))
         copies.append(pair)
@@ -341,8 +342,8 @@
     return own, coded
 
 
-def add_kernel(own_ref, coded_ref, out_ref):
-    out_ref[...] = own_ref[...] + decode(coded_ref)
+def add_kernel(own_ref, early_ref, late_ref, out_ref):
+    out_ref[...] = own_ref[...] + decode(early_ref) + decode(late_ref)
 
 
 def fold_kernel(own_ref, *refs):
@@ -367,9 +368,11 @@
     )(*inputs)
 
 
-def swap_halves(block, axis):
-    half = lax.axis_size(axis) // 2
-    return lax.ppermute(block, axis, [(i, (i + half) % (2 * half)) for i in range(2 * half)])
+def mirror(block, axis, inner):
+    count = lax.axis_size(axis)
+    quarter = count // 4
+    places = [i for i in range(count) if (quarter <= i < 3 * quarter) == inner]
+    return lax.ppermute(block, axis, [(i, i ^ (3 * quarter)) for i in places])
 
 
 def send_along(term, axis, turn):
@@ -402,7 +405,8 @@
     owners = [lax.rem(side + turn, space_count) for turn in range(space_count)]
     far = lax.dynamic_index_in_dim(slabs, 1 - half, 0, keepdims=False)
     far, q = lax.optimization_barrier((far, q))
-    far = lax.all_to_all(far, "tm", 0, 0, axis_index_groups=groups, tiled=True)
+    turned = [places[group // 2 :] + places[: group // 2] for places in groups]
+    far = lax.all_to_all(far, "tm", 0, 0, axis_index_groups=turned, tiled=True)
     chunk_totals, block_totals = call(
         totals_kernel, (me, decay, seen, q, r), [shape((3,) + flat), shape((3, modes))], [strips] * 2, 40 * steps * modes
     )
@@ -416,15 +420,16 @@
     arriving = [send_along(term, "space", turn + 1) for turn, term in enumerate(theirs)]
     coded = jax.ShapeDtypeStruct((steps + PAD, modes), jnp.int16)
     (crossing,) = call(fold_kernel, (own, *arriving), [coded], [], 8 * steps * modes)
-    near, crossing = lax.optimization_barrier((near, crossing))
-    crossing = swap_halves(crossing, "tm")
+    early = mirror(crossing, "tm", True)
+    near, crossing, early = lax.optimization_barrier((near, crossing, early))
+    crossing = mirror(crossing, "tm", False)
     rest = gather_far(blocks, "tm")
 
     own, theirs = project(near, basis, first, owners, modes, True)
     parts = [send_along(term, "space", turn + 1) for turn, term in enumerate(theirs)]
     own, chunk_totals, rest = lax.optimization_barrier((own, chunk_totals, rest))
     blocks = jnp.concatenate([blocks] + rest, 0)
-    (own,) = call(add_kernel, (own, crossing), [shape((steps, modes))], [], EARLY)
+    (own,) = call(add_kernel, (own, early, crossing), [shape((steps, modes))], [], EARLY)
     parts.insert(0, own)
     *maps, whole, carry, edge, log_variance = call(
         functools.partial(gains_kernel, tm_count),

time: 97.8 us -> 99.2 us (1.014)
  starting transfers between devices: 20.9 us -> 27.4 us
  waiting for transfers between devices: 35 us -> 30.4 us
  blocking collectives: 11.8 us -> 10.4 us
    all_to_all x1, waiting for transfers between devices: 9.36 us -> 1.21 us  [body(): lax.all_to_all(near, 'tm', 0, 0, axis_index_groups=groups, tiled=True)]
    ppermute x2, waiting for transfers between devices: 3.13 us -> 9.68 us  [send_along(): lax.ppermute(term, axis, [(i, (i + turn) % count) for i in range(count)])]
    ppermute x1 -> x2, starting transfers between devices: 2.01 us -> 6.04 us  [mirror(): return lax.ppermute(block, axis, [(i, i ^ 3 * quarter) for i in places])]
    ppermute x1 -> x2, waiting for transfers between devices: 2.73 us -> 0.01 us  [mirror(): return lax.ppermute(block, axis, [(i, i ^ 3 * quarter) for i in places])]
    all_to_all x1, blocking collectives: 11.8 us -> 10.4 us  [body(): ends = lax.all_to_all(ends, 'tm', 0, 0, tiled=True)]
    all_to_all x1, starting transfers between devices: 5.37 us -> 6.69 us  [body(): far = lax.all_to_all(far, 'tm', 0, 0, axis_index_groups=turned, tiled=True)]
    ppermute x6, starting transfers between devices: 6.69 us -> 7.84 us  [swap(): lax.ppermute(block, axis, [(i, i ^ turn) for i in range(lax.axis_size(axi...]
    unnamed x18 -> x22, local copies, waits for them, and re-layouts: 2.37 us -> 3.08 us
  transfers between devices with their start and end apart: 11 -> 12, of which waited for: 5 -> 5; matrix products, arithmetic and copies ran while one was open for 5% -> 5% of each run, Pallas kernels for 15% -> 15%
where the time goes in v6:
time: 99.2 us; the launch traced here: 98.6 us
  waiting for transfers between devices  30.4 us (31%)
  starting transfers between devices  27.4 us (28%)
  Pallas kernels  18.3 us (18%)
  blocking collectives  10.4 us (10%)
  local copies, waits for them, and re-layouts  9.3 us (9%)
  other arithmetic  2.02 us (2%)
    ppermute x6, waiting for transfers between devices, swap(): lax.ppermute(block, axis, [(i, i ^ turn) for i in range(lax.axis_size(axi...  19.5 us
    pallas_call x2, Pallas kernels, project(): pl.pallas_call(functools.partial(project_kernel, held), in_specs=[pl.Bloc...  10.9 us
    all_to_all x1, blocking collectives, body(): ends = lax.all_to_all(ends, 'tm', 0, 0, tiled=True)  10.4 us
    ppermute x2, waiting for transfers between devices, send_along(): lax.ppermute(term, axis, [(i, (i + turn) % count) for i in range(count)])  9.68 us
    ppermute x6, starting transfers between devices, swap(): lax.ppermute(block, axis, [(i, i ^ turn) for i in range(lax.axis_size(axi...  7.84 us
    pallas_call x6, Pallas kernels, call(): pl.pallas_call(kernel, in_specs=[smem if x.dtype == jnp.int32 else vmem f...  7.41 us
    all_to_all x1, starting transfers between devices, body(): far = lax.all_to_all(far, 'tm', 0, 0, axis_index_groups=turned, tiled=True)  6.69 us
    ppermute x2, starting transfers between devices, mirror(): return lax.ppermute(block, axis, [(i, i ^ 3 * quarter) for i in places])  6.04 us
  transfers between devices with their start and end apart: 12, of which 5 were waited for; matrix products, arithmetic and copies ran while one was open for 5% of the time, Pallas kernels for 15%

profile of v6, /device:TPU:0, one launch (start us, length us, event | category | flops | bytes accessed | tf_op | source)
XLA Modules:
  0.0 98.6 jit_solution(17956918978649703367)
XLA Ops:
  0.7 3.0 %dynamic-slice_bitcast_fusion.1 = bf16[8,256,512]{2,1,0:T(8,128)(2,1)} fusion(bf16[2,8,256,512]{3,2,1,0:T(8,128)(2,1)} %bitcast.27, s32[]{:T(128)S(6)} %select_n.13), kind=kLoop, calls=%fused_computation.1 | loop fusion | bytes 4194308 | tf_op jit(solution)/shard_map/jit(dynamic_index_in_dim)/squeeze | solution.py:406
  3.7 6.7 %all-to-all-start = ((bf16[8,256,512]{2,1,0:T(8,128)(2,1)}), bf16[8,256,512]{2,1,0:T(8,128)(2,1)S(1)}, u32[]{:S(2)}, u32[]{:S(2)}) async-start(bf16[8,256,512]{2,1,0:T(8,128)(2,1)} %dynamic-slice_bitcast_fusion.1), calls=%async_computation | async-start | bytes 4194304 | tf_op jit(solution)/shard_map/all_to_all | solution.py:409
  10.5 0.9 shard_map.111
  11.4 1.3 %collective-permute-start.2 = (f32[3,512]{1,0:T(4,128)S(1)}, f32[3,512]{1,0:T(4,128)S(1)}, u32[]{:S(2)}, u32[]{:S(2)}) collective-permute-start(f32[3,512]{1,0:T(4,128)S(1)} %get-tuple-element.45), channel_id=1, source_target_pairs={{0,6},{2,4},{4,2},{6,0},{8,14},{10,12},{12,10},{14,8},{16,22},{18,... | collective-permute-start | bytes 18440 | tf_op jit(solution)/shard_map/ppermute | solution.py:21
  13.4 3.1 %dynamic-slice_bitcast_fusion = bf16[8,256,512]{2,1,0:T(8,128)(2,1)} fusion(bf16[2,8,256,512]{3,2,1,0:T(8,128)(2,1)} %bitcast.28, s32[]{:T(128)S(6)} %select_n.14), kind=kLoop, calls=%fused_computation | loop fusion | bytes 4194308 | tf_op jit(solution)/shard_map/jit(dynamic_index_in_dim)/squeeze | solution.py:414
  16.4 18.8 %collective-permute-done.2 = f32[3,512]{1,0:T(4,128)S(1)} collective-permute-done((f32[3,512]{1,0:T(4,128)S(1)}, f32[3,512]{1,0:T(4,128)S(1)}, u32[]{:S(2)}, u32[]{:S(2)}) %collective-permute-start.2) | collective-permute-done | bytes 6176 | tf_op jit(solution)/shard_map/ppermute | solution.py:21
  36.5 1.3 %copy-done.9 = bf16[8,256,512]{2,1,0:T(8,128)(2,1)} copy-done((bf16[8,256,512]{2,1,0:T(8,128)(2,1)}, bf16[8,256,512]{2,1,0:T(8,128)(2,1)S(1)}, u32[]{:S(2)}) %copy-start.9) | copy-done | bytes 2097176
  37.8 3.6 %all-to-all-start.1 = ((bf16[8,256,512]{2,1,0:T(8,128)(2,1)}), bf16[8,256,512]{2,1,0:T(8,128)(2,1)S(1)}, u32[]{:S(2)}, u32[]{:S(2)}) async-start(bf16[8,256,512]{2,1,0:T(8,128)(2,1)} %dynamic-slice_bitcast_fusion), calls=%async_computation.1 | async-start | bytes 4194304 | tf_op jit(solution)/shard_map/all_to_all | solution.py:417
  42.0 6.2 %shard_map.112 = (f32[256,512]{1,0:T(8,128)}, s16[272,512]{1,0:T(8,128)(2,1)}) custom-call(s32[3]{0:T(128)} %pad_add_fusion.at_ref, bf16[8,256,512]{2,1,0:T(8,128)(2,1)} %copy-done.9, bf16[16,512,1024]{2,1,0:T(8,128)(2,1)} %bitcast.25), custom_call_target="tpu_custom_call" | custom-call | flops 2147483648 | bytes 11010048 | tf_op jit(solution)/shard_map/pallas_call | solution.py:319
  48.2 1.6 %collective-permute-start.3 = (s16[272,512]{1,0:T(8,128)(2,1)}, s16[272,512]{1,0:T(8,128)(2,1)S(1)}, u32[]{:S(2)}, u32[]{:S(2)}) collective-permute-start(s16[272,512]{1,0:T(8,128)(2,1)} %get-tuple-element.49), channel_id=1, source_target_pairs={{0,1},{1,0},{2,3},{3,2},{4,5},{5,4},{6,7},{7,6},{8,9},{9,8},{10,11... | collective-permute-start | bytes 835592 | tf_op jit(solution)/shard_map/ppermute | solution.py:380
  49.8 7.6 %collective-permute-done.3.refs_0_ = s16[272,512]{1,0:T(8,128)(2,1)S(1)} collective-permute-done((s16[272,512]{1,0:T(8,128)(2,1)}, s16[272,512]{1,0:T(8,128)(2,1)S(1)}, u32[]{:S(2)}, u32[]{:S(2)}) %collective-permute-start.3) | collective-permute-done | bytes 278560 | tf_op jit(solution)/shard_map/ppermute | solution.py:380
  57.4 1.0 %copy-done.1 = f32[256,512]{1,0:T(8,128)S(1)} copy-done((f32[256,512]{1,0:T(8,128)S(1)}, f32[256,512]{1,0:T(8,128)}, u32[]{:S(2)}) %copy-start.1) | copy-done | bytes 524312
  59.4 3.8 %collective-permute-start.7 = (f32[4,3,512]{2,1,0:T(4,128)}, f32[4,3,512]{2,1,0:T(4,128)}, u32[]{:S(2)}, u32[]{:S(2)}) collective-permute-start(f32[4,3,512]{2,1,0:T(4,128)} %pad_maximum_fusion.1), channel_id=1, source_target_pairs={{0,24},{2,26},{4,28},{6,30},{8,16},{10,18},{12,20},{14,22},{16,8},... | collective-permute-start | bytes 73736 | tf_op jit(solution)/shard_map/ppermute | solution.py:21
  63.1 2.1 %collective-permute-start.6 = (f32[4,3,512]{2,1,0:T(4,128)}, f32[4,3,512]{2,1,0:T(4,128)}, u32[]{:S(2)}, u32[]{:S(2)}) collective-permute-start(f32[4,3,512]{2,1,0:T(4,128)} %pad_maximum_fusion.1), channel_id=1, source_target_pairs={{0,16},{2,18},{4,20},{6,22},{8,24},{10,26},{12,28},{14,30},{16,0},... | collective-permute-start | bytes 73736 | tf_op jit(solution)/shard_map/ppermute | solution.py:21
  66.0 1.2 %all-to-all-done.1.slab_ref = bf16[8,256,512]{2,1,0:T(8,128)(2,1)S(1)} async-done(((bf16[8,256,512]{2,1,0:T(8,128)(2,1)}), bf16[8,256,512]{2,1,0:T(8,128)(2,1)S(1)}, u32[]{:S(2)}, u32[]{:S(2)}) %all-to-all-start.1) | async-done | bytes 2097184 | tf_op jit(solution)/shard_map/all_to_all | solution.py:417
  67.2 5.4 %collective-permute-start.8 = (s16[272,512]{1,0:T(8,128)(2,1)S(1)}, s16[272,512]{1,0:T(8,128)(2,1)S(1)}, u32[]{:S(2)}, u32[]{:S(2)}) collective-permute-start(s16[272,512]{1,0:T(8,128)(2,1)S(1)} %shard_map.113), channel_id=1, source_target_pairs={{0,24},{2,26},{4,28},{6,30},{24,0},{26,2},{28,4},{30,6},{1,25},{3,... | collective-permute-start | bytes 835592 | tf_op jit(solution)/shard_map/ppermute | solution.py:375
  72.6 4.7 %shard_map.114 = (f32[256,512]{1,0:T(8,128)S(1)}, s16[272,512]{1,0:T(8,128)(2,1)S(1)}) custom-call(s32[3]{0:T(128)S(1)} %copy-done.4, bf16[8,256,512]{2,1,0:T(8,128)(2,1)S(1)} %all-to-all-done.1.slab_ref, bf16[16,512,1024]{2,1,0:T(8,128)(2,1)} %bitcast.26), custom_call_target="tpu_custom_call" | custom-call | flops 2147483648 | bytes 11010048 | tf_op jit(solution)/shard_map/pallas_call | solution.py:319
  77.3 1.6 %collective-permute-start.9 = (s16[272,512]{1,0:T(8,128)(2,1)S(1)}, s16[272,512]{1,0:T(8,128)(2,1)S(1)}, u32[]{:S(2)}, u32[]{:S(2)}) collective-permute-start(s16[272,512]{1,0:T(8,128)(2,1)S(1)} %get-tuple-element.57), channel_id=1, source_target_pairs={{0,1},{1,0},{2,3},{3,2},{4,5},{5,4},{6,7},{7,6},{8,9},{9,8},{10,11... | collective-permute-start | bytes 835592 | tf_op jit(solution)/shard_map/ppermute | solution.py:380
  78.9 0.8 pad_maximum_fusion.blocks_ref
  79.8 2.8 %shard_map.116 = (f32[16,16,512]{2,1,0:T(8,128)S(1)}, f32[16,16,512]{2,1,0:T(8,128)S(1)}, f32[16,16,512]{2,1,0:T(8,128)S(1)}, f32[16,16,512]{2,1,0:T(8,128)S(1)}...) custom-call(s32[1]{0:T(128)} %bitcast.6.me_ref, ...), custom_call_target="tpu_custom_call" | custom-call | flops 10485760 | bytes 6625284 | tf_op jit(solution)/shard_map/pallas_call | solution.py:360
  82.7 2.1 %collective-permute-done.9.refs_1_ = s16[272,512]{1,0:T(8,128)(2,1)S(1)} collective-permute-done((s16[272,512]{1,0:T(8,128)(2,1)S(1)}, s16[272,512]{1,0:T(8,128)(2,1)S(1)}, u32[]{:S(2)}, u32[]{:S(2)}) %collective-permute-start.9) | collective-permute-done | bytes 278560 | tf_op jit(solution)/shard_map/ppermute | solution.py:380
  84.8 1.7 %shard_map.117 = (f32[256,512]{1,0:T(8,128)}, f32[16,16,512]{2,1,0:T(8,128)S(1)}, f32[16,16,512]{2,1,0:T(8,128)S(1)}, f32[2,512]{1,0:T(2,128)S(1)}) custom-call(f32[256,512]{1,0:T(8,128)S(1)} %shard_map.115.refs_0_, s16[272,512]{1,0:T(8,128)(2,1)S(1)} %collective-permute-done.9.refs_1_, f32[16,16,512]{2,1,0:T(8,128)S(1)} %get-tuple-element.62.refs_2_, ...), custom_call_target="tpu_custom_call" | custom-call | flops 1572864 | bytes 5869568 | tf_op jit(solution)/shard_map/pallas_call | solution.py:360
  86.5 10.4 %all_to_all.15.blocks_ref = f32[16,2,512]{2,1,0:T(2,128)S(1)} all-to-all(f32[16,2,512]{2,1,0:T(2,128)S(1)} %broadcast_in_dim.29), channel_id=1, replica_groups=mesh['tm'=16,'space'=2] {'tm'}, dimensions={0} | all-to-all | bytes 131072 | tf_op jit(solution)/shard_map/all_to_all | solution.py:450
  97.0 1.6 %shard_map.118 = (f32[256,512]{1,0:T(8,128)}, f32[256,512]{1,0:T(8,128)}) custom-call(s32[1]{0:T(128)} %bitcast.6.me_ref, f32[1,512]{1,0:T(1,128)S(1)} %bitcast.24, f32[3,16,16,512]{3,2,1,0:T(8,128)S(1)} %get-tuple-element.70.whole_ref, f32[2,16,512]{2,1,0:T(8,128)S(1)} %get-tuple-element.71.edge_ref, f32[16,2,512]{2,1,0:T(2,128)S(1)} %all_to_all.15.blocks_ref, ...), custom_call_target="tpu_custom_call" | custom-call | flops 1048576 | bytes 3803140 | tf_op jit(solution)/shard_map/pallas_call | solution.py:360
  (39 shorter events, 4.4 us)
Async XLA Ops:
  3.7 6.7 %copy-start.10 = (s32[256]{0:T(256)S(1)}, s32[256]{0:T(256)}, u32[]{:S(2)}) copy-start(s32[256]{0:T(256)} %param.11) | copy-start | bytes 3076
  3.7 6.8 %copy-start = (f32[256,512]{1,0:T(8,128)S(1)}, f32[256,512]{1,0:T(8,128)}, u32[]{:S(2)}) copy-start(f32[256,512]{1,0:T(8,128)} %decay_in.3) | copy-start | bytes 1572868
  3.7 6.8 %copy-start.2 = (f32[512]{0:T(512)S(1)}, f32[512]{0:T(512)}, u32[]{:S(2)}) copy-start(f32[512]{0:T(512)} %param.12) | copy-start | bytes 6148
  3.7 6.8 %copy-start.3 = (f32[512]{0:T(512)S(1)}, f32[512]{0:T(512)}, u32[]{:S(2)}) copy-start(f32[512]{0:T(512)} %param.13) | copy-start | bytes 6148
  3.7 32.8 %all-to-all-start = ((bf16[8,256,512]{2,1,0:T(8,128)(2,1)}), bf16[8,256,512]{2,1,0:T(8,128)(2,1)S(1)}, u32[]{:S(2)}, u32[]{:S(2)}) async-start(bf16[8,256,512]{2,1,0:T(8,128)(2,1)} %dynamic-slice_bitcast_fusion.1), calls=%async_computation | async-start | bytes 4194304 | tf_op jit(solution)/shard_map/all_to_all | solution.py:409
  11.4 23.8 %collective-permute-start.2 = (f32[3,512]{1,0:T(4,128)S(1)}, f32[3,512]{1,0:T(4,128)S(1)}, u32[]{:S(2)}, u32[]{:S(2)}) collective-permute-start(f32[3,512]{1,0:T(4,128)S(1)} %get-tuple-element.45), channel_id=1, source_target_pairs={{0,6},{2,4},{4,2},{6,0},{8,14},{10,12},{12,10},{14,8},{16,22},{18,... | collective-permute-start | bytes 18440 | tf_op jit(solution)/shard_map/ppermute | solution.py:21
  12.7 23.2 %collective-permute-start.1 = (f32[3,512]{1,0:T(4,128)S(1)}, f32[3,512]{1,0:T(4,128)S(1)}, u32[]{:S(2)}, u32[]{:S(2)}) collective-permute-start(f32[3,512]{1,0:T(4,128)S(1)} %get-tuple-element.45), channel_id=1, source_target_pairs={{0,4},{2,6},{4,0},{6,2},{8,12},{10,14},{12,8},{14,10},{16,20},{18,... | collective-permute-start | bytes 18440 | tf_op jit(solution)/shard_map/ppermute | solution.py:21
  13.3 22.6 %collective-permute-start = (f32[3,512]{1,0:T(4,128)S(1)}, f32[3,512]{1,0:T(4,128)S(1)}, u32[]{:S(2)}, u32[]{:S(2)}) collective-permute-start(f32[3,512]{1,0:T(4,128)S(1)} %get-tuple-element.45), channel_id=1, source_target_pairs={{0,2},{2,0},{4,6},{6,4},{8,10},{10,8},{12,14},{14,12},{16,18},{18,... | collective-permute-start | bytes 18440 | tf_op jit(solution)/shard_map/ppermute | solution.py:21
  36.5 1.3 %copy-start.9 = (bf16[8,256,512]{2,1,0:T(8,128)(2,1)}, bf16[8,256,512]{2,1,0:T(8,128)(2,1)S(1)}, u32[]{:S(2)}) copy-start(bf16[8,256,512]{2,1,0:T(8,128)(2,1)S(1)} %all-to-all-done.slab_ref) | copy-start | bytes 6291460
  37.8 29.4 %all-to-all-start.1 = ((bf16[8,256,512]{2,1,0:T(8,128)(2,1)}), bf16[8,256,512]{2,1,0:T(8,128)(2,1)S(1)}, u32[]{:S(2)}, u32[]{:S(2)}) async-start(bf16[8,256,512]{2,1,0:T(8,128)(2,1)} %dynamic-slice_bitcast_fusion), calls=%async_computation.1 | async-start | bytes 4194304 | tf_op jit(solution)/shard_map/all_to_all | solution.py:417
  42.0 30.6 %copy-start.4 = (s32[3]{0:T(128)S(1)}, s32[3]{0:T(128)}, u32[]{:S(2)}) copy-start(s32[3]{0:T(128)} %pad_add_fusion.at_ref) | copy-start | bytes 40
  48.2 9.2 %collective-permute-start.3 = (s16[272,512]{1,0:T(8,128)(2,1)}, s16[272,512]{1,0:T(8,128)(2,1)S(1)}, u32[]{:S(2)}, u32[]{:S(2)}) collective-permute-start(s16[272,512]{1,0:T(8,128)(2,1)} %get-tuple-element.49), channel_id=1, source_target_pairs={{0,1},{1,0},{2,3},{3,2},{4,5},{5,4},{6,7},{7,6},{8,9},{9,8},{10,11... | collective-permute-start | bytes 835592 | tf_op jit(solution)/shard_map/ppermute | solution.py:380
  57.4 1.0 %copy-start.1 = (f32[256,512]{1,0:T(8,128)S(1)}, f32[256,512]{1,0:T(8,128)}, u32[]{:S(2)}) copy-start(f32[256,512]{1,0:T(8,128)} %get-tuple-element.48.own_ref) | copy-start | bytes 1572868
  58.7 21.1 %copy-start.5 = (f32[512]{0:T(512)S(1)}, f32[512]{0:T(512)}, u32[]{:S(2)}) copy-start(f32[512]{0:T(512)} %param.15) | copy-start | bytes 6148
  58.7 6.6 %collective-permute-start.4 = (s16[272,512]{1,0:T(8,128)(2,1)S(1)}, s16[272,512]{1,0:T(8,128)(2,1)S(1)}, u32[]{:S(2)}, u32[]{:S(2)}) collective-permute-start(s16[272,512]{1,0:T(8,128)(2,1)S(1)} %shard_map.113), channel_id=1, source_target_pairs={{8,16},{10,18},{12,20},{14,22},{16,8},{18,10},{20,12},{22,14},{9,1... | collective-permute-start | bytes 835592 | tf_op jit(solution)/shard_map/ppermute | solution.py:375
  59.4 17.9 %collective-permute-start.7 = (f32[4,3,512]{2,1,0:T(4,128)}, f32[4,3,512]{2,1,0:T(4,128)}, u32[]{:S(2)}, u32[]{:S(2)}) collective-permute-start(f32[4,3,512]{2,1,0:T(4,128)} %pad_maximum_fusion.1), channel_id=1, source_target_pairs={{0,24},{2,26},{4,28},{6,30},{8,16},{10,18},{12,20},{14,22},{16,8},... | collective-permute-start | bytes 73736 | tf_op jit(solution)/shard_map/ppermute | solution.py:21
  63.1 14.2 %collective-permute-start.6 = (f32[4,3,512]{2,1,0:T(4,128)}, f32[4,3,512]{2,1,0:T(4,128)}, u32[]{:S(2)}, u32[]{:S(2)}) collective-permute-start(f32[4,3,512]{2,1,0:T(4,128)} %pad_maximum_fusion.1), channel_id=1, source_target_pairs={{0,16},{2,18},{4,20},{6,22},{8,24},{10,26},{12,28},{14,30},{16,0},... | collective-permute-start | bytes 73736 | tf_op jit(solution)/shard_map/ppermute | solution.py:21
  65.3 12.0 %collective-permute-start.5 = (f32[4,3,512]{2,1,0:T(4,128)}, f32[4,3,512]{2,1,0:T(4,128)}, u32[]{:S(2)}, u32[]{:S(2)}) collective-permute-start(f32[4,3,512]{2,1,0:T(4,128)} %pad_maximum_fusion.1), channel_id=1, source_target_pairs={{0,8},{2,10},{4,12},{6,14},{8,0},{10,2},{12,4},{14,6},{16,24},{18,... | collective-permute-start | bytes 73736 | tf_op jit(solution)/shard_map/ppermute | solution.py:21
  65.3 0.7 copy-start.7
  67.2 15.4 %copy-start.8 = (s16[272,512]{1,0:T(8,128)(2,1)S(1)}, s16[272,512]{1,0:T(8,128)(2,1)}, u32[]{:S(2)}) copy-start(s16[272,512]{1,0:T(8,128)(2,1)} %copy-done.7) | copy-start | bytes 835588
  67.2 15.4 %collective-permute-start.8 = (s16[272,512]{1,0:T(8,128)(2,1)S(1)}, s16[272,512]{1,0:T(8,128)(2,1)S(1)}, u32[]{:S(2)}, u32[]{:S(2)}) collective-permute-start(s16[272,512]{1,0:T(8,128)(2,1)S(1)} %shard_map.113), channel_id=1, source_target_pairs={{0,24},{2,26},{4,28},{6,30},{24,0},{26,2},{28,4},{30,6},{1,25},{3,... | collective-permute-start | bytes 835592 | tf_op jit(solution)/shard_map/ppermute | solution.py:375
  77.3 7.5 %collective-permute-start.9 = (s16[272,512]{1,0:T(8,128)(2,1)S(1)}, s16[272,512]{1,0:T(8,128)(2,1)S(1)}, u32[]{:S(2)}, u32[]{:S(2)}) collective-permute-start(s16[272,512]{1,0:T(8,128)(2,1)S(1)} %get-tuple-element.57), channel_id=1, source_target_pairs={{0,1},{1,0},{2,3},{3,2},{4,5},{5,4},{6,7},{7,6},{8,9},{9,8},{10,11... | collective-permute-start | bytes 835592 | tf_op jit(solution)/shard_map/ppermute | solution.py:380
  84.8 12.2 %copy-start.6 = (f32[512]{0:T(512)S(1)}, f32[512]{0:T(512)}, u32[]{:S(2)}) copy-start(f32[512]{0:T(512)} %param.14) | copy-start | bytes 6148
